TPU v7x, 512 devices: a whole 4x8x8 slice. The times are simulated.
512 devices in a mesh: mem: 8 (over x, z_hi), col: 64 (over z_lo, y, core).
Axes of the slice: x: 4, y: 8, z: 8 (z_hi: 2, z_lo: 4; z = z_hi * 4 + z_lo), core: 2. Of those that a mesh axis runs over, the one named last changes fastest.
Arguments:
- perturbations: bfloat16 [8, 64, 384, 768], P('mem', None, 'col'), may hold values from -6 to 6
- gradient: float32 [64, 384, 768], P(None, 'col'), may hold values from -6 to 6
- member_weights: float32 [8], P('mem'), may hold values from 0.5 to 2
- scale_weights: float32 [3], replicated, may hold values from 0.2 to 2
- lon_filter: bfloat16 [3, 768, 768], P(None, 'mem'), may hold values from -1 to 1.5
- lat_filter: bfloat16 [3, 384, 384], P(None, 'col'), may hold values from -1 to 1.5
Outputs:
- increment: float32 [64, 384, 768], P('mem', 'col')
All inputs are finite; a program needn't handle non-finite values.
Results may differ from a plain program's by a relative error of at most 0.01.
Values may be sent and summed in bfloat16 or wider, within the bound.
No kernel may reach another device: no remote copies, remote signals or barrier semaphores. Data moves between devices by JAX's collectives and lax.ppermute only.
A program may use at most 64 MiB of HBM per device.

v0:
```python
import jax
import jax.numpy as jnp
from jax import lax
from jax.sharding import PartitionSpec as P


def on_device(perturbations, gradient, member_weights, scale_weights, lon_filter, lat_filter):
    member = perturbations[0].astype(jnp.float32)
    schur = (member * gradient).astype(jnp.bfloat16)
    levels = lax.all_to_all(schur, "col", split_axis=0, concat_axis=1, tiled=True)
    stacked = levels[None]
    blocks = jnp.einsum(
        "klaj,sij->klsai",
        lax.all_gather(stacked, "mem", axis=0, tiled=True),
        lon_filter,
        preferred_element_type=jnp.float32,
    ).astype(jnp.bfloat16)
    along = lax.all_to_all(blocks, "mem", split_axis=0, concat_axis=4, tiled=True)[0]
    across = jnp.einsum(
        "sab,lsbi->lsai",
        lax.all_gather(lat_filter, "col", axis=1, tiled=True),
        along,
        preferred_element_type=jnp.float32,
    )
    filtered = jnp.einsum("s,lsai->lai", scale_weights, across).astype(jnp.bfloat16)
    back = lax.all_to_all(filtered, "col", split_axis=1, concat_axis=0, tiled=True)
    terms = member_weights[0] * member * back.astype(jnp.float32)
    return lax.psum_scatter(terms, "mem", scatter_dimension=0, tiled=True)


def solution(mesh):
    placed = (
        P("mem", None, "col", None),
        P(None, "col", None),
        P("mem"),
        P(),
        P(None, "mem", None),
        P(None, "col", None),
    )
    return jax.shard_map(
        on_device, mesh=mesh, in_specs=placed, out_specs=P("mem", "col", None), check_vma=False
    )
```

profile of v0, /device:TPU:1, one launch (start us, length us, event | category | flops | bytes accessed | tf_op | source)
XLA Modules:
  0.0 407.2 jit_solution(3971693382576732496)
XLA Ops:
  6.5 2.4 fusion.5
  9.0 37.6 %all_to_all.33 = bf16[64,6,768]{2,1,0:T(8,128)(2,1)S(1)} all-to-all(bf16[64,6,768]{2,1,0:T(8,128)(2,1)S(1)} %fusion.5), channel_id=1, replica_groups=mesh['mem'=8,'col'=64] {'col'}, dimensions={0} | all-to-all | bytes 1179648 | tf_op jit(solution)/shard_map/all_to_all | solution.py:10
  46.6 1.0 broadcast_in_dim.3
  47.6 119.9 %all-gather.2.cloned.1.call-done = bf16[8,1,384,768]{3,2,1,0:T(8,128)(2,1)} async-done(((bf16[1,1,384,768]{3,2,1,0:T(8,128)(2,1)}), bf16[8,1,384,768]{3,2,1,0:T(8,128)(2,1)}) %all-gather.2.cloned.1.call-update) | async-done | bytes 4718608 | tf_op jit(solution)/shard_map/all_gather | solution.py:14
  167.6 5.2 %convert_bitcast_fusion = bf16[8,1,3,384,96]{3,4,2,1,0:T(8,128)(2,1)} fusion(bf16[8,1,384,768]{3,2,1,0:T(8,128)(2,1)} %all-gather.2.cloned.1.call-done, bf16[3,96,768]{2,1,0:T(8,128)(2,1)S(1)} %copy-done), kind=kOutput, calls=%fused_computation.5 | convolution fusion | flops 1359839232 | bytes 6930432 | tf_op jit(solution)/shard_map/klaj,sij->klsai/dot_general | solution.py:12
  172.7 3.7 all-to-all-start.1
  176.5 83.1 %all_gather.7 = bf16[3,384,384]{2,0,1:T(4,128)(2,1)S(1)} all-gather(bf16[3,6,384]{2,0,1:T(4,128)(2,1)S(1)} %copy.24), channel_id=1, replica_groups=mesh['mem'=8,'col'=64] {'col'}, dimensions={1}, use_global_device_ids=true | all-gather | bytes 898560 | tf_op jit(solution)/shard_map/all_gather | solution.py:21
  259.5 0.2 copy.23
  259.8 2.5 convolution_bitcast_fusion
  262.3 4.0 copy.29
  266.3 1.4 fusion.12
  267.7 0.9 copy.42
  268.6 0.5 broadcast.1
  269.2 4.2 %reduce.2 = bf16[384,768]{1,0:T(8,128)(2,1)S(1)} reduce(bf16[384,1,768]{2,1,0:T(2,128)(2,1)S(1)} %bitcast.63, bf16[]{:T(256)} %broadcast.1), dimensions={1}, to_apply=%bitcast.61.reduce_sub_computation | reduce | bytes 1179650
  273.4 1.1 reshape.37
  274.5 4.2 %all-to-all-start.2 = ((bf16[64,2,2304]{2,1,0:T(2,128)(2,1)}), bf16[64,2,2304]{2,1,0:T(2,128)(2,1)S(1)}, u32[]{:S(2)}, u32[]{:S(2)}) async-start(bf16[64,2,2304]{2,1,0:T(2,128)(2,1)} %reshape.37), calls=%async_computation.2 | async-start | bytes 1179648 | tf_op jit(solution)/shard_map/all_to_all | solution.py:26
  278.8 0.3 reduce-scatter.2.cloned.1.call-start
  279.7 18.1 %all-to-all-done.2 = bf16[64,2,2304]{2,1,0:T(2,128)(2,1)S(1)} async-done(((bf16[64,2,2304]{2,1,0:T(2,128)(2,1)}), bf16[64,2,2304]{2,1,0:T(2,128)(2,1)S(1)}, u32[]{:S(2)}, u32[]{:S(2)}) %all-to-all-start.2) | async-done | bytes 589856 | tf_op jit(solution)/shard_map/all_to_all | solution.py:26
  297.8 0.5 reshape.38
  298.3 3.4 convert_reduce_fusion
  301.7 0.2 reshape.31
  301.9 2.7 fusion.4
  304.6 94.2 %reduce-scatter.2.cloned.1.call-done = f32[8,6,768]{2,1,0:T(8,128)} async-done(((f32[64,6,768]{2,1,0:T(8,128)}), f32[8,6,768]{2,1,0:T(8,128)}) %reduce-scatter.2.cloned.1.call-update) | async-done | bytes 147472 | tf_op jit(solution)/shard_map/reduce_scatter | solution.py:28
  398.8 1.6 copy.27
  (12 shorter events, 0.1 us)
Async XLA Ops:
  6.5 161.0 %copy-start = (bf16[3,96,768]{2,1,0:T(8,128)(2,1)S(1)}, bf16[3,96,768]{2,1,0:T(8,128)(2,1)}, u32[]{:S(2)}) copy-start(bf16[3,96,768]{2,1,0:T(8,128)(2,1)} %param.10) | copy-start | bytes 1327108
  6.5 161.0 %all-gather.2.cloned.1.call-start = ((), (), s32[]{:S(2)}) async-start(), calls=%async_computation.4 | async-start | bytes 5308416 | tf_op jit(solution)/shard_map/all_gather | solution.py:14
  172.7 3.7 copy-start.1
  172.7 86.8 %all-to-all-start.1 = ((bf16[8,1,3,384,96]{3,4,2,1,0:T(8,128)(2,1)}), bf16[8,1,3,384,96]{3,4,2,1,0:T(8,128)(2,1)S(1)}, u32[]{:S(2)}, u32[]{:S(2)}) async-start(bf16[8,1,3,384,96]{3,4,2,1,0:T(8,128)(2,1)} %convert_bitcast_fusion), calls=%async_computation.1 | async-start | bytes 3538944 | tf_op jit(solution)/shard_map/all_to_all | solution.py:18
  262.3 4.0 copy-start.2
  274.5 23.3 %all-to-all-start.2 = ((bf16[64,2,2304]{2,1,0:T(2,128)(2,1)}), bf16[64,2,2304]{2,1,0:T(2,128)(2,1)S(1)}, u32[]{:S(2)}, u32[]{:S(2)}) async-start(bf16[64,2,2304]{2,1,0:T(2,128)(2,1)} %reshape.37), calls=%async_computation.2 | async-start | bytes 1179648 | tf_op jit(solution)/shard_map/all_to_all | solution.py:26
  278.8 120.0 %reduce-scatter.2.cloned.1.call-start = ((), (), s32[]{:S(2)}) async-start(), calls=%async_computation.5 | async-start | bytes 1769472 | tf_op jit(solution)/shard_map/reduce_scatter | solution.py:28
Sparse Core Ops, SparseCore 0:
  47.7 119.7 all-gather.1
  304.7 94.0 reduce-scatter.1
where the time goes:
time: 408 us; the launch traced here: 407 us
  waiting for transfers between devices  232 us (57%)
  blocking collectives  121 us (30%)
  between operations  14.2 us (3%)
  other arithmetic  12.7 us (3%)
  local copies, waits for them, and re-layouts  10.2 us (2%)
  matrix products  9.04 us (2%)
  starting transfers between devices  8.21 us (2%)
    all_gather x1, waiting for transfers between devices, on_device(): lax.all_gather(stacked, 'mem', axis=0, tiled=True)  120 us
    reduce_scatter x1, waiting for transfers between devices, on_device(): return lax.psum_scatter(terms, 'mem', scatter_dimension=0, tiled=True)  94.2 us
    all_gather x1, blocking collectives, on_device(): lax.all_gather(lat_filter, 'col', axis=1, tiled=True)  83.1 us
    all_to_all x1, blocking collectives, on_device(): lax.all_to_all(schur, 'col', split_axis=0, concat_axis=1, tiled=True)  37.6 us
    all_to_all x1, waiting for transfers between devices, on_device(): lax.all_to_all(filtered, 'col', split_axis=1, concat_axis=0, tiled=True)  18.1 us
  transfers between devices with their start and end apart: 4, of which 3 were waited for; matrix products, arithmetic and copies ran while one was open for 0% of the time, Pallas kernels for 0%

commit v1 on v0

v1 whole, which is shorter than its diff:
```python
import jax
import jax.numpy as jnp
from jax import lax
from jax.experimental import pallas as pl
from jax.experimental.pallas import tpu as pltpu
from jax.sharding import Mesh, PartitionSpec as P

MEM = ("x", "zh")
COL = ("zl", "y", "c")
SWAP = [(0, 1), (1, 0)]
F32, BF16 = jnp.float32, jnp.bfloat16


def filter_kernel(core, scale, field, lat, mine, other, out, lon, mid, sems):
    at = core[0]
    copies = []
    for x in range(4):
        for half, source in ((at, mine), (1 - at, other)):
            rows = pl.ds(pl.multiple_of((2 * x + half) * 96, 32), 96)
            copy = pltpu.make_async_copy(source.at[x], lon.at[:, rows, :], sems.at[len(copies)])
            copy.start()
            copies.append(copy)
    for s in range(3):
        across = jnp.dot(lat[s], field[...], preferred_element_type=F32)
        mid[s] = (scale[s] * across).astype(BF16)
    for copy in copies:
        copy.wait()
    total = jnp.zeros(out.shape, F32)
    for s in range(3):
        total += lax.dot_general(
            mid[s], lon[s], (((1,), (1,)), ((), ())), preferred_element_type=F32
        )
    out[...] = total.astype(BF16)


def filter_pair(core, scale, field, lat, mine, other):
    vmem = pl.BlockSpec(memory_space=pltpu.VMEM)
    smem = pl.BlockSpec(memory_space=pltpu.SMEM)
    hbm = pl.BlockSpec(memory_space=pl.ANY)
    return pl.pallas_call(
        filter_kernel,
        out_shape=jax.ShapeDtypeStruct((384, 768), BF16),
        in_specs=[smem, smem, vmem, vmem, hbm, hbm],
        out_specs=vmem,
        scratch_shapes=[
            pltpu.VMEM((3, 768, 768), BF16),
            pltpu.VMEM((3, 384, 768), BF16),
            pltpu.SemaphoreType.DMA((8,)),
        ],
        compiler_params=pltpu.CompilerParams(vmem_limit_bytes=40 * 2**20),
        cost_estimate=pl.CostEstimate(flops=2 * 10**9, bytes_accessed=5 * 10**6, transcendentals=0),
    )(core, scale, field, lat, mine, other)


def on_device(perturbations, gradient, member_weights, scale_weights, lon_filter, lat_filter):
    core = lax.axis_index("c")
    member = lax.axis_index(MEM)
    block = lax.ppermute(lon_filter, ("zh", "c"), [(0, 0), (1, 2), (2, 1), (3, 3)])
    mine = lax.all_gather(block, "x", axis=0)
    other = lax.ppermute(mine, "c", SWAP)
    turn = [(4 * x + z, 4 * z + x) for x in range(4) for z in range(4)]
    rows = jnp.pad(lat_filter.reshape(18, 384), ((0, 14), (0, 0)))
    rows = lax.ppermute(rows, ("x", "zl"), turn)
    rows = lax.all_gather(rows, "y", axis=0)
    rows = lax.all_gather(rows, "x", axis=0)
    swapped = lax.ppermute(rows, "c", SWAP)
    first = jnp.where(core == 0, rows, swapped)
    second = jnp.where(core == 0, swapped, rows)
    lat = jnp.stack([first, second], axis=2)[:, :, :, :18, :].reshape(64, 3, 6, 384)
    lat = lat.transpose(1, 0, 2, 3).reshape(3, 384, 384)
    weights = lax.all_gather(member_weights, MEM, axis=0, tiled=True)

    own = lax.all_to_all(perturbations[0].transpose(1, 0, 2), MEM, split_axis=1, concat_axis=1, tiled=True)
    level = lax.dynamic_slice_in_dim(gradient.transpose(1, 0, 2), member * 8, 8, axis=1)
    own = own.reshape(6, 8, 8, 768).astype(F32)
    schur = (own * level[:, None]).astype(BF16)
    schur = schur.transpose(1, 2, 0, 3).reshape(64, 2, 2304)
    field = lax.all_to_all(schur, COL, split_axis=0, concat_axis=0, tiled=True).reshape(384, 768)
    filtered = filter_pair(core.reshape(1).astype(jnp.int32), scale_weights, field, lat, mine, other)
    back = lax.all_to_all(filtered.reshape(64, 2, 2304), COL, split_axis=0, concat_axis=0, tiled=True)
    back = back.reshape(8, 8, 6, 768).transpose(2, 0, 1, 3).astype(F32)
    total = jnp.sum(weights[None, :, None, None] * own * back, axis=1)
    return total.transpose(1, 0, 2)


def solution(mesh):
    fine = Mesh(mesh.devices.reshape(4, 2, 4, 8, 2), MEM + COL)
    placed = (
        P(MEM, None, COL, None),
        P(None, COL, None),
        P(MEM),
        P(),
        P(None, MEM, None),
        P(None, COL, None),
    )
    return jax.shard_map(
        on_device, mesh=fine, in_specs=placed, out_specs=P(MEM, COL, None), check_vma=False
    )
```

time: 408 us -> 200 us (0.49)
  waiting for transfers between devices: 232 us -> 52.1 us
  blocking collectives: 121 us -> 55.5 us
  starting transfers between devices: 8.21 us -> 47.1 us
  other arithmetic: 12.7 us -> 3.03 us
  matrix products: 9.04 us -> 0 us
  local copies, waits for them, and re-layouts: 10.2 us -> 18.7 us
  Pallas kernels: 0 us -> 5.22 us
    reduce_scatter x1 -> x0, waiting for transfers between devices: 94.2 us -> none  [on_device(): return lax.psum_scatter(terms, 'mem', scatter_dimension=0, tiled=True)]
    all_gather x1, waiting for transfers between devices: 120 us -> 32.5 us  [on_device(): mine = lax.all_gather(block, 'x', axis=0)]
    all_gather x1 -> x2, blocking collectives: 83.1 us -> 30.4 us  [the longest x1 19.7 us: on_device(): rows = lax.all_gather(rows, 'y', axis=0)]
    all_to_all x1 -> x0, blocking collectives: 37.6 us -> none  [on_device(): lax.all_to_all(schur, 'col', split_axis=0, concat_axis=1, tiled=True)]
    ppermute x0 -> x4, starting transfers between devices: none -> 25.9 us  [the longest x1 12.1 us: on_device(): lax.ppermute(lon_filter, ('zh', 'c'), [(0, 0), (1, 2), (2, 1), (3, 3)])]
    unnamed x0 -> x1, blocking collectives: none -> 25 us
    all_to_all x2 -> x3, starting transfers between devices: 7.95 us -> 21.2 us  [the longest x1 11.2 us: on_device(): lax.all_to_all(schur, COL, split_axis=0, concat_axis=0, tiled=True)]
    dot_general x3 -> x0, matrix products: 9.04 us -> none  [the longest x1 5.16 us: on_device(): jnp.einsum('klaj,sij->klsai', lax.all_gather(stacked, 'mem', axis=0, tile...]
  transfers between devices with their start and end apart: 4 -> 8, of which waited for: 3 -> 3; matrix products, arithmetic and copies ran while one was open for 0% -> 8% of each run, Pallas kernels for 0% -> 0%
where the time goes in v1:
time: 200 us; the launch traced here: 196 us
  blocking collectives  55.5 us (28%)
  waiting for transfers between devices  52.1 us (26%)
  starting transfers between devices  47.1 us (24%)
  local copies, waits for them, and re-layouts  18.7 us (9%)
  between operations  14.3 us (7%)
  Pallas kernels  5.22 us (3%)
  other arithmetic  3.03 us (2%)
    all_gather x1, waiting for transfers between devices, on_device(): mine = lax.all_gather(block, 'x', axis=0)  32.5 us
    unnamed x1, blocking collectives  25 us
    all_gather x1, blocking collectives, on_device(): rows = lax.all_gather(rows, 'y', axis=0)  19.7 us
    all_to_all x1, waiting for transfers between devices, on_device(): lax.all_to_all(schur, COL, split_axis=0, concat_axis=0, tiled=True)  13.3 us
    ppermute x1, starting transfers between devices, on_device(): lax.ppermute(lon_filter, ('zh', 'c'), [(0, 0), (1, 2), (2, 1), (3, 3)])  12.1 us
    all_to_all x1, starting transfers between devices, on_device(): lax.all_to_all(schur, COL, split_axis=0, concat_axis=0, tiled=True)  11.2 us
    all_gather x1, blocking collectives, on_device(): rows = lax.all_gather(rows, 'x', axis=0)  10.7 us
    ppermute x1, starting transfers between devices, on_device(): swapped = lax.ppermute(rows, 'c', SWAP)  10.5 us
  transfers between devices with their start and end apart: 8, of which 3 were waited for; matrix products, arithmetic and copies ran while one was open for 8% of the time, Pallas kernels for 0%

profile of v1, /device:TPU:1, one launch (start us, length us, event | category | flops | bytes accessed | tf_op | source)
XLA Modules:
  0.0 195.9 jit_solution(8799523639548082274)
XLA Ops:
  6.5 12.1 %collective-permute-start.2 = (bf16[3,96,768]{2,1,0:T(8,128)(2,1)}, bf16[3,96,768]{2,1,0:T(8,128)(2,1)S(1)}, u32[]{:S(2)}, u32[]{:S(2)}) collective-permute-start(bf16[3,96,768]{2,1,0:T(8,128)(2,1)} %param.10), channel_id=1, source_target_pairs={{0,0},{1,64},{64,1},{65,65},{2,2},{3,66},{66,3},{67,67},{4,4},{5,6... | collective-permute-start | bytes 1327112 | tf_op jit(solution)/shard_map/ppermute | solution.py:58
  18.7 6.3 %collective-permute-done.2 = bf16[3,96,768]{2,1,0:T(8,128)(2,1)S(1)} collective-permute-done((bf16[3,96,768]{2,1,0:T(8,128)(2,1)}, bf16[3,96,768]{2,1,0:T(8,128)(2,1)S(1)}, u32[]{:S(2)}, u32[]{:S(2)}) %collective-permute-start.2) | collective-permute-done | bytes 442400 | tf_op jit(solution)/shard_map/ppermute | solution.py:58
  25.8 2.3 %copy.24 = bf16[1,64,6,768]{3,2,1,0:T(8,128)(2,1)} copy(bf16[1,64,6,768]{3,1,2,0:T(8,128)(2,1)} %param.6) | data formatting | bytes 1179648 | tf_op args[0]
  28.1 4.0 %all-to-all-start = ((bf16[6,64,768]{2,0,1:T(8,128)(2,1)}), bf16[6,64,768]{2,0,1:T(8,128)(2,1)S(1)}, u32[]{:S(2)}, u32[]{:S(2)}) async-start(bf16[6,64,768]{2,0,1:T(8,128)(2,1)} %bitcast.26), calls=%async_computation | async-start | bytes 1572864 | tf_op jit(solution)/shard_map/all_to_all | solution.py:73
  33.6 32.5 %all-gather.5.cloned.1.call-done = bf16[12,96,768]{2,1,0:T(8,128)(2,1)} async-done(((bf16[3,96,768]{2,1,0:T(8,128)(2,1)}), bf16[12,96,768]{2,1,0:T(8,128)(2,1)}) %all-gather.5.cloned.1.call-update) | async-done | bytes 1769488 | tf_op jit(solution)/shard_map/all_gather | solution.py:59
  66.1 2.6 %collective-permute-start.3 = (bf16[4,3,96,768]{3,2,1,0:T(8,128)(2,1)}, bf16[4,3,96,768]{3,2,1,0:T(8,128)(2,1)}, u32[]{:S(2)}, u32[]{:S(2)}) collective-permute-start(bf16[4,3,96,768]{3,2,1,0:T(8,128)(2,1)} %bitcast.27), channel_id=1, source_target_pairs={{0,1},{1,0},{2,3},{3,2},{4,5},{5,4},{6,7},{7,6},{8,9},{9,8},{10,11... | collective-permute-start | bytes 5308424 | tf_op jit(solution)/shard_map/ppermute | solution.py:60
  68.7 19.7 %all-gather = bf16[256,384]{1,0:T(8,128)(2,1)S(1)} all-gather(bf16[32,384]{1,0:T(8,128)(2,1)S(1)} %collective-permute-done), channel_id=2, replica_groups=mesh['x'=4,'zh'=2,'zl'=4,'y'=8,'c'=2] {'y'}, dimensions={0}, use_global_device_ids=true | all-gather | bytes 221184 | tf_op jit(solution)/shard_map/all_gather | solution.py:64
  88.4 10.7 %all-gather.1 = bf16[32,32,384]{2,1,0:T(8,128)(2,1)S(1)} all-gather(bf16[8,32,384]{2,1,0:T(8,128)(2,1)S(1)} %bitcast.33), channel_id=3, replica_groups=mesh['x'=4,'zh'=2,'zl'=4,'y'=8,'c'=2] {'x'}, dimensions={0}, use_global_device_ids=true | all-gather | bytes 983040 | tf_op jit(solution)/shard_map/all_gather | solution.py:65
  99.1 10.5 %collective-permute-start.1 = (bf16[4,8,32,384]{3,2,1,0:T(8,128)(2,1)S(1)}, bf16[4,8,32,384]{3,2,1,0:T(8,128)(2,1)}, u32[]{:S(2)}, u32[]{:S(2)}) collective-permute-start(bf16[4,8,32,384]{3,2,1,0:T(8,128)(2,1)S(1)} %bitcast.31), channel_id=1, source_target_pairs={{0,1},{1,0},{2,3},{3,2},{4,5},{5,4},{6,7},{7,6},{8,9},{9,8},{10,11... | collective-permute-start | bytes 2359304 | tf_op jit(solution)/shard_map/ppermute | solution.py:66
  109.6 1.3 fusion.3
  110.9 1.2 reshape.30
  112.2 11.2 %all-to-all-start.1 = ((bf16[64,2,2304]{2,1,0:T(2,128)(2,1)}), bf16[64,2,2304]{2,1,0:T(2,128)(2,1)}, u32[]{:S(2)}, u32[]{:S(2)}) async-start(bf16[64,2,2304]{2,1,0:T(2,128)(2,1)} %reshape.30), calls=%async_computation.1 | async-start | bytes 1179648 | tf_op jit(solution)/shard_map/all_to_all | solution.py:78
  123.4 1.3 select_bitcast_fusion.1
  125.7 1.2 reshape.33
  127.0 1.7 copy.21
  129.0 13.3 %all-to-all-done.1 = bf16[64,2,2304]{2,1,0:T(2,128)(2,1)} async-done(((bf16[64,2,2304]{2,1,0:T(2,128)(2,1)}), bf16[64,2,2304]{2,1,0:T(2,128)(2,1)}, u32[]{:S(2)}, u32[]{:S(2)}) %all-to-all-start.1) | async-done | bytes 589856 | tf_op jit(solution)/shard_map/all_to_all | solution.py:78
  142.3 2.1 %reshape.31.field = bf16[384,768]{1,0:T(8,128)(2,1)S(1)} reshape(bf16[64,2,2304]{2,1,0:T(2,128)(2,1)} %all-to-all-done.1) | data formatting | bytes 1179648 | tf_op jit(solution)/shard_map/reshape | solution.py:78
  144.5 1.5 copy-done.1
  145.9 5.2 %shard_map.64 = bf16[384,768]{1,0:T(8,128)(2,1)S(1)} custom-call(s32[1]{0:T(128)} %bitcast.4.core, f32[3]{0:T(128)S(1)} %copy-done.2, bf16[384,768]{1,0:T(8,128)(2,1)S(1)} %reshape.31.field, bf16[3,384,384]{2,1,0:T(8,128)(2,1)S(1)} %reshape.34.lat, bf16[4,3,96,768]{3,2,1,0:T(8,128)(2,1)S(1)} %bitcast.28, bf16[4,3,96,768]{3,2,1,0:T(8,128)(2,1)} %collective-permute-done.3.other), custom_call_target="tpu_custom_call" | custom-call | flops 2000000000 | bytes 5000000 | tf_op jit(solution)/shard_map/pallas_call | solution.py:40
  151.2 1.1 reshape.35
  152.3 6.0 %all-to-all-start.2 = ((bf16[64,2,2304]{2,1,0:T(2,128)(2,1)}), bf16[64,2,2304]{2,1,0:T(2,128)(2,1)}, u32[]{:S(2)}, u32[]{:S(2)}) async-start(bf16[64,2,2304]{2,1,0:T(2,128)(2,1)} %reshape.35), calls=%async_computation.2 | async-start | bytes 1179648 | tf_op jit(solution)/shard_map/all_to_all | solution.py:80
  159.0 1.3 dynamic-slice.4
  161.0 25.0 %all-reduce.1 = f32[8]{0:T(128)S(1)} all-reduce(f32[8]{0:T(128)S(1)} %dynamic-update-slice), channel_id=1, replica_groups=mesh['x'=4,'zh'=2,'zl'=4,'y'=8,'c'=2] {'x','zh'}, use_global_device_ids=true, to_apply=%add.1 | all-reduce | flops 8 | bytes 64
  186.0 2.0 %reshape.37 = f32[8,8,6,768]{3,2,1,0:T(8,128)S(1)} reshape(bf16[64,2,2304]{2,1,0:T(2,128)(2,1)} %all-to-all-done.2) | data formatting | bytes 1769472 | tf_op jit(solution)/shard_map/convert_element_type | solution.py:81
  (32 shorter events, 5.4 us)
Async XLA Ops:
  6.5 26.3 %copy-start = (f32[64,6,768]{2,0,1:T(8,128)S(1)}, f32[64,6,768]{2,0,1:T(8,128)}, u32[]{:S(2)}) copy-start(f32[64,6,768]{2,0,1:T(8,128)} %param.7) | copy-start | bytes 3538948
  6.5 59.6 %all-gather.5.cloned.1.call-start = ((), (), s32[]{:S(2)}) async-start(), calls=%async_computation.3 | async-start | bytes 2211840 | tf_op jit(solution)/shard_map/all_gather | solution.py:59
  6.5 18.4 %collective-permute-start.2 = (bf16[3,96,768]{2,1,0:T(8,128)(2,1)}, bf16[3,96,768]{2,1,0:T(8,128)(2,1)S(1)}, u32[]{:S(2)}, u32[]{:S(2)}) collective-permute-start(bf16[3,96,768]{2,1,0:T(8,128)(2,1)} %param.10), channel_id=1, source_target_pairs={{0,0},{1,64},{64,1},{65,65},{2,2},{3,66},{66,3},{67,67},{4,4},{5,6... | collective-permute-start | bytes 1327112 | tf_op jit(solution)/shard_map/ppermute | solution.py:58
  25.0 0.8 copy-start.5
  25.8 6.3 %copy-start.6 = (bf16[3,6,384]{2,1,0:T(8,128)(2,1)S(1)}, bf16[3,6,384]{2,1,0:T(8,128)(2,1)}, u32[]{:S(2)}) copy-start(bf16[3,6,384]{2,1,0:T(8,128)(2,1)} %param.11) | copy-start | bytes 41476
  28.1 81.5 %all-to-all-start = ((bf16[6,64,768]{2,0,1:T(8,128)(2,1)}), bf16[6,64,768]{2,0,1:T(8,128)(2,1)S(1)}, u32[]{:S(2)}, u32[]{:S(2)}) async-start(bf16[6,64,768]{2,0,1:T(8,128)(2,1)} %bitcast.26), calls=%async_computation | async-start | bytes 1572864 | tf_op jit(solution)/shard_map/all_to_all | solution.py:73
  32.1 36.5 %collective-permute-start = (bf16[32,384]{1,0:T(8,128)(2,1)S(1)}, bf16[32,384]{1,0:T(8,128)(2,1)S(1)}, u32[]{:S(2)}, u32[]{:S(2)}) collective-permute-start(bf16[32,384]{1,0:T(8,128)(2,1)S(1)} %pad.4), channel_id=1, source_target_pairs={{0,0},{16,128},{32,256},{48,384},{128,16},{144,144},{160,272},{176... | collective-permute-start | bytes 73736 | tf_op jit(solution)/shard_map/ppermute | solution.py:63
  66.1 78.3 %collective-permute-start.3 = (bf16[4,3,96,768]{3,2,1,0:T(8,128)(2,1)}, bf16[4,3,96,768]{3,2,1,0:T(8,128)(2,1)}, u32[]{:S(2)}, u32[]{:S(2)}) collective-permute-start(bf16[4,3,96,768]{3,2,1,0:T(8,128)(2,1)} %bitcast.27), channel_id=1, source_target_pairs={{0,1},{1,0},{2,3},{3,2},{4,5},{5,4},{6,7},{7,6},{8,9},{9,8},{10,11... | collective-permute-start | bytes 5308424 | tf_op jit(solution)/shard_map/ppermute | solution.py:60
  99.1 24.2 %collective-permute-start.1 = (bf16[4,8,32,384]{3,2,1,0:T(8,128)(2,1)S(1)}, bf16[4,8,32,384]{3,2,1,0:T(8,128)(2,1)}, u32[]{:S(2)}, u32[]{:S(2)}) collective-permute-start(bf16[4,8,32,384]{3,2,1,0:T(8,128)(2,1)S(1)} %bitcast.31), channel_id=1, source_target_pairs={{0,1},{1,0},{2,3},{3,2},{4,5},{5,4},{6,7},{7,6},{8,9},{9,8},{10,11... | collective-permute-start | bytes 2359304 | tf_op jit(solution)/shard_map/ppermute | solution.py:66
  109.6 2.5 %copy-start.3 = (bf16[6,64,768]{2,0,1:T(8,128)(2,1)}, bf16[6,64,768]{2,0,1:T(8,128)(2,1)S(1)}, u32[]{:S(2)}) copy-start(bf16[6,64,768]{2,0,1:T(8,128)(2,1)S(1)} %all-to-all-done) | copy-start | bytes 1769476
  112.2 30.1 %all-to-all-start.1 = ((bf16[64,2,2304]{2,1,0:T(2,128)(2,1)}), bf16[64,2,2304]{2,1,0:T(2,128)(2,1)}, u32[]{:S(2)}, u32[]{:S(2)}) async-start(bf16[64,2,2304]{2,1,0:T(2,128)(2,1)} %reshape.30), calls=%async_computation.1 | async-start | bytes 1179648 | tf_op jit(solution)/shard_map/all_to_all | solution.py:78
  128.7 15.8 %copy-start.2 = (f32[3]{0:T(128)S(1)}, f32[3]{0:T(128)}, u32[]{:S(2)}) copy-start(f32[3]{0:T(128)} %scale.1) | copy-start | bytes 40
  144.4 1.5 copy-start.1
  152.3 35.8 %copy-start.4 = (bf16[6,64,768]{2,0,1:T(8,128)(2,1)S(1)}, bf16[6,64,768]{2,0,1:T(8,128)(2,1)}, u32[]{:S(2)}) copy-start(bf16[6,64,768]{2,0,1:T(8,128)(2,1)} %copy-done.3) | copy-start | bytes 1769476
  152.3 33.7 %all-to-all-start.2 = ((bf16[64,2,2304]{2,1,0:T(2,128)(2,1)}), bf16[64,2,2304]{2,1,0:T(2,128)(2,1)}, u32[]{:S(2)}, u32[]{:S(2)}) async-start(bf16[64,2,2304]{2,1,0:T(2,128)(2,1)} %reshape.35), calls=%async_computation.2 | async-start | bytes 1179648 | tf_op jit(solution)/shard_map/all_to_all | solution.py:80
Sparse Core Ops, SparseCore 0:
  25.9 40.1 all-gather.4

commit v2 on v1

v2 whole, which is shorter than its diff:
```python
import jax
import jax.numpy as jnp
from jax import lax
from jax.experimental import pallas as pl
from jax.experimental.pallas import tpu as pltpu
from jax.sharding import Mesh, PartitionSpec as P

MEM = ("x", "zh")
COL = ("zl", "y", "c")
SWAP = [(0, 1), (1, 0)]
F32, BF16 = jnp.float32, jnp.bfloat16


VMEM = pl.BlockSpec(memory_space=pltpu.VMEM)
SMEM = pl.BlockSpec(memory_space=pltpu.SMEM)
ANY = pl.BlockSpec(memory_space=pl.ANY)
PLACES = ((0, 0, 48, 0), (1, 0, 48, 384), (2, 0, 32, 0), (2, 32, 16, 384))
STARTS = (288, 288, 336, 336)


def pack_kernel(y, block, *rest):
    pieces, (out, tiles, sem) = rest[:8], rest[8:]
    copy = pltpu.make_async_copy(block, out.at[pl.ds(0, 288)], sem)
    copy.start()
    for d, piece in enumerate(pieces):
        tiles[lax.rem(y[0] + 8 - d, 8)] = piece[...].astype(F32)
    for s, first, rows, column in PLACES:
        start = STARTS[PLACES.index((s, first, rows, column))]
        whole = jnp.concatenate([tiles[n, s, :6, :] for n in range(8)], axis=0)
        out[pl.ds(start, rows), pl.ds(column, 384)] = whole[first : first + rows].astype(BF16)
    out[pl.ds(352, 16), pl.ds(384, 384)] = jnp.zeros((16, 384), BF16)
    copy.wait()


def pack(y, block, pieces):
    return pl.pallas_call(
        pack_kernel,
        out_shape=jax.ShapeDtypeStruct((368, 768), BF16),
        in_specs=[SMEM, ANY] + [VMEM] * 8,
        out_specs=VMEM,
        scratch_shapes=[pltpu.VMEM((8, 3, 8, 384), F32), pltpu.SemaphoreType.DMA],
        cost_estimate=pl.CostEstimate(flops=10**6, bytes_accessed=2 * 10**6, transcendentals=0),
    )(y, block, *pieces)


def filter_kernel(place, scale, member, field, *rest):
    blocks, (out, lon, lat, mid, lon_sems, lat_sems) = rest[:8], rest[8:]
    lon_copies, lat_copies = [], []
    for n, block in enumerate(blocks):
        for m, ((s, first, rows, column), start) in enumerate(zip(PLACES, STARTS)):
            to = pl.ds(pl.multiple_of(place[1, n] * 48 + first, 16), rows)
            copy = pltpu.make_async_copy(
                block.at[pl.ds(start, rows), pl.ds(column, 384)], lat.at[s, to, :], lat_sems.at[n, m]
            )
            copy.start()
            lat_copies.append(copy)
    for n, block in enumerate(blocks):
        for s in range(3):
            to = pl.ds(pl.multiple_of(place[0, n] * 96, 32), 96)
            copy = pltpu.make_async_copy(
                block.at[pl.ds(96 * s, 96), :], lon.at[s, to, :], lon_sems.at[n, s]
            )
            copy.start()
            lon_copies.append(copy)
    for copy in lat_copies:
        copy.wait()
    for s in range(3):
        across = jnp.dot(lat[s], field[...], preferred_element_type=F32)
        mid[s] = (scale[s] * member[0] * across).astype(BF16)
    for copy in lon_copies:
        copy.wait()
    total = jnp.zeros(out.shape, F32)
    for s in range(3):
        total += lax.dot_general(
            mid[s], lon[s], (((1,), (1,)), ((), ())), preferred_element_type=F32
        )
    out[...] = total.astype(BF16)


def filter_pair(place, scale, member, field, blocks):
    return pl.pallas_call(
        filter_kernel,
        out_shape=jax.ShapeDtypeStruct((384, 768), BF16),
        in_specs=[SMEM, SMEM, SMEM, VMEM] + [ANY] * 8,
        out_specs=VMEM,
        scratch_shapes=[
            pltpu.VMEM((3, 768, 768), BF16),
            pltpu.VMEM((3, 384, 384), BF16),
            pltpu.VMEM((3, 384, 768), BF16),
            pltpu.SemaphoreType.DMA((8, 3)),
            pltpu.SemaphoreType.DMA((8, 4)),
        ],
        compiler_params=pltpu.CompilerParams(vmem_limit_bytes=40 * 2**20),
        cost_estimate=pl.CostEstimate(flops=2 * 10**9, bytes_accessed=5 * 10**6, transcendentals=0),
    )(place, scale, member, field, *blocks)


def on_device(perturbations, gradient, member_weights, scale_weights, lon_filter, lat_filter):
    x, y, core = lax.axis_index("x"), lax.axis_index("y"), lax.axis_index("c")
    block = lax.ppermute(lon_filter, ("zh", "c"), [(0, 0), (1, 2), (2, 1), (3, 3)])
    own = perturbations[0].transpose(1, 0, 2).reshape(6, 8, 8, 768).transpose(1, 0, 2, 3)
    own = lax.all_to_all(own, MEM, split_axis=0, concat_axis=0, tiled=True)
    rows = jnp.pad(lat_filter, ((0, 0), (0, 2), (0, 0)))
    pieces = [
        lax.ppermute(rows, ("x", "zl", "y"), [
            (32 * a + 8 * b + r, 32 * b + 8 * a + (r + d) % 8)
            for a in range(4) for b in range(4) for r in range(8)
        ])
        for d in range(8)
    ]
    turn = [((c // 8) * 64 + m * 8 + c % 8, m * 64 + c) for m in range(8) for c in range(64)]
    weight = lax.ppermute(member_weights, MEM + COL, turn)
    own, block, pieces, weight = lax.optimization_barrier((own, block, pieces, weight))

    packed = pack(y.reshape(1).astype(jnp.int32), block.reshape(288, 768), pieces)
    own, packed = lax.optimization_barrier((own, packed))
    mine = [packed] + [
        lax.ppermute(packed, "x", [(i, (i + d) % 4) for i in range(4)]) for d in (1, 3, 2)
    ]
    blocks = mine + [lax.ppermute(b, "c", SWAP) for b in mine]
    froms = jnp.stack([(x + 4 - d) % 4 for d in (0, 1, 3, 2)]).astype(jnp.int32)
    place = jnp.concatenate([2 * froms + core, 2 * froms + 1 - core]).astype(jnp.int32)
    place = jnp.stack([place, place])

    member = lax.axis_index(MEM)
    level = lax.dynamic_slice_in_dim(gradient.transpose(1, 0, 2), member * 8, 8, axis=1)
    own = own.astype(F32)
    schur = (own * level[None]).astype(BF16)
    schur = schur.transpose(0, 2, 1, 3).reshape(64, 2, 2304)
    field = lax.all_to_all(schur, COL, split_axis=0, concat_axis=0, tiled=True).reshape(384, 768)
    filtered = filter_pair(place, scale_weights, weight, field, blocks).reshape(64, 2, 2304)
    back = lax.all_to_all(filtered, ("zl", "c", "y"), split_axis=0, concat_axis=0, tiled=True)
    back = back.reshape(4, 2, 2, 4, 6, 768).transpose(0, 2, 4, 3, 1, 5).reshape(8, 6, 8, 768)
    return jnp.sum(own * back.astype(F32), axis=0).transpose(1, 0, 2)


def solution(mesh):
    fine = Mesh(mesh.devices.reshape(4, 2, 4, 8, 2), MEM + COL)
    placed = (
        P(MEM, None, COL, None),
        P(None, COL, None),
        P(MEM),
        P(),
        P(None, MEM, None),
        P(None, COL, None),
    )
    return jax.shard_map(
        on_device, mesh=fine, in_specs=placed, out_specs=P(MEM, COL, None), check_vma=False
    )
```

time: 200 us -> 183 us (0.915); the launches traced: 196 us -> 182 us
  starting transfers between devices: 47.1 us -> 110 us
  waiting for transfers between devices: 52.1 us -> 15.9 us
  blocking collectives: 55.5 us -> 29.6 us
  between operations: 14.3 us -> 0.52 us
  Pallas kernels: 5.22 us -> 9.92 us
  local copies, waits for them, and re-layouts: 18.7 us -> 14.5 us
    ppermute x3 -> x16, starting transfers between devices: 13.8 us -> 57.2 us  [the longest x8 35.4 us: on_device(): lax.ppermute(rows, ('x', 'zl', 'y'), [(32 * a + 8 * b + r, 32 * b + 8 * a...]
    all_gather x1 -> x0, waiting for transfers between devices: 32.5 us -> none  [on_device(): mine = lax.all_gather(block, 'x', axis=0)]
    all_gather x2 -> x0, blocking collectives: 30.4 us -> none  [the longest x1 19.7 us: on_device(): rows = lax.all_gather(rows, 'y', axis=0)]
    all_to_all x0 -> x1, blocking collectives: none -> 29.6 us  [on_device(): lax.all_to_all(filtered, ('zl', 'c', 'y'), split_axis=0, concat_axis=0, t...]
    unnamed x1 -> x0, blocking collectives: 25 us -> none
    all_to_all x1, starting transfers between devices: 11.2 us -> 31.4 us  [on_device(): lax.all_to_all(schur, COL, split_axis=0, concat_axis=0, tiled=True)]
    ppermute x3 -> x16, waiting for transfers between devices: 0.01 us -> 15.8 us  [the longest x3 12.8 us: on_device(): lax.ppermute(packed, 'x', [(i, (i + d) % 4) for i in range(4)])]
    all_to_all x1, waiting for transfers between devices: 13.3 us -> 0.01 us  [on_device(): lax.all_to_all(schur, COL, split_axis=0, concat_axis=0, tiled=True)]
  transfers between devices with their start and end apart: 8 -> 19, of which waited for: 3 -> 5; matrix products, arithmetic and copies ran while one was open for 8% -> 1% of each run, Pallas kernels for 0% -> 0%
where the time goes in v2:
time: 183 us; the launch traced here: 182 us
  starting transfers between devices  110 us (60%)
  blocking collectives  29.6 us (16%)
  waiting for transfers between devices  15.9 us (9%)
  local copies, waits for them, and re-layouts  14.5 us (8%)
  Pallas kernels  9.92 us (5%)
    ppermute x8, starting transfers between devices, on_device(): lax.ppermute(rows, ('x', 'zl', 'y'), [(32 * a + 8 * b + r, 32 * b + 8 * a...  35.4 us
    all_to_all x1, starting transfers between devices, on_device(): lax.all_to_all(schur, COL, split_axis=0, concat_axis=0, tiled=True)  31.4 us
    all_to_all x1, blocking collectives, on_device(): lax.all_to_all(filtered, ('zl', 'c', 'y'), split_axis=0, concat_axis=0, t...  29.6 us
    all_to_all x1, starting transfers between devices, on_device(): own = lax.all_to_all(own, MEM, split_axis=0, concat_axis=0, tiled=True)  13.3 us
    ppermute x3, waiting for transfers between devices, on_device(): lax.ppermute(packed, 'x', [(i, (i + d) % 4) for i in range(4)])  12.8 us
    ppermute x4, starting transfers between devices, on_device(): blocks = mine + [lax.ppermute(b, 'c', SWAP) for b in mine]  12.4 us
    ppermute x1, starting transfers between devices, on_device(): lax.ppermute(lon_filter, ('zh', 'c'), [(0, 0), (1, 2), (2, 1), (3, 3)])  8.38 us
    ppermute x3, starting transfers between devices, on_device(): lax.ppermute(packed, 'x', [(i, (i + d) % 4) for i in range(4)])  7.49 us
  transfers between devices with their start and end apart: 19, of which 5 were waited for; matrix products, arithmetic and copies ran while one was open for 1% of the time, Pallas kernels for 0%

profile of v2, /device:TPU:1, one launch (start us, length us, event | category | flops | bytes accessed | tf_op | source)
XLA Modules:
  0.0 181.7 jit_solution(16785000486139507842)
XLA Ops:
  0.0 2.0 %copy.16 = bf16[8,6,8,768]{3,2,1,0:T(8,128)(2,1)} copy(bf16[8,6,8,768]{3,2,0,1:T(8,128)(2,1)} %bitcast.22) | data formatting | bytes 1179648 | tf_op jit(solution)/shard_map/transpose | solution.py:101
  2.0 13.3 %all-to-all-start = ((bf16[8,6,8,768]{3,2,1,0:T(8,128)(2,1)}), bf16[8,6,8,768]{3,2,1,0:T(8,128)(2,1)S(1)}, u32[]{:S(2)}, u32[]{:S(2)}) async-start(bf16[8,6,8,768]{3,2,1,0:T(8,128)(2,1)} %copy.16), calls=%async_computation | async-start | bytes 1179648 | tf_op jit(solution)/shard_map/all_to_all | solution.py:102
  15.3 8.4 %collective-permute-start = (bf16[3,96,768]{2,1,0:T(8,128)(2,1)S(1)}, bf16[3,96,768]{2,1,0:T(8,128)(2,1)S(1)}, u32[]{:S(2)}, u32[]{:S(2)}) collective-permute-start(bf16[3,96,768]{2,1,0:T(8,128)(2,1)S(1)} %copy-done.17), channel_id=1, source_target_pairs={{0,0},{1,64},{64,1},{65,65},{2,2},{3,66},{66,3},{67,67},{4,4},{5,6... | collective-permute-start | bytes 1327112 | tf_op jit(solution)/shard_map/ppermute | solution.py:100
  23.8 5.1 %collective-permute-start.8 = (bf16[3,8,384]{2,1,0:T(8,128)(2,1)S(1)}, bf16[3,8,384]{2,1,0:T(8,128)(2,1)S(1)}, u32[]{:S(2)}, u32[]{:S(2)}) collective-permute-start(bf16[3,8,384]{2,1,0:T(8,128)(2,1)S(1)} %pad.4), channel_id=1, source_target_pairs={{0,14},{2,0},{4,2},{6,4},{8,6},{10,8},{12,10},{14,12},{16,142},{18... | collective-permute-start | bytes 55304 | tf_op jit(solution)/shard_map/ppermute | solution.py:105
  28.9 3.8 %collective-permute-start.7 = (bf16[3,8,384]{2,1,0:T(8,128)(2,1)S(1)}, bf16[3,8,384]{2,1,0:T(8,128)(2,1)S(1)}, u32[]{:S(2)}, u32[]{:S(2)}) collective-permute-start(bf16[3,8,384]{2,1,0:T(8,128)(2,1)S(1)} %pad.4), channel_id=1, source_target_pairs={{0,12},{2,14},{4,0},{6,2},{8,4},{10,6},{12,8},{14,10},{16,140},{18... | collective-permute-start | bytes 55304 | tf_op jit(solution)/shard_map/ppermute | solution.py:105
  32.6 2.7 %collective-permute-start.6 = (bf16[3,8,384]{2,1,0:T(8,128)(2,1)S(1)}, bf16[3,8,384]{2,1,0:T(8,128)(2,1)S(1)}, u32[]{:S(2)}, u32[]{:S(2)}) collective-permute-start(bf16[3,8,384]{2,1,0:T(8,128)(2,1)S(1)} %pad.4), channel_id=1, source_target_pairs={{0,10},{2,12},{4,14},{6,0},{8,2},{10,4},{12,6},{14,8},{16,138},{18... | collective-permute-start | bytes 55304 | tf_op jit(solution)/shard_map/ppermute | solution.py:105
  37.3 17.0 %collective-permute-start.5 = (bf16[3,8,384]{2,1,0:T(8,128)(2,1)S(1)}, bf16[3,8,384]{2,1,0:T(8,128)(2,1)S(1)}, u32[]{:S(2)}, u32[]{:S(2)}) collective-permute-start(bf16[3,8,384]{2,1,0:T(8,128)(2,1)S(1)} %pad.4), channel_id=1, source_target_pairs={{0,8},{2,10},{4,12},{6,14},{8,0},{10,2},{12,4},{14,6},{16,136},{18... | collective-permute-start | bytes 55304 | tf_op jit(solution)/shard_map/ppermute | solution.py:105
  56.3 2.3 %collective-permute-start.3 = (bf16[3,8,384]{2,1,0:T(8,128)(2,1)S(1)}, bf16[3,8,384]{2,1,0:T(8,128)(2,1)S(1)}, u32[]{:S(2)}, u32[]{:S(2)}) collective-permute-start(bf16[3,8,384]{2,1,0:T(8,128)(2,1)S(1)} %pad.4), channel_id=1, source_target_pairs={{0,4},{2,6},{4,8},{6,10},{8,12},{10,14},{12,0},{14,2},{16,132},{18... | collective-permute-start | bytes 55304 | tf_op jit(solution)/shard_map/ppermute | solution.py:105
  65.1 2.7 %shard_map.64.rest_0_ = bf16[368,768]{1,0:T(8,128)(2,1)} custom-call(s32[1]{0:T(128)} %bitcast.4.y, bf16[288,768]{1,0:T(8,128)(2,1)} %bitcast.23, bf16[3,8,384]{2,1,0:T(8,128)(2,1)} %copy-done.16, bf16[3,8,384]{2,1,0:T(8,128)(2,1)} %copy-done.15, bf16[3,8,384]{2,1,0:T(8,128)(2,1)} %copy-done.14, bf16[3,8,384]{2,1,0:T(8,128)(2,1)} %copy-done.13, ...), custom_call_target="tpu_custom_call" | custom-call | flops 1000000 | bytes 2000000 | tf_op jit(solution)/shard_map/pallas_call | solution.py:36
  68.9 2.7 %reshape.28 = bf16[64,2,2304]{2,1,0:T(2,128)(2,1)} reshape(bf16[8,8,6,768]{3,2,1,0:T(8,128)(2,1)} %copy.17) | data formatting | bytes 1179648 | tf_op jit(solution)/shard_map/reshape | solution.py:129
  71.7 31.4 %all-to-all-start.1 = ((bf16[64,2,2304]{2,1,0:T(2,128)(2,1)}), bf16[64,2,2304]{2,1,0:T(2,128)(2,1)}, u32[]{:S(2)}, u32[]{:S(2)}) async-start(bf16[64,2,2304]{2,1,0:T(2,128)(2,1)} %reshape.28), calls=%async_computation.1 | async-start | bytes 1179648 | tf_op jit(solution)/shard_map/all_to_all | solution.py:130
  105.1 3.6 %collective-permute-start.11 = (bf16[368,768]{1,0:T(8,128)(2,1)S(1)}, bf16[368,768]{1,0:T(8,128)(2,1)S(1)}, u32[]{:S(2)}, u32[]{:S(2)}) collective-permute-start(bf16[368,768]{1,0:T(8,128)(2,1)S(1)} %copy-done.1), channel_id=1, source_target_pairs={{0,384},{128,0},{256,128},{384,256},{1,385},{129,1},{257,129},{385... | collective-permute-start | bytes 1695752 | tf_op jit(solution)/shard_map/ppermute | solution.py:118
  108.7 1.9 %collective-permute-start.10 = (bf16[368,768]{1,0:T(8,128)(2,1)S(1)}, bf16[368,768]{1,0:T(8,128)(2,1)}, u32[]{:S(2)}, u32[]{:S(2)}) collective-permute-start(bf16[368,768]{1,0:T(8,128)(2,1)S(1)} %copy-done.1), channel_id=1, source_target_pairs={{0,128},{128,256},{256,384},{384,0},{1,129},{129,257},{257,385},{3... | collective-permute-start | bytes 1695752 | tf_op jit(solution)/shard_map/ppermute | solution.py:118
  110.6 3.0 %collective-permute-start.13 = (bf16[368,768]{1,0:T(8,128)(2,1)S(1)}, bf16[368,768]{1,0:T(8,128)(2,1)}, u32[]{:S(2)}, u32[]{:S(2)}) collective-permute-start(bf16[368,768]{1,0:T(8,128)(2,1)S(1)} %copy-done.1), channel_id=1, source_target_pairs={{0,1},{1,0},{2,3},{3,2},{4,5},{5,4},{6,7},{7,6},{8,9},{9,8},{10,11... | collective-permute-start | bytes 1695752 | tf_op jit(solution)/shard_map/ppermute | solution.py:120
  113.6 6.9 %collective-permute-done.12.rest_3_ = bf16[368,768]{1,0:T(8,128)(2,1)S(1)} collective-permute-done((bf16[368,768]{1,0:T(8,128)(2,1)S(1)}, bf16[368,768]{1,0:T(8,128)(2,1)S(1)}, u32[]{:S(2)}, u32[]{:S(2)}) %collective-permute-start.12) | collective-permute-done | bytes 565280 | tf_op jit(solution)/shard_map/ppermute | solution.py:118
  120.5 4.1 %collective-permute-start.16 = (bf16[368,768]{1,0:T(8,128)(2,1)S(1)}, bf16[368,768]{1,0:T(8,128)(2,1)}, u32[]{:S(2)}, u32[]{:S(2)}) collective-permute-start(bf16[368,768]{1,0:T(8,128)(2,1)S(1)} %collective-permute-done.12.rest_3_), channel_id=1, source_target_pairs={{0,1},{1,0},{2,3},{3,2},{4,5},{5,4},{6,7},{7,6},{8,9},{9,8},{10,11... | collective-permute-start | bytes 1695752 | tf_op jit(solution)/shard_map/ppermute | solution.py:120
  124.7 5.9 %collective-permute-done.11.rest_2_ = bf16[368,768]{1,0:T(8,128)(2,1)S(1)} collective-permute-done((bf16[368,768]{1,0:T(8,128)(2,1)S(1)}, bf16[368,768]{1,0:T(8,128)(2,1)S(1)}, u32[]{:S(2)}, u32[]{:S(2)}) %collective-permute-start.11) | collective-permute-done | bytes 565280 | tf_op jit(solution)/shard_map/ppermute | solution.py:118
  130.6 3.2 %collective-permute-start.15 = (bf16[368,768]{1,0:T(8,128)(2,1)S(1)}, bf16[368,768]{1,0:T(8,128)(2,1)}, u32[]{:S(2)}, u32[]{:S(2)}) collective-permute-start(bf16[368,768]{1,0:T(8,128)(2,1)S(1)} %collective-permute-done.11.rest_2_), channel_id=1, source_target_pairs={{0,1},{1,0},{2,3},{3,2},{4,5},{5,4},{6,7},{7,6},{8,9},{9,8},{10,11... | collective-permute-start | bytes 1695752 | tf_op jit(solution)/shard_map/ppermute | solution.py:120
  133.7 2.1 %collective-permute-start.14 = (bf16[368,768]{1,0:T(8,128)(2,1)}, bf16[368,768]{1,0:T(8,128)(2,1)}, u32[]{:S(2)}, u32[]{:S(2)}) collective-permute-start(bf16[368,768]{1,0:T(8,128)(2,1)} %collective-permute-done.10.rest_1_), channel_id=1, source_target_pairs={{0,1},{1,0},{2,3},{3,2},{4,5},{5,4},{6,7},{7,6},{8,9},{9,8},{10,11... | collective-permute-start | bytes 1695752 | tf_op jit(solution)/shard_map/ppermute | solution.py:120
  136.1 2.1 %reshape.29.field = bf16[384,768]{1,0:T(8,128)(2,1)S(1)} reshape(bf16[64,2,2304]{2,1,0:T(2,128)(2,1)} %all-to-all-done.1) | data formatting | bytes 1179648 | tf_op jit(solution)/shard_map/reshape | solution.py:130
  139.3 7.2 %shard_map.65 = bf16[384,768]{1,0:T(8,128)(2,1)S(1)} custom-call(s32[2,8]{1,0:T(2,128)S(1)} %pad_add_fusion.place, f32[3]{0:T(128)S(1)} %copy-done.4, f32[1]{0:T(128)} %collective-permute-done.9.member, bf16[384,768]{1,0:T(8,128)(2,1)S(1)} %reshape.29.field, bf16[368,768]{1,0:T(8,128)(2,1)S(1)} %copy-done.1, ...), custom_call_target="tpu_custom_call" | custom-call | flops 2000000000 | bytes 5000000 | tf_op jit(solution)/shard_map/pallas_call | solution.py:81
  146.9 29.6 %all_to_all.15 = bf16[64,2,2304]{2,1,0:T(2,128)(2,1)S(1)} all-to-all(bf16[64,2,2304]{2,1,0:T(2,128)(2,1)S(1)} %reshape.30), channel_id=1, replica_groups=mesh['x'=4,'zh'=2,'zl'=4,'y'=8,'c'=2] {'zl','c','y'}, dimensions={0} | all-to-all | bytes 1179648 | tf_op jit(solution)/shard_map/all_to_all | solution.py:132
  176.8 1.9 %copy.18 = f32[4,2,6,4,2,768]{5,4,3,2,1,0:T(2,128)} copy(f32[4,2,6,4,2,768]{5,2,3,1,4,0:T(8,128)S(1)} %bitcast.21) | data formatting | bytes 2359296 | tf_op jit(solution)/shard_map/convert_element_type | solution.py:134
  178.8 2.2 %reshape.31 = f32[8,6,8,768]{3,2,1,0:T(8,128)S(1)} reshape(f32[4,2,6,4,2,768]{5,4,3,2,1,0:T(2,128)} %copy.18) | data formatting | bytes 2359296 | tf_op jit(solution)/shard_map/convert_element_type | solution.py:134
  (69 shorter events, 15.9 us)
Async XLA Ops:
  0.0 61.2 %copy-start = (f32[64,6,768]{2,0,1:T(8,128)S(1)}, f32[64,6,768]{2,0,1:T(8,128)}, u32[]{:S(2)}) copy-start(f32[64,6,768]{2,0,1:T(8,128)} %param.7) | copy-start | bytes 3538948
  0.0 15.3 %copy-start.17 = (bf16[3,96,768]{2,1,0:T(8,128)(2,1)S(1)}, bf16[3,96,768]{2,1,0:T(8,128)(2,1)}, u32[]{:S(2)}) copy-start(bf16[3,96,768]{2,1,0:T(8,128)(2,1)} %param.10) | copy-start | bytes 1327108
  0.0 23.7 %copy-start.8 = (bf16[3,6,384]{2,1,0:T(8,128)(2,1)S(1)}, bf16[3,6,384]{2,1,0:T(8,128)(2,1)}, u32[]{:S(2)}) copy-start(bf16[3,6,384]{2,1,0:T(8,128)(2,1)} %param.11) | copy-start | bytes 41476
  2.0 62.3 %all-to-all-start = ((bf16[8,6,8,768]{3,2,1,0:T(8,128)(2,1)}), bf16[8,6,8,768]{3,2,1,0:T(8,128)(2,1)S(1)}, u32[]{:S(2)}, u32[]{:S(2)}) async-start(bf16[8,6,8,768]{3,2,1,0:T(8,128)(2,1)} %copy.16), calls=%async_computation | async-start | bytes 1179648 | tf_op jit(solution)/shard_map/all_to_all | solution.py:102
  15.3 49.0 %collective-permute-start = (bf16[3,96,768]{2,1,0:T(8,128)(2,1)S(1)}, bf16[3,96,768]{2,1,0:T(8,128)(2,1)S(1)}, u32[]{:S(2)}, u32[]{:S(2)}) collective-permute-start(bf16[3,96,768]{2,1,0:T(8,128)(2,1)S(1)} %copy-done.17), channel_id=1, source_target_pairs={{0,0},{1,64},{64,1},{65,65},{2,2},{3,66},{66,3},{67,67},{4,4},{5,6... | collective-permute-start | bytes 1327112 | tf_op jit(solution)/shard_map/ppermute | solution.py:100
  23.8 30.5 %collective-permute-start.8 = (bf16[3,8,384]{2,1,0:T(8,128)(2,1)S(1)}, bf16[3,8,384]{2,1,0:T(8,128)(2,1)S(1)}, u32[]{:S(2)}, u32[]{:S(2)}) collective-permute-start(bf16[3,8,384]{2,1,0:T(8,128)(2,1)S(1)} %pad.4), channel_id=1, source_target_pairs={{0,14},{2,0},{4,2},{6,4},{8,6},{10,8},{12,10},{14,12},{16,142},{18... | collective-permute-start | bytes 55304 | tf_op jit(solution)/shard_map/ppermute | solution.py:105
  28.9 27.4 %collective-permute-start.7 = (bf16[3,8,384]{2,1,0:T(8,128)(2,1)S(1)}, bf16[3,8,384]{2,1,0:T(8,128)(2,1)S(1)}, u32[]{:S(2)}, u32[]{:S(2)}) collective-permute-start(bf16[3,8,384]{2,1,0:T(8,128)(2,1)S(1)} %pad.4), channel_id=1, source_target_pairs={{0,12},{2,14},{4,0},{6,2},{8,4},{10,6},{12,8},{14,10},{16,140},{18... | collective-permute-start | bytes 55304 | tf_op jit(solution)/shard_map/ppermute | solution.py:105
  32.6 25.9 %collective-permute-start.6 = (bf16[3,8,384]{2,1,0:T(8,128)(2,1)S(1)}, bf16[3,8,384]{2,1,0:T(8,128)(2,1)S(1)}, u32[]{:S(2)}, u32[]{:S(2)}) collective-permute-start(bf16[3,8,384]{2,1,0:T(8,128)(2,1)S(1)} %pad.4), channel_id=1, source_target_pairs={{0,10},{2,12},{4,14},{6,0},{8,2},{10,4},{12,6},{14,8},{16,138},{18... | collective-permute-start | bytes 55304 | tf_op jit(solution)/shard_map/ppermute | solution.py:105
  35.4 1.9 %collective-permute-start.9 = (f32[1]{0:T(128)}, f32[1]{0:T(128)}, u32[]{:S(2)}, u32[]{:S(2)}) collective-permute-start(f32[1]{0:T(128)} %param.8), channel_id=1, source_target_pairs={{0,0},{1,1},{2,2},{3,3},{4,4},{5,5},{6,6},{7,7},{64,8},{65,9},{66,... | collective-permute-start | bytes 20 | tf_op jit(solution)/shard_map/ppermute | solution.py:112
  37.3 23.3 %collective-permute-start.5 = (bf16[3,8,384]{2,1,0:T(8,128)(2,1)S(1)}, bf16[3,8,384]{2,1,0:T(8,128)(2,1)S(1)}, u32[]{:S(2)}, u32[]{:S(2)}) collective-permute-start(bf16[3,8,384]{2,1,0:T(8,128)(2,1)S(1)} %pad.4), channel_id=1, source_target_pairs={{0,8},{2,10},{4,12},{6,14},{8,0},{10,2},{12,4},{14,6},{16,136},{18... | collective-permute-start | bytes 55304 | tf_op jit(solution)/shard_map/ppermute | solution.py:105
  54.3 7.5 %collective-permute-start.4 = (bf16[3,8,384]{2,1,0:T(8,128)(2,1)S(1)}, bf16[3,8,384]{2,1,0:T(8,128)(2,1)S(1)}, u32[]{:S(2)}, u32[]{:S(2)}) collective-permute-start(bf16[3,8,384]{2,1,0:T(8,128)(2,1)S(1)} %pad.4), channel_id=1, source_target_pairs={{0,6},{2,8},{4,10},{6,12},{8,14},{10,0},{12,2},{14,4},{16,134},{18... | collective-permute-start | bytes 55304 | tf_op jit(solution)/shard_map/ppermute | solution.py:105
  56.3 6.7 %collective-permute-start.3 = (bf16[3,8,384]{2,1,0:T(8,128)(2,1)S(1)}, bf16[3,8,384]{2,1,0:T(8,128)(2,1)S(1)}, u32[]{:S(2)}, u32[]{:S(2)}) collective-permute-start(bf16[3,8,384]{2,1,0:T(8,128)(2,1)S(1)} %pad.4), channel_id=1, source_target_pairs={{0,4},{2,6},{4,8},{6,10},{8,12},{10,14},{12,0},{14,2},{16,132},{18... | collective-permute-start | bytes 55304 | tf_op jit(solution)/shard_map/ppermute | solution.py:105
  58.6 5.7 %collective-permute-start.2 = (bf16[3,8,384]{2,1,0:T(8,128)(2,1)S(1)}, bf16[3,8,384]{2,1,0:T(8,128)(2,1)S(1)}, u32[]{:S(2)}, u32[]{:S(2)}) collective-permute-start(bf16[3,8,384]{2,1,0:T(8,128)(2,1)S(1)} %pad.4), channel_id=1, source_target_pairs={{0,2},{2,4},{4,6},{6,8},{8,10},{10,12},{12,14},{14,0},{16,130},{18... | collective-permute-start | bytes 55304 | tf_op jit(solution)/shard_map/ppermute | solution.py:105
  60.5 3.8 %collective-permute-start.1 = (bf16[3,8,384]{2,1,0:T(8,128)(2,1)S(1)}, bf16[3,8,384]{2,1,0:T(8,128)(2,1)S(1)}, u32[]{:S(2)}, u32[]{:S(2)}) collective-permute-start(bf16[3,8,384]{2,1,0:T(8,128)(2,1)S(1)} %pad.4), channel_id=1, source_target_pairs={{0,0},{2,2},{4,4},{6,6},{8,8},{10,10},{12,12},{14,14},{16,128},{18... | collective-permute-start | bytes 55304 | tf_op jit(solution)/shard_map/ppermute | solution.py:105
  68.9 34.2 %copy-start.1 = (bf16[368,768]{1,0:T(8,128)(2,1)S(1)}, bf16[368,768]{1,0:T(8,128)(2,1)}, u32[]{:S(2)}) copy-start(bf16[368,768]{1,0:T(8,128)(2,1)} %shard_map.64.rest_0_) | copy-start | bytes 1695748
  71.7 66.6 %copy-start.4 = (f32[3]{0:T(128)S(1)}, f32[3]{0:T(128)}, u32[]{:S(2)}) copy-start(f32[3]{0:T(128)} %scale.1) | copy-start | bytes 40
  71.7 64.4 %all-to-all-start.1 = ((bf16[64,2,2304]{2,1,0:T(2,128)(2,1)}), bf16[64,2,2304]{2,1,0:T(2,128)(2,1)}, u32[]{:S(2)}, u32[]{:S(2)}) async-start(bf16[64,2,2304]{2,1,0:T(2,128)(2,1)} %reshape.28), calls=%async_computation.1 | async-start | bytes 1179648 | tf_op jit(solution)/shard_map/all_to_all | solution.py:130
  103.1 17.4 %collective-permute-start.12 = (bf16[368,768]{1,0:T(8,128)(2,1)S(1)}, bf16[368,768]{1,0:T(8,128)(2,1)S(1)}, u32[]{:S(2)}, u32[]{:S(2)}) collective-permute-start(bf16[368,768]{1,0:T(8,128)(2,1)S(1)} %copy-done.1), channel_id=1, source_target_pairs={{0,256},{128,384},{256,0},{384,128},{1,257},{129,385},{257,1},{385... | collective-permute-start | bytes 1695752 | tf_op jit(solution)/shard_map/ppermute | solution.py:118
  105.1 25.5 %collective-permute-start.11 = (bf16[368,768]{1,0:T(8,128)(2,1)S(1)}, bf16[368,768]{1,0:T(8,128)(2,1)S(1)}, u32[]{:S(2)}, u32[]{:S(2)}) collective-permute-start(bf16[368,768]{1,0:T(8,128)(2,1)S(1)} %copy-done.1), channel_id=1, source_target_pairs={{0,384},{128,0},{256,128},{384,256},{1,385},{129,1},{257,129},{385... | collective-permute-start | bytes 1695752 | tf_op jit(solution)/shard_map/ppermute | solution.py:118
  108.7 25.0 %collective-permute-start.10 = (bf16[368,768]{1,0:T(8,128)(2,1)S(1)}, bf16[368,768]{1,0:T(8,128)(2,1)}, u32[]{:S(2)}, u32[]{:S(2)}) collective-permute-start(bf16[368,768]{1,0:T(8,128)(2,1)S(1)} %copy-done.1), channel_id=1, source_target_pairs={{0,128},{128,256},{256,384},{384,0},{1,129},{129,257},{257,385},{3... | collective-permute-start | bytes 1695752 | tf_op jit(solution)/shard_map/ppermute | solution.py:118
  110.6 27.6 %collective-permute-start.13 = (bf16[368,768]{1,0:T(8,128)(2,1)S(1)}, bf16[368,768]{1,0:T(8,128)(2,1)}, u32[]{:S(2)}, u32[]{:S(2)}) collective-permute-start(bf16[368,768]{1,0:T(8,128)(2,1)S(1)} %copy-done.1), channel_id=1, source_target_pairs={{0,1},{1,0},{2,3},{3,2},{4,5},{5,4},{6,7},{7,6},{8,9},{9,8},{10,11... | collective-permute-start | bytes 1695752 | tf_op jit(solution)/shard_map/ppermute | solution.py:120
  120.5 17.7 %collective-permute-start.16 = (bf16[368,768]{1,0:T(8,128)(2,1)S(1)}, bf16[368,768]{1,0:T(8,128)(2,1)}, u32[]{:S(2)}, u32[]{:S(2)}) collective-permute-start(bf16[368,768]{1,0:T(8,128)(2,1)S(1)} %collective-permute-done.12.rest_3_), channel_id=1, source_target_pairs={{0,1},{1,0},{2,3},{3,2},{4,5},{5,4},{6,7},{7,6},{8,9},{9,8},{10,11... | collective-permute-start | bytes 1695752 | tf_op jit(solution)/shard_map/ppermute | solution.py:120
  130.6 7.7 %collective-permute-start.15 = (bf16[368,768]{1,0:T(8,128)(2,1)S(1)}, bf16[368,768]{1,0:T(8,128)(2,1)}, u32[]{:S(2)}, u32[]{:S(2)}) collective-permute-start(bf16[368,768]{1,0:T(8,128)(2,1)S(1)} %collective-permute-done.11.rest_2_), channel_id=1, source_target_pairs={{0,1},{1,0},{2,3},{3,2},{4,5},{5,4},{6,7},{7,6},{8,9},{9,8},{10,11... | collective-permute-start | bytes 1695752 | tf_op jit(solution)/shard_map/ppermute | solution.py:120
  133.7 4.5 %collective-permute-start.14 = (bf16[368,768]{1,0:T(8,128)(2,1)}, bf16[368,768]{1,0:T(8,128)(2,1)}, u32[]{:S(2)}, u32[]{:S(2)}) collective-permute-start(bf16[368,768]{1,0:T(8,128)(2,1)} %collective-permute-done.10.rest_1_), channel_id=1, source_target_pairs={{0,1},{1,0},{2,3},{3,2},{4,5},{5,4},{6,7},{7,6},{8,9},{9,8},{10,11... | collective-permute-start | bytes 1695752 | tf_op jit(solution)/shard_map/ppermute | solution.py:120
  (13 other events, 48.3 us)

commit v3 on v2

v3 whole, which is shorter than its diff:
```python
import jax
import jax.numpy as jnp
from jax import lax
from jax.experimental import pallas as pl
from jax.experimental.pallas import tpu as pltpu
from jax.sharding import Mesh, PartitionSpec as P

MEM = ("x", "zh")
COL = ("zl", "y", "c")
SWAP = [(0, 1), (1, 0)]
F32, BF16 = jnp.float32, jnp.bfloat16


VMEM = pl.BlockSpec(memory_space=pltpu.VMEM)
SMEM = pl.BlockSpec(memory_space=pltpu.SMEM)
ANY = pl.BlockSpec(memory_space=pl.ANY)
PLACES = ((288, 0, 48, 0, 0), (288, 384, 48, 1, 0), (336, 0, 32, 2, 0), (336, 384, 16, 2, 32))


def pack_kernel(block, tiles, out, sem):
    copy = pltpu.make_async_copy(block, out.at[pl.ds(0, 288)], sem)
    copy.start()
    for row, column, rows, s, first in PLACES:
        whole = jnp.concatenate([tiles[n, s, :6, :].astype(F32) for n in range(8)], axis=0)
        out[pl.ds(row, rows), pl.ds(column, 384)] = whole[first : first + rows].astype(BF16)
    out[pl.ds(352, 16), pl.ds(384, 384)] = jnp.zeros((16, 384), BF16)
    copy.wait()


def pack(block, tiles):
    return pl.pallas_call(
        pack_kernel,
        out_shape=jax.ShapeDtypeStruct((368, 768), BF16),
        in_specs=[ANY, VMEM],
        out_specs=VMEM,
        scratch_shapes=[pltpu.SemaphoreType.DMA],
        cost_estimate=pl.CostEstimate(flops=10**6, bytes_accessed=2 * 10**6, transcendentals=0),
    )(block, tiles)


def filter_kernel(core, scale, member, field, mine, other, out, lon, lat, mid, lon_sems, lat_sems):
    lon_copies, lat_copies = [], []
    for n in range(8):
        x, part, half = n % 4, (mine, other)[n // 4], (core[0], 1 - core[0])[n // 4]
        for m, (row, column, rows, s, first) in enumerate(PLACES):
            to = pl.ds(pl.multiple_of((2 * x + half) * 48 + first, 16), rows)
            copy = pltpu.make_async_copy(
                part.at[x, pl.ds(row, rows), pl.ds(column, 384)], lat.at[s, to, :], lat_sems.at[n, m]
            )
            copy.start()
            lat_copies.append(copy)
    for n in range(8):
        x, part, half = n % 4, (mine, other)[n // 4], (core[0], 1 - core[0])[n // 4]
        for s in range(3):
            to = pl.ds(pl.multiple_of((2 * x + half) * 96, 32), 96)
            copy = pltpu.make_async_copy(
                part.at[x, pl.ds(96 * s, 96), :], lon.at[s, to, :], lon_sems.at[n, s]
            )
            copy.start()
            lon_copies.append(copy)
    for copy in lat_copies:
        copy.wait()
    for s in range(3):
        across = jnp.dot(lat[s], field[...], preferred_element_type=F32)
        mid[s] = (scale[s] * member[0] * across).astype(BF16)
    for copy in lon_copies:
        copy.wait()
    total = jnp.zeros(out.shape, F32)
    for s in range(3):
        total += lax.dot_general(
            mid[s], lon[s], (((1,), (1,)), ((), ())), preferred_element_type=F32
        )
    out[...] = total.astype(BF16)


def filter_pair(core, scale, member, field, mine, other):
    return pl.pallas_call(
        filter_kernel,
        out_shape=jax.ShapeDtypeStruct((384, 768), BF16),
        in_specs=[SMEM, SMEM, SMEM, VMEM, ANY, ANY],
        out_specs=VMEM,
        scratch_shapes=[
            pltpu.VMEM((3, 768, 768), BF16),
            pltpu.VMEM((3, 384, 384), BF16),
            pltpu.VMEM((3, 384, 768), BF16),
            pltpu.SemaphoreType.DMA((8, 3)),
            pltpu.SemaphoreType.DMA((8, 4)),
        ],
        compiler_params=pltpu.CompilerParams(vmem_limit_bytes=40 * 2**20),
        cost_estimate=pl.CostEstimate(flops=2 * 10**9, bytes_accessed=5 * 10**6, transcendentals=0),
    )(core, scale, member, field, mine, other)


def final_kernel(own, back, out):
    for r in range(6):
        total = jnp.zeros((8, 768), F32)
        for k in range(8):
            parts = [
                back[k // 2, l % 2, 4 * (k % 2) + l // 2, r, :].astype(F32).reshape(1, 768)
                for l in range(8)
            ]
            total += own[k, r].astype(F32) * jnp.concatenate(parts, axis=0)
        out[r] = total


def final_sum(own, back):
    return pl.pallas_call(
        final_kernel,
        out_shape=jax.ShapeDtypeStruct((6, 8, 768), F32),
        in_specs=[VMEM, VMEM],
        out_specs=VMEM,
        cost_estimate=pl.CostEstimate(flops=10**6, bytes_accessed=2 * 10**6, transcendentals=0),
    )(own, back)


def on_device(perturbations, gradient, member_weights, scale_weights, lon_filter, lat_filter):
    core = lax.axis_index("c")
    own = perturbations[0].transpose(1, 0, 2).reshape(6, 8, 8, 768).transpose(1, 0, 2, 3)
    own = lax.all_to_all(own, MEM, split_axis=0, concat_axis=0, tiled=True)
    block = lax.ppermute(lon_filter, ("zh", "c"), [(0, 0), (1, 2), (2, 1), (3, 3)])
    rows = jnp.pad(lat_filter, ((0, 0), (0, 2), (0, 0)))
    rows = lax.ppermute(rows, ("x", "zl"), [(4 * a + b, 4 * b + a) for a in range(4) for b in range(4)])
    tiles = jnp.broadcast_to(rows[None], (8, 3, 8, 384))
    tiles = lax.all_to_all(tiles, "y", split_axis=0, concat_axis=0, tiled=True)
    packed = pack(block.reshape(288, 768), tiles)
    mine = lax.all_gather(packed, "x", axis=0)
    member = lax.axis_index(MEM)
    level = lax.dynamic_slice_in_dim(gradient.transpose(1, 0, 2), member * 8, 8, axis=1)
    schur = (own.astype(F32) * level[None]).astype(BF16)
    schur = schur.transpose(0, 2, 1, 3).reshape(64, 2, 2304)
    turn = [((c // 8) * 64 + m * 8 + c % 8, m * 64 + c) for m in range(8) for c in range(64)]
    weight = lax.optimization_barrier((member_weights, schur))[0]
    weight = lax.ppermute(weight, MEM + COL, turn)
    mine = lax.optimization_barrier((mine, schur))[0]
    other = lax.ppermute(mine, "c", SWAP)
    field = lax.all_to_all(schur, COL, split_axis=0, concat_axis=0, tiled=True).reshape(384, 768)
    core = core.reshape(1).astype(jnp.int32)
    filtered = filter_pair(core, scale_weights, weight, field, mine, other).reshape(64, 2, 2304)
    back = lax.all_to_all(filtered, ("zl", "c", "y"), split_axis=0, concat_axis=0, tiled=True)
    return final_sum(own, back.reshape(4, 2, 8, 6, 768)).transpose(1, 0, 2)


def solution(mesh):
    fine = Mesh(mesh.devices.reshape(4, 2, 4, 8, 2), MEM + COL)
    placed = (
        P(MEM, None, COL, None),
        P(None, COL, None),
        P(MEM),
        P(),
        P(None, MEM, None),
        P(None, COL, None),
    )
    return jax.shard_map(
        on_device, mesh=fine, in_specs=placed, out_specs=P(MEM, COL, None), check_vma=False
    )
```

time: 183 us -> 162 us (0.89)
  starting transfers between devices: 110 us -> 40.4 us
  waiting for transfers between devices: 15.9 us -> 45.4 us
  between operations: 0.52 us -> 13.5 us
  blocking collectives: 29.6 us -> 40.3 us
  local copies, waits for them, and re-layouts: 14.5 us -> 8 us
  Pallas kernels: 9.92 us -> 13.4 us
    ppermute x16 -> x3, starting transfers between devices: 57.2 us -> 5.13 us  [the longest x1 2.65 us: on_device(): other = lax.ppermute(mine, 'c', SWAP)]
    all_to_all x1, starting transfers between devices: 31.4 us -> 8.74 us  [on_device(): lax.all_to_all(schur, COL, split_axis=0, concat_axis=0, tiled=True)]
    all_to_all x1, waiting for transfers between devices: 0.01 us -> 17.2 us  [on_device(): lax.all_to_all(schur, COL, split_axis=0, concat_axis=0, tiled=True)]
    all_gather x0 -> x1, waiting for transfers between devices: none -> 16.2 us  [on_device(): mine = lax.all_gather(packed, 'x', axis=0)]
    ppermute x16 -> x3, waiting for transfers between devices: 15.8 us -> 0.01 us  [the longest x1 0.01 us: on_device(): weight = lax.ppermute(weight, MEM + COL, turn)]
    all_to_all x0 -> x1, blocking collectives: none -> 14.8 us  [on_device(): tiles = lax.all_to_all(tiles, 'y', split_axis=0, concat_axis=0, tiled=True)]
    all_to_all x1, waiting for transfers between devices: 0.01 us -> 12 us  [on_device(): own = lax.all_to_all(own, MEM, split_axis=0, concat_axis=0, tiled=True)]
    convert_element_type x3 -> x0, local copies, waits for them, and re-layouts: 4.41 us -> none  [on_device(): return jnp.sum(own * back.astype(F32), axis=0).transpose(1, 0, 2)]
  transfers between devices with their start and end apart: 19 -> 7, of which waited for: 5 -> 3; matrix products, arithmetic and copies ran while one was open for 1% -> 2% of each run, Pallas kernels for 0% -> 0%
where the time goes in v3:
time: 162 us; the launch traced here: 161 us
  waiting for transfers between devices  45.4 us (28%)
  starting transfers between devices  40.4 us (25%)
  blocking collectives  40.3 us (25%)
  between operations  13.5 us (8%)
  Pallas kernels  13.4 us (8%)
  local copies, waits for them, and re-layouts  8 us (5%)
    all_to_all x1, blocking collectives, on_device(): lax.all_to_all(filtered, ('zl', 'c', 'y'), split_axis=0, concat_axis=0, t...  25.5 us
    all_to_all x1, waiting for transfers between devices, on_device(): lax.all_to_all(schur, COL, split_axis=0, concat_axis=0, tiled=True)  17.2 us
    all_gather x1, waiting for transfers between devices, on_device(): mine = lax.all_gather(packed, 'x', axis=0)  16.2 us
    all_to_all x1, blocking collectives, on_device(): tiles = lax.all_to_all(tiles, 'y', split_axis=0, concat_axis=0, tiled=True)  14.8 us
    all_to_all x1, starting transfers between devices, on_device(): own = lax.all_to_all(own, MEM, split_axis=0, concat_axis=0, tiled=True)  14.4 us
    ppermute x1, starting transfers between devices, on_device(): lax.ppermute(lon_filter, ('zh', 'c'), [(0, 0), (1, 2), (2, 1), (3, 3)])  12.1 us
    all_to_all x1, waiting for transfers between devices, on_device(): own = lax.all_to_all(own, MEM, split_axis=0, concat_axis=0, tiled=True)  12 us
    all_to_all x1, starting transfers between devices, on_device(): lax.all_to_all(schur, COL, split_axis=0, concat_axis=0, tiled=True)  8.74 us
  transfers between devices with their start and end apart: 7, of which 3 were waited for; matrix products, arithmetic and copies ran while one was open for 2% of the time, Pallas kernels for 0%

profile of v3, /device:TPU:1, one launch (start us, length us, event | category | flops | bytes accessed | tf_op | source)
XLA Modules:
  0.0 161.1 jit_solution(16894234519422531432)
XLA Ops:
  6.5 12.1 %collective-permute-start.1 = (bf16[3,96,768]{2,1,0:T(8,128)(2,1)}, bf16[3,96,768]{2,1,0:T(8,128)(2,1)S(1)}, u32[]{:S(2)}, u32[]{:S(2)}) collective-permute-start(bf16[3,96,768]{2,1,0:T(8,128)(2,1)} %param.10), channel_id=1, source_target_pairs={{0,0},{1,64},{64,1},{65,65},{2,2},{3,66},{66,3},{67,67},{4,4},{5,6... | collective-permute-start | bytes 1327112 | tf_op jit(solution)/shard_map/ppermute | solution.py:120
  18.7 0.7 pad.4
  19.4 0.7 collective-permute-start.2
  20.1 14.8 %all_to_all.20.tiles = bf16[8,3,8,384]{3,2,1,0:T(8,128)(2,1)} all-to-all(bf16[8,3,8,384]{3,2,1,0:T(8,128)(2,1)S(1)} %broadcast_in_dim.2), channel_id=1, replica_groups=mesh['x'=4,'zh'=2,'zl'=4,'y'=8,'c'=2] {'y'}, dimensions={0} | all-to-all | bytes 294912 | tf_op jit(solution)/shard_map/all_to_all | solution.py:124
  35.0 0.8 copy-done.5
  35.7 2.7 %shard_map.64 = bf16[368,768]{1,0:T(8,128)(2,1)} custom-call(bf16[288,768]{1,0:T(8,128)(2,1)} %bitcast.19, bf16[8,3,8,384]{3,2,1,0:T(8,128)(2,1)} %all_to_all.20.tiles), custom_call_target="tpu_custom_call" | custom-call | flops 1000000 | bytes 2000000 | tf_op jit(solution)/shard_map/pallas_call | solution.py:31
  38.5 0.9 copy_bitcast_fusion
  39.4 14.4 %all-to-all-start = ((bf16[8,6,8,768]{3,2,1,0:T(8,128)(2,1)}), bf16[8,6,8,768]{3,2,1,0:T(8,128)(2,1)S(1)}, u32[]{:S(2)}, u32[]{:S(2)}) async-start(bf16[8,6,8,768]{3,2,1,0:T(8,128)(2,1)} %copy_bitcast_fusion), calls=%async_computation | async-start | bytes 1179648 | tf_op jit(solution)/shard_map/all_to_all | solution.py:119
  53.8 12.0 %all-to-all-done.own = bf16[8,6,8,768]{3,2,1,0:T(8,128)(2,1)S(1)} async-done(((bf16[8,6,8,768]{3,2,1,0:T(8,128)(2,1)}), bf16[8,6,8,768]{3,2,1,0:T(8,128)(2,1)S(1)}, u32[]{:S(2)}, u32[]{:S(2)}) %all-to-all-start) | async-done | bytes 589856 | tf_op jit(solution)/shard_map/all_to_all | solution.py:119
  65.9 0.1 copy.8
  66.0 0.6 copy-done.3
  66.6 1.3 reshape.25
  67.8 16.2 %all-gather.3.cloned.1.call-done = bf16[1472,768]{1,0:T(8,128)(2,1)} async-done(((bf16[368,768]{1,0:T(8,128)(2,1)}), bf16[1472,768]{1,0:T(8,128)(2,1)}) %all-gather.3.cloned.1.call-update) | async-done | bytes 2261008 | tf_op jit(solution)/shard_map/all_gather | solution.py:126
  84.1 2.6 %collective-permute-start.3 = (bf16[4,368,768]{2,1,0:T(8,128)(2,1)}, bf16[4,368,768]{2,1,0:T(8,128)(2,1)}, u32[]{:S(2)}, u32[]{:S(2)}) collective-permute-start(bf16[4,368,768]{2,1,0:T(8,128)(2,1)} %bitcast.17), channel_id=1, source_target_pairs={{0,1},{1,0},{2,3},{3,2},{4,5},{5,4},{6,7},{7,6},{8,9},{9,8},{10,11... | collective-permute-start | bytes 6782984 | tf_op jit(solution)/shard_map/ppermute | solution.py:135
  86.7 8.7 %all-to-all-start.1 = ((bf16[64,2,2304]{2,1,0:T(2,128)(2,1)}), bf16[64,2,2304]{2,1,0:T(2,128)(2,1)S(1)}, u32[]{:S(2)}, u32[]{:S(2)}) async-start(bf16[64,2,2304]{2,1,0:T(2,128)(2,1)} %reshape.25), calls=%async_computation.1 | async-start | bytes 1179648 | tf_op jit(solution)/shard_map/all_to_all | solution.py:136
  95.5 1.8 %collective-permute-start = (f32[1]{0:T(128)}, f32[1]{0:T(128)}, u32[]{:S(2)}, u32[]{:S(2)}) collective-permute-start(f32[1]{0:T(128)} %param.8), channel_id=1, source_target_pairs={{0,0},{1,1},{2,2},{3,3},{4,4},{5,5},{6,6},{7,7},{64,8},{65,9},{66,... | collective-permute-start | bytes 20 | tf_op jit(solution)/shard_map/ppermute | solution.py:133
  97.3 17.2 %all-to-all-done.1 = bf16[64,2,2304]{2,1,0:T(2,128)(2,1)S(1)} async-done(((bf16[64,2,2304]{2,1,0:T(2,128)(2,1)}), bf16[64,2,2304]{2,1,0:T(2,128)(2,1)S(1)}, u32[]{:S(2)}, u32[]{:S(2)}) %all-to-all-start.1) | async-done | bytes 589856 | tf_op jit(solution)/shard_map/all_to_all | solution.py:136
  114.5 0.4 reshape.26.field
  114.9 1.6 %copy-done.1 = bf16[1472,768]{1,0:T(8,128)(2,1)S(1)} copy-done((bf16[1472,768]{1,0:T(8,128)(2,1)S(1)}, bf16[1472,768]{1,0:T(8,128)(2,1)}, u32[]{:S(2)}) %copy-start.1) | copy-done | bytes 2261016
  116.6 7.7 %shard_map.65 = bf16[384,768]{1,0:T(8,128)(2,1)S(1)} custom-call(s32[1]{0:T(128)} %bitcast.4.core, f32[3]{0:T(128)S(1)} %copy-done.2, f32[1]{0:T(128)} %collective-permute-done.member, bf16[384,768]{1,0:T(8,128)(2,1)S(1)} %reshape.26.field, bf16[4,368,768]{2,1,0:T(8,128)(2,1)S(1)} %bitcast.18, bf16[4,368,768]{2,1,0:T(8,128)(2,1)} %collective-permute-done.3.other), custom_call_target="tpu_custom_call" | custom-call | flops 2000000000 | bytes 5000000 | tf_op jit(solution)/shard_map/pallas_call | solution.py:77
  124.3 0.3 reshape.28
  124.6 25.5 %all_to_all.21 = bf16[64,2,2304]{2,1,0:T(2,128)(2,1)S(1)} all-to-all(bf16[64,2,2304]{2,1,0:T(2,128)(2,1)S(1)} %reshape.28), channel_id=1, replica_groups=mesh['x'=4,'zh'=2,'zl'=4,'y'=8,'c'=2] {'zl','c','y'}, dimensions={0} | all-to-all | bytes 1179648 | tf_op jit(solution)/shard_map/all_to_all | solution.py:139
  150.1 1.3 reshape.29.back
  151.4 2.9 %shard_map.66 = f32[6,8,768]{2,1,0:T(8,128)} custom-call(bf16[8,6,8,768]{3,2,1,0:T(8,128)(2,1)} %copy-done.3, bf16[4,2,8,6,768]{4,3,2,1,0:T(8,128)(2,1)} %reshape.29.back), custom_call_target="tpu_custom_call" | custom-call | flops 1000000 | bytes 2000000 | tf_op jit(solution)/shard_map/pallas_call | solution.py:107
  (18 shorter events, 0.2 us)
Async XLA Ops:
  6.5 47.2 %copy-start = (f32[64,6,768]{2,0,1:T(8,128)S(1)}, f32[64,6,768]{2,0,1:T(8,128)}, u32[]{:S(2)}) copy-start(f32[64,6,768]{2,0,1:T(8,128)} %param.7) | copy-start | bytes 3538948
  6.5 31.9 %copy-start.4 = (bf16[1,64,6,768]{3,1,2,0:T(8,128)(2,1)S(1)}, bf16[1,64,6,768]{3,1,2,0:T(8,128)(2,1)}, u32[]{:S(2)}) copy-start(bf16[1,64,6,768]{3,1,2,0:T(8,128)(2,1)} %param.6) | copy-start | bytes 1769476
  6.5 77.5 %all-gather.3.cloned.1.call-start = ((), (), s32[]{:S(2)}) async-start(), calls=%async_computation.4 | async-start | bytes 2826240 | tf_op jit(solution)/shard_map/all_gather | solution.py:126
  6.5 28.4 %collective-permute-start.1 = (bf16[3,96,768]{2,1,0:T(8,128)(2,1)}, bf16[3,96,768]{2,1,0:T(8,128)(2,1)S(1)}, u32[]{:S(2)}, u32[]{:S(2)}) collective-permute-start(bf16[3,96,768]{2,1,0:T(8,128)(2,1)} %param.10), channel_id=1, source_target_pairs={{0,0},{1,64},{64,1},{65,65},{2,2},{3,66},{66,3},{67,67},{4,4},{5,6... | collective-permute-start | bytes 1327112 | tf_op jit(solution)/shard_map/ppermute | solution.py:120
  19.4 0.7 collective-permute-start.2
  35.0 0.8 copy-start.5
  39.4 26.4 %all-to-all-start = ((bf16[8,6,8,768]{3,2,1,0:T(8,128)(2,1)}), bf16[8,6,8,768]{3,2,1,0:T(8,128)(2,1)S(1)}, u32[]{:S(2)}, u32[]{:S(2)}) async-start(bf16[8,6,8,768]{3,2,1,0:T(8,128)(2,1)} %copy_bitcast_fusion), calls=%async_computation | async-start | bytes 1179648 | tf_op jit(solution)/shard_map/all_to_all | solution.py:119
  65.7 0.8 copy-start.3
  84.1 30.8 %copy-start.2 = (f32[3]{0:T(128)S(1)}, f32[3]{0:T(128)}, u32[]{:S(2)}) copy-start(f32[3]{0:T(128)} %scale.1) | copy-start | bytes 40
  84.1 30.8 %collective-permute-start.3 = (bf16[4,368,768]{2,1,0:T(8,128)(2,1)}, bf16[4,368,768]{2,1,0:T(8,128)(2,1)}, u32[]{:S(2)}, u32[]{:S(2)}) collective-permute-start(bf16[4,368,768]{2,1,0:T(8,128)(2,1)} %bitcast.17), channel_id=1, source_target_pairs={{0,1},{1,0},{2,3},{3,2},{4,5},{5,4},{6,7},{7,6},{8,9},{9,8},{10,11... | collective-permute-start | bytes 6782984 | tf_op jit(solution)/shard_map/ppermute | solution.py:135
  86.7 27.8 %all-to-all-start.1 = ((bf16[64,2,2304]{2,1,0:T(2,128)(2,1)}), bf16[64,2,2304]{2,1,0:T(2,128)(2,1)S(1)}, u32[]{:S(2)}, u32[]{:S(2)}) async-start(bf16[64,2,2304]{2,1,0:T(2,128)(2,1)} %reshape.25), calls=%async_computation.1 | async-start | bytes 1179648 | tf_op jit(solution)/shard_map/all_to_all | solution.py:136
  95.5 19.4 %collective-permute-start = (f32[1]{0:T(128)}, f32[1]{0:T(128)}, u32[]{:S(2)}, u32[]{:S(2)}) collective-permute-start(f32[1]{0:T(128)} %param.8), channel_id=1, source_target_pairs={{0,0},{1,1},{2,2},{3,3},{4,4},{5,5},{6,6},{7,7},{64,8},{65,9},{66,... | collective-permute-start | bytes 20 | tf_op jit(solution)/shard_map/ppermute | solution.py:133
  114.9 1.6 %copy-start.1 = (bf16[1472,768]{1,0:T(8,128)(2,1)S(1)}, bf16[1472,768]{1,0:T(8,128)(2,1)}, u32[]{:S(2)}) copy-start(bf16[1472,768]{1,0:T(8,128)(2,1)} %all-gather.3.cloned.1.call-done) | copy-start | bytes 6782980
Sparse Core Ops, SparseCore 0:
  38.6 45.4 all-gather.2

commit v4 on v3

v4 whole, which is shorter than its diff:
```python
import jax
import jax.numpy as jnp
from jax import lax
from jax.experimental import pallas as pl
from jax.experimental.pallas import tpu as pltpu
from jax.sharding import Mesh, PartitionSpec as P

MEM = ("x", "zh")
COL = ("zl", "y", "c")
SWAP = [(0, 1), (1, 0)]
F32, BF16 = jnp.float32, jnp.bfloat16


VMEM = pl.BlockSpec(memory_space=pltpu.VMEM)
SMEM = pl.BlockSpec(memory_space=pltpu.SMEM)
ANY = pl.BlockSpec(memory_space=pl.ANY)
HBM = pl.BlockSpec(memory_space=pltpu.MemorySpace.HBM)


def pack_kernel(block, tiles, out, sem):
    copy = pltpu.make_async_copy(block, out.at[pl.ds(0, 288)], sem)
    copy.start()
    for half in range(2):
        for part in range(4):
            first = 16 * half + 4 * part
            rows = [tiles[first + n, :6, :].astype(F32) for n in range(4)]
            out[pl.ds(288 + 24 * part, 24), pl.ds(384 * half, 384)] = jnp.concatenate(rows, axis=0).astype(BF16)
    copy.wait()


def pack(block, tiles):
    return pl.pallas_call(
        pack_kernel,
        out_shape=jax.ShapeDtypeStruct((384, 768), BF16),
        in_specs=[ANY, VMEM],
        out_specs=VMEM,
        scratch_shapes=[pltpu.SemaphoreType.DMA],
        cost_estimate=pl.CostEstimate(flops=10**6, bytes_accessed=2 * 10**6, transcendentals=0),
    )(block, tiles)


def filter_kernel(core, scale, member, field, mine, other, out, lon, lat, mid, lon_sems, lat_sems):
    lon_copies, lat_copies = [], []
    sides = ((mine, core[0]), (other, 1 - core[0]))
    for m, (part, half) in enumerate(sides):
        for s in range(3):
            for h in range(2):
                to = pl.ds(pl.multiple_of(half * 192 + 96 * h, 32), 96)
                copy = pltpu.make_async_copy(
                    part.at[s, pl.ds(288, 96), pl.ds(384 * h, 384)], lat.at[s, to, :], lat_sems.at[m, s, h]
                )
                copy.start()
                lat_copies.append(copy)
    for s in range(3):
        for m, (part, half) in enumerate(sides):
            for x in range(4):
                to = pl.ds(pl.multiple_of((2 * x + half) * 96, 32), 96)
                copy = pltpu.make_async_copy(
                    part.at[x, pl.ds(96 * s, 96), :], lon.at[s, to, :], lon_sems.at[m, s, x]
                )
                copy.start()
                lon_copies.append(copy)
    for copy in lat_copies:
        copy.wait()
    for s in range(3):
        across = jnp.dot(lat[s], field[...], preferred_element_type=F32)
        mid[s] = (scale[s] * member[0] * across).astype(BF16)
    for copy in lon_copies:
        copy.wait()
    total = jnp.zeros(out.shape, F32)
    for s in range(3):
        total += lax.dot_general(
            mid[s], lon[s], (((1,), (1,)), ((), ())), preferred_element_type=F32
        )
    out[...] = total.astype(BF16)


def filter_pair(core, scale, member, field, mine, other):
    return pl.pallas_call(
        filter_kernel,
        out_shape=jax.ShapeDtypeStruct((384, 768), BF16),
        in_specs=[SMEM, SMEM, SMEM, VMEM, HBM, HBM],
        out_specs=VMEM,
        scratch_shapes=[
            pltpu.VMEM((3, 768, 768), BF16),
            pltpu.VMEM((3, 384, 384), BF16),
            pltpu.VMEM((3, 384, 768), BF16),
            pltpu.SemaphoreType.DMA((2, 3, 4)),
            pltpu.SemaphoreType.DMA((2, 3, 2)),
        ],
        compiler_params=pltpu.CompilerParams(vmem_limit_bytes=62 * 2**20),
        cost_estimate=pl.CostEstimate(flops=2 * 10**9, bytes_accessed=5 * 10**6, transcendentals=0),
    )(core, scale, member, field, mine, other)


def final_kernel(own, back, out):
    for r in range(6):
        total = jnp.zeros((8, 768), F32)
        for k in range(8):
            parts = [
                back[l % 2, k // 2, 4 * (k % 2) + l // 2, r, :].astype(F32).reshape(1, 768)
                for l in range(8)
            ]
            total += own[k, r].astype(F32) * jnp.concatenate(parts, axis=0)
        out[r] = total


def final_sum(own, back):
    return pl.pallas_call(
        final_kernel,
        out_shape=jax.ShapeDtypeStruct((6, 8, 768), F32),
        in_specs=[VMEM, VMEM],
        out_specs=VMEM,
        cost_estimate=pl.CostEstimate(flops=10**6, bytes_accessed=2 * 10**6, transcendentals=0),
    )(own, back)


def on_device(perturbations, gradient, member_weights, scale_weights, lon_filter, lat_filter):
    core = lax.axis_index("c")
    own = perturbations[0].transpose(1, 0, 2).reshape(6, 8, 8, 768).transpose(1, 0, 2, 3)
    own = lax.all_to_all(own, MEM, split_axis=0, concat_axis=0, tiled=True)
    block = lax.ppermute(lon_filter, ("zh", "c"), [(0, 0), (1, 2), (2, 1), (3, 3)])
    rows = lax.dynamic_index_in_dim(lat_filter, jnp.minimum(lax.axis_index("x"), 2), 0, False)
    tiles = jnp.broadcast_to(jnp.pad(rows, ((0, 2), (0, 0)))[None], (32, 8, 384))
    tiles = lax.all_to_all(tiles, ("zl", "y"), split_axis=0, concat_axis=0, tiled=True)
    packed = pack(block.reshape(288, 768), tiles)
    mine = lax.all_gather(packed, "x", axis=0)
    turn = [((c // 8) * 64 + m * 8 + c % 8, m * 64 + c) for m in range(8) for c in range(64)]
    weight = lax.ppermute(member_weights, MEM + COL, turn)
    own, weight = lax.optimization_barrier((own, weight))

    member = lax.axis_index(MEM)
    level = lax.dynamic_slice_in_dim(gradient.transpose(1, 0, 2), member * 8, 8, axis=1)
    schur = (own.astype(F32) * level[None]).astype(BF16)
    schur = schur.transpose(0, 2, 1, 3).reshape(64, 2, 2304)
    field = lax.all_to_all(schur, COL, split_axis=0, concat_axis=0, tiled=True).reshape(384, 768)
    mine = lax.optimization_barrier((mine, field))[0]
    other = lax.ppermute(mine, "c", SWAP)
    core = core.reshape(1).astype(jnp.int32)
    filtered = filter_pair(core, scale_weights, weight, field, mine, other).reshape(64, 2, 2304)
    back = lax.all_to_all(filtered, ("c", "zl", "y"), split_axis=0, concat_axis=0, tiled=True)
    return final_sum(own, back.reshape(2, 4, 8, 6, 768)).transpose(1, 0, 2)


def solution(mesh):
    fine = Mesh(mesh.devices.reshape(4, 2, 4, 8, 2), MEM + COL)
    placed = (
        P(MEM, None, COL, None),
        P(None, COL, None),
        P(MEM),
        P(),
        P(None, MEM, None),
        P(None, COL, None),
    )
    return jax.shard_map(
        on_device, mesh=fine, in_specs=placed, out_specs=P(MEM, COL, None), check_vma=False
    )
```

time: 162 us -> 152 us (0.938)
  blocking collectives: 40.3 us -> 79.6 us
  waiting for transfers between devices: 45.4 us -> 15 us
  starting transfers between devices: 40.4 us -> 20.6 us
    all_to_all x2 -> x3, blocking collectives: 40.3 us -> 79.6 us  [the longest x1 35.3 us: on_device(): lax.all_to_all(schur, COL, split_axis=0, concat_axis=0, tiled=True)]
    all_to_all x1 -> x0, waiting for transfers between devices: 17.2 us -> none  [on_device(): lax.all_to_all(schur, COL, split_axis=0, concat_axis=0, tiled=True)]
    all_gather x1, waiting for transfers between devices: 16.2 us -> 0.01 us  [on_device(): mine = lax.all_gather(packed, 'x', axis=0)]
    all_to_all x1, starting transfers between devices: 14.4 us -> 4.02 us  [on_device(): own = lax.all_to_all(own, MEM, split_axis=0, concat_axis=0, tiled=True)]
    all_to_all x1 -> x0, starting transfers between devices: 8.74 us -> none  [on_device(): lax.all_to_all(schur, COL, split_axis=0, concat_axis=0, tiled=True)]
    ppermute x1, waiting for transfers between devices: 0.01 us -> 4.48 us  [on_device(): other = lax.ppermute(mine, 'c', SWAP)]
    reshape x1, local copies, waits for them, and re-layouts: 0.32 us -> 1.95 us  [on_device(): filter_pair(core, scale_weights, weight, field, mine, other)]
  transfers between devices with their start and end apart: 7 -> 5, of which waited for: 3 -> 2; matrix products, arithmetic and copies ran while one was open for 2% -> 2% of each run, Pallas kernels for 0% -> 0%
where the time goes in v4:
time: 152 us; the launch traced here: 151 us
  blocking collectives  79.6 us (52%)
  starting transfers between devices  20.6 us (14%)
  waiting for transfers between devices  15 us (10%)
  Pallas kernels  14.5 us (10%)
  between operations  13.5 us (9%)
  local copies, waits for them, and re-layouts  7.94 us (5%)
    all_to_all x1, blocking collectives, on_device(): lax.all_to_all(schur, COL, split_axis=0, concat_axis=0, tiled=True)  35.3 us
    all_to_all x1, blocking collectives, on_device(): lax.all_to_all(filtered, ('c', 'zl', 'y'), split_axis=0, concat_axis=0, t...  24.8 us
    all_to_all x1, blocking collectives, on_device(): lax.all_to_all(tiles, ('zl', 'y'), split_axis=0, concat_axis=0, tiled=True)  19.5 us
    ppermute x1, starting transfers between devices, on_device(): lax.ppermute(lon_filter, ('zh', 'c'), [(0, 0), (1, 2), (2, 1), (3, 3)])  12.1 us
    all_to_all x1, waiting for transfers between devices, on_device(): own = lax.all_to_all(own, MEM, split_axis=0, concat_axis=0, tiled=True)  10.5 us
    pallas_call x1, Pallas kernels, filter_pair(): pl.pallas_call(filter_kernel, out_shape=jax.ShapeDtypeStruct((384, 768),...  8.76 us
    ppermute x1, waiting for transfers between devices, on_device(): other = lax.ppermute(mine, 'c', SWAP)  4.48 us
    all_to_all x1, starting transfers between devices, on_device(): own = lax.all_to_all(own, MEM, split_axis=0, concat_axis=0, tiled=True)  4.02 us
  transfers between devices with their start and end apart: 5, of which 2 were waited for; matrix products, arithmetic and copies ran while one was open for 2% of the time, Pallas kernels for 0%

profile of v4, /device:TPU:1, one launch (start us, length us, event | category | flops | bytes accessed | tf_op | source)
XLA Modules:
  0.0 151.2 jit_solution(395855886104232671)
XLA Ops:
  6.5 12.1 %collective-permute-start.1 = (bf16[3,96,768]{2,1,0:T(8,128)(2,1)}, bf16[3,96,768]{2,1,0:T(8,128)(2,1)S(1)}, u32[]{:S(2)}, u32[]{:S(2)}) collective-permute-start(bf16[3,96,768]{2,1,0:T(8,128)(2,1)} %param.10), channel_id=1, source_target_pairs={{0,0},{1,64},{64,1},{65,65},{2,2},{3,66},{66,3},{67,67},{4,4},{5,6... | collective-permute-start | bytes 1327112 | tf_op jit(solution)/shard_map/ppermute | solution.py:122
  18.7 0.7 dynamic-slice_bitcast_fusion.1
  19.4 19.5 %all_to_all.20.tiles = bf16[32,8,384]{2,1,0:T(8,128)(2,1)} all-to-all(bf16[32,8,384]{2,1,0:T(8,128)(2,1)S(1)} %broadcast_in_dim.2), channel_id=1, replica_groups=mesh['x'=4,'zh'=2,'zl'=4,'y'=8,'c'=2] {'zl','y'}, dimensions={0} | all-to-all | bytes 393216 | tf_op jit(solution)/shard_map/all_to_all | solution.py:125
  39.0 0.8 copy-done.3
  39.7 2.8 %shard_map.64 = bf16[384,768]{1,0:T(8,128)(2,1)} custom-call(bf16[288,768]{1,0:T(8,128)(2,1)} %bitcast.19, bf16[32,8,384]{2,1,0:T(8,128)(2,1)} %all_to_all.20.tiles), custom_call_target="tpu_custom_call" | custom-call | flops 1000000 | bytes 2000000 | tf_op jit(solution)/shard_map/pallas_call | solution.py:32
  42.5 0.0 all-gather.3.cloned.1.call-update
  42.5 0.8 copy_bitcast_fusion
  43.4 4.0 %all-to-all-start = ((bf16[8,6,8,768]{3,2,1,0:T(8,128)(2,1)}), bf16[8,6,8,768]{3,2,1,0:T(8,128)(2,1)S(1)}, u32[]{:S(2)}, u32[]{:S(2)}) async-start(bf16[8,6,8,768]{3,2,1,0:T(8,128)(2,1)} %copy_bitcast_fusion), calls=%async_computation | async-start | bytes 1179648 | tf_op jit(solution)/shard_map/all_to_all | solution.py:121
  47.4 1.9 %collective-permute-start = (f32[1]{0:T(128)}, f32[1]{0:T(128)}, u32[]{:S(2)}, u32[]{:S(2)}) collective-permute-start(f32[1]{0:T(128)} %param.8), channel_id=1, source_target_pairs={{0,0},{1,1},{2,2},{3,3},{4,4},{5,5},{6,6},{7,7},{64,8},{65,9},{66,... | collective-permute-start | bytes 20 | tf_op jit(solution)/shard_map/ppermute | solution.py:129
  49.3 0.0 collective-permute-done.member
  49.3 10.5 %all-to-all-done.own = bf16[8,6,8,768]{3,2,1,0:T(8,128)(2,1)S(1)} async-done(((bf16[8,6,8,768]{3,2,1,0:T(8,128)(2,1)}), bf16[8,6,8,768]{3,2,1,0:T(8,128)(2,1)S(1)}, u32[]{:S(2)}, u32[]{:S(2)}) %all-to-all-start) | async-done | bytes 589856 | tf_op jit(solution)/shard_map/all_to_all | solution.py:121
  59.9 0.1 fusion
  60.0 0.1 copy.8
  60.1 0.6 copy-done.1
  60.7 0.4 reshape.25
  61.1 35.3 %all_to_all.21 = bf16[64,2,2304]{2,1,0:T(2,128)(2,1)S(1)} all-to-all(bf16[64,2,2304]{2,1,0:T(2,128)(2,1)S(1)} %reshape.25), channel_id=1, replica_groups=mesh['x'=4,'zh'=2,'zl'=4,'y'=8,'c'=2] {'zl','y','c'}, dimensions={0} | all-to-all | bytes 1179648 | tf_op jit(solution)/shard_map/all_to_all | solution.py:136
  96.4 1.2 reshape.26.field
  97.7 2.5 %collective-permute-start.2 = (bf16[4,384,768]{2,1,0:T(8,128)(2,1)}, bf16[4,384,768]{2,1,0:T(8,128)(2,1)}, u32[]{:S(2)}, u32[]{:S(2)}) collective-permute-start(bf16[4,384,768]{2,1,0:T(8,128)(2,1)} %bitcast.20), channel_id=1, source_target_pairs={{0,1},{1,0},{2,3},{3,2},{4,5},{5,4},{6,7},{7,6},{8,9},{9,8},{10,11... | collective-permute-start | bytes 7077896 | tf_op jit(solution)/shard_map/ppermute | solution.py:138
  100.2 4.5 %collective-permute-done.2.other = bf16[4,384,768]{2,1,0:T(8,128)(2,1)} collective-permute-done((bf16[4,384,768]{2,1,0:T(8,128)(2,1)}, bf16[4,384,768]{2,1,0:T(8,128)(2,1)}, u32[]{:S(2)}, u32[]{:S(2)}) %collective-permute-start.2) | collective-permute-done | bytes 2359328 | tf_op jit(solution)/shard_map/ppermute | solution.py:138
  104.7 8.8 %shard_map.65 = bf16[384,768]{1,0:T(8,128)(2,1)} custom-call(s32[1]{0:T(128)} %bitcast.4.core, f32[3]{0:T(128)} %scale.1, f32[1]{0:T(128)} %collective-permute-done.member, bf16[384,768]{1,0:T(8,128)(2,1)} %reshape.26.field, bf16[4,384,768]{2,1,0:T(8,128)(2,1)} %bitcast.21, bf16[4,384,768]{2,1,0:T(8,128)(2,1)} %collective-permute-done.2.other), custom_call_target="tpu_custom_call" | custom-call | flops 2000000000 | bytes 5000000 | tf_op jit(solution)/shard_map/pallas_call | solution.py:79
  113.4 2.0 %reshape.28 = bf16[64,2,2304]{2,1,0:T(2,128)(2,1)S(1)} reshape(bf16[384,768]{1,0:T(8,128)(2,1)} %shard_map.65) | data formatting | bytes 1179648 | tf_op jit(solution)/shard_map/reshape | solution.py:140
  115.4 24.8 %all_to_all.22 = bf16[64,2,2304]{2,1,0:T(2,128)(2,1)S(1)} all-to-all(bf16[64,2,2304]{2,1,0:T(2,128)(2,1)S(1)} %reshape.28), channel_id=1, replica_groups=mesh['x'=4,'zh'=2,'zl'=4,'y'=8,'c'=2] {'c','zl','y'}, dimensions={0} | all-to-all | bytes 1179648 | tf_op jit(solution)/shard_map/all_to_all | solution.py:141
  140.2 1.3 reshape.29.back
  141.5 2.9 %shard_map.66 = f32[6,8,768]{2,1,0:T(8,128)} custom-call(bf16[8,6,8,768]{3,2,1,0:T(8,128)(2,1)} %copy-done.1, bf16[2,4,8,6,768]{4,3,2,1,0:T(8,128)(2,1)} %reshape.29.back), custom_call_target="tpu_custom_call" | custom-call | flops 1000000 | bytes 2000000 | tf_op jit(solution)/shard_map/pallas_call | solution.py:109
  (12 shorter events, 0.1 us)
Async XLA Ops:
  6.5 42.8 %copy-start = (f32[64,6,768]{2,0,1:T(8,128)S(1)}, f32[64,6,768]{2,0,1:T(8,128)}, u32[]{:S(2)}) copy-start(f32[64,6,768]{2,0,1:T(8,128)} %param.7) | copy-start | bytes 3538948
  6.5 91.1 %all-gather.3.cloned.1.call-start = ((), (), s32[]{:S(2)}) async-start(), calls=%async_computation.4 | async-start | bytes 2949120 | tf_op jit(solution)/shard_map/all_gather | solution.py:127
  6.5 32.4 %collective-permute-start.1 = (bf16[3,96,768]{2,1,0:T(8,128)(2,1)}, bf16[3,96,768]{2,1,0:T(8,128)(2,1)S(1)}, u32[]{:S(2)}, u32[]{:S(2)}) collective-permute-start(bf16[3,96,768]{2,1,0:T(8,128)(2,1)} %param.10), channel_id=1, source_target_pairs={{0,0},{1,64},{64,1},{65,65},{2,2},{3,66},{66,3},{67,67},{4,4},{5,6... | collective-permute-start | bytes 1327112 | tf_op jit(solution)/shard_map/ppermute | solution.py:122
  19.4 23.1 %copy-start.2 = (bf16[1,64,6,768]{3,1,2,0:T(8,128)(2,1)S(1)}, bf16[1,64,6,768]{3,1,2,0:T(8,128)(2,1)}, u32[]{:S(2)}) copy-start(bf16[1,64,6,768]{3,1,2,0:T(8,128)(2,1)} %param.6) | copy-start | bytes 1769476
  39.0 0.8 copy-start.3
  43.4 16.5 %all-to-all-start = ((bf16[8,6,8,768]{3,2,1,0:T(8,128)(2,1)}), bf16[8,6,8,768]{3,2,1,0:T(8,128)(2,1)S(1)}, u32[]{:S(2)}, u32[]{:S(2)}) async-start(bf16[8,6,8,768]{3,2,1,0:T(8,128)(2,1)} %copy_bitcast_fusion), calls=%async_computation | async-start | bytes 1179648 | tf_op jit(solution)/shard_map/all_to_all | solution.py:121
  47.4 1.9 %collective-permute-start = (f32[1]{0:T(128)}, f32[1]{0:T(128)}, u32[]{:S(2)}, u32[]{:S(2)}) collective-permute-start(f32[1]{0:T(128)} %param.8), channel_id=1, source_target_pairs={{0,0},{1,1},{2,2},{3,3},{4,4},{5,5},{6,6},{7,7},{64,8},{65,9},{66,... | collective-permute-start | bytes 20 | tf_op jit(solution)/shard_map/ppermute | solution.py:129
  59.9 0.8 copy-start.1
  97.7 7.0 %collective-permute-start.2 = (bf16[4,384,768]{2,1,0:T(8,128)(2,1)}, bf16[4,384,768]{2,1,0:T(8,128)(2,1)}, u32[]{:S(2)}, u32[]{:S(2)}) collective-permute-start(bf16[4,384,768]{2,1,0:T(8,128)(2,1)} %bitcast.20), channel_id=1, source_target_pairs={{0,1},{1,0},{2,3},{3,2},{4,5},{5,4},{6,7},{7,6},{8,9},{9,8},{10,11... | collective-permute-start | bytes 7077896 | tf_op jit(solution)/shard_map/ppermute | solution.py:138
Sparse Core Ops, SparseCore 0:
  42.7 37.2 all-gather.2

commit v5 on v4

--- a/solution.py
+++ b/solution.py
@@ -17,37 +17,35 @@
 HBM = pl.BlockSpec(memory_space=pltpu.MemorySpace.HBM)
 
 
-def pack_kernel(block, tiles, out, sem):
-    copy = pltpu.make_async_copy(block, out.at[pl.ds(0, 288)], sem)
-    copy.start()
+def pack_kernel(block, tiles, out):
+    out[pl.ds(0, 288), :] = block[...]
     for half in range(2):
         for part in range(4):
             first = 16 * half + 4 * part
             rows = [tiles[first + n, :6, :].astype(F32) for n in range(4)]
             out[pl.ds(288 + 24 * part, 24), pl.ds(384 * half, 384)] = jnp.concatenate(rows, axis=0).astype(BF16)
-    copy.wait()
 
 
 def pack(block, tiles):
     return pl.pallas_call(
         pack_kernel,
         out_shape=jax.ShapeDtypeStruct((384, 768), BF16),
-        in_specs=[ANY, VMEM],
+        in_specs=[VMEM, VMEM],
         out_specs=VMEM,
-        scratch_shapes=[pltpu.SemaphoreType.DMA],
         cost_estimate=pl.CostEstimate(flops=10**6, bytes_accessed=2 * 10**6, transcendentals=0),
     )(block, tiles)
 
 
-def filter_kernel(core, scale, member, field, mine, other, out, lon, lat, mid, lon_sems, lat_sems):
+def filter_kernel(core, scale, member, field, mine, *rest):
+    others, (out, lon, lat, mid, lon_sems, lat_sems) = rest[:4], rest[4:]
     lon_copies, lat_copies = [], []
-    sides = ((mine, core[0]), (other, 1 - core[0]))
+    sides = (([mine.at[x] for x in range(4)], core[0]), (others, 1 - core[0]))
     for m, (part, half) in enumerate(sides):
         for s in range(3):
             for h in range(2):
                 to = pl.ds(pl.multiple_of(half * 192 + 96 * h, 32), 96)
                 copy = pltpu.make_async_copy(
-                    part.at[s, pl.ds(288, 96), pl.ds(384 * h, 384)], lat.at[s, to, :], lat_sems.at[m, s, h]
+                    part[s].at[pl.ds(288, 96), pl.ds(384 * h, 384)], lat.at[s, to, :], lat_sems.at[m, s, h]
                 )
                 copy.start()
                 lat_copies.append(copy)
@@ -56,7 +54,7 @@
             for x in range(4):
                 to = pl.ds(pl.multiple_of((2 * x + half) * 96, 32), 96)
                 copy = pltpu.make_async_copy(
-                    part.at[x, pl.ds(96 * s, 96), :], lon.at[s, to, :], lon_sems.at[m, s, x]
+                    part[x].at[pl.ds(96 * s, 96), :], lon.at[s, to, :], lon_sems.at[m, s, x]
                 )
                 copy.start()
                 lon_copies.append(copy)
@@ -75,11 +73,11 @@
     out[...] = total.astype(BF16)
 
 
-def filter_pair(core, scale, member, field, mine, other):
+def filter_pair(core, scale, member, field, mine, others):
     return pl.pallas_call(
         filter_kernel,
         out_shape=jax.ShapeDtypeStruct((384, 768), BF16),
-        in_specs=[SMEM, SMEM, SMEM, VMEM, HBM, HBM],
+        in_specs=[SMEM, SMEM, SMEM, VMEM] + [HBM] * 5,
         out_specs=VMEM,
         scratch_shapes=[
             pltpu.VMEM((3, 768, 768), BF16),
@@ -88,9 +86,9 @@
             pltpu.SemaphoreType.DMA((2, 3, 4)),
             pltpu.SemaphoreType.DMA((2, 3, 2)),
         ],
-        compiler_params=pltpu.CompilerParams(vmem_limit_bytes=62 * 2**20),
+        compiler_params=pltpu.CompilerParams(vmem_limit_bytes=20 * 2**20),
         cost_estimate=pl.CostEstimate(flops=2 * 10**9, bytes_accessed=5 * 10**6, transcendentals=0),
-    )(core, scale, member, field, mine, other)
+    )(core, scale, member, field, mine, *others)
 
 
 def final_kernel(own, back, out):
@@ -123,21 +121,20 @@
     rows = lax.dynamic_index_in_dim(lat_filter, jnp.minimum(lax.axis_index("x"), 2), 0, False)
     tiles = jnp.broadcast_to(jnp.pad(rows, ((0, 2), (0, 0)))[None], (32, 8, 384))
     tiles = lax.all_to_all(tiles, ("zl", "y"), split_axis=0, concat_axis=0, tiled=True)
+    turn = [((c // 8) * 64 + m * 8 + c % 8, m * 64 + c) for m in range(8) for c in range(64)]
+    weight = lax.ppermute(member_weights, MEM + COL, turn)
+    block, weight = lax.optimization_barrier((block, weight))
     packed = pack(block.reshape(288, 768), tiles)
     mine = lax.all_gather(packed, "x", axis=0)
-    turn = [((c // 8) * 64 + m * 8 + c % 8, m * 64 + c) for m in range(8) for c in range(64)]
-    weight = lax.ppermute(member_weights, MEM + COL, turn)
-    own, weight = lax.optimization_barrier((own, weight))
-
     member = lax.axis_index(MEM)
     level = lax.dynamic_slice_in_dim(gradient.transpose(1, 0, 2), member * 8, 8, axis=1)
     schur = (own.astype(F32) * level[None]).astype(BF16)
     schur = schur.transpose(0, 2, 1, 3).reshape(64, 2, 2304)
     field = lax.all_to_all(schur, COL, split_axis=0, concat_axis=0, tiled=True).reshape(384, 768)
-    mine = lax.optimization_barrier((mine, field))[0]
-    other = lax.ppermute(mine, "c", SWAP)
+    mine = lax.optimization_barrier((mine, schur))[0]
+    others = [lax.ppermute(mine[n], "c", SWAP) for n in range(4)]
     core = core.reshape(1).astype(jnp.int32)
-    filtered = filter_pair(core, scale_weights, weight, field, mine, other).reshape(64, 2, 2304)
+    filtered = filter_pair(core, scale_weights, weight, field, mine, others).reshape(64, 2, 2304)
     back = lax.all_to_all(filtered, ("c", "zl", "y"), split_axis=0, concat_axis=0, tiled=True)
     return final_sum(own, back.reshape(2, 4, 8, 6, 768)).transpose(1, 0, 2)
 

time: 152 us -> 153 us (level)
  blocking collectives: 79.6 us -> 27.2 us
  starting transfers between devices: 20.6 us -> 56.6 us
  waiting for transfers between devices: 15 us -> 26.5 us
  local copies, waits for them, and re-layouts: 7.94 us -> 16.1 us
  Pallas kernels: 14.5 us -> 12.3 us
    all_to_all x2 -> x0, blocking collectives: 54.8 us -> none  [the longest x1 35.3 us: on_device(): lax.all_to_all(schur, COL, split_axis=0, concat_axis=0, tiled=True)]
    all_to_all x0 -> x2, starting transfers between devices: none -> 26 us  [the longest x1 16.1 us: on_device(): lax.all_to_all(schur, COL, split_axis=0, concat_axis=0, tiled=True)]
    all_to_all x0 -> x2, waiting for transfers between devices: none -> 11.3 us  [the longest x1 7.65 us: on_device(): lax.all_to_all(tiles, ('zl', 'y'), split_axis=0, concat_axis=0, tiled=True)]
    ppermute x1 -> x4, starting transfers between devices: 2.53 us -> 8.95 us  [on_device(): others = [lax.ppermute(mine[n], 'c', SWAP) for n in range(4)]]
    ppermute x1 -> x4, waiting for transfers between devices: 4.48 us -> 0.01 us  [on_device(): others = [lax.ppermute(mine[n], 'c', SWAP) for n in range(4)]]
    all_to_all x1, starting transfers between devices: 4.02 us -> 7.64 us  [on_device(): own = lax.all_to_all(own, MEM, split_axis=0, concat_axis=0, tiled=True)]
    squeeze x0 -> x1, local copies, waits for them, and re-layouts: none -> 3.25 us  [on_device(): others = [lax.ppermute(mine[n], 'c', SWAP) for n in range(4)]]
    all_gather x1, waiting for transfers between devices: 0.01 us -> 3.02 us  [on_device(): mine = lax.all_gather(packed, 'x', axis=0)]
  transfers between devices with their start and end apart: 5 -> 10, of which waited for: 2 -> 4; matrix products, arithmetic and copies ran while one was open for 2% -> 6% of each run, Pallas kernels for 0% -> 0%
where the time goes in v5:
time: 153 us; the launch traced here: 152 us
  starting transfers between devices  56.6 us (37%)
  blocking collectives  27.2 us (18%)
  waiting for transfers between devices  26.5 us (17%)
  local copies, waits for them, and re-layouts  16.1 us (11%)
  between operations  13.6 us (9%)
  Pallas kernels  12.3 us (8%)
    all_to_all x1, blocking collectives, on_device(): lax.all_to_all(filtered, ('c', 'zl', 'y'), split_axis=0, concat_axis=0, t...  27.2 us
    all_to_all x1, starting transfers between devices, on_device(): lax.all_to_all(schur, COL, split_axis=0, concat_axis=0, tiled=True)  16.1 us
    ppermute x1, starting transfers between devices, on_device(): lax.ppermute(lon_filter, ('zh', 'c'), [(0, 0), (1, 2), (2, 1), (3, 3)])  12.1 us
    all_to_all x1, waiting for transfers between devices, on_device(): own = lax.all_to_all(own, MEM, split_axis=0, concat_axis=0, tiled=True)  12.1 us
    all_to_all x1, starting transfers between devices, on_device(): lax.all_to_all(tiles, ('zl', 'y'), split_axis=0, concat_axis=0, tiled=True)  9.94 us
    ppermute x4, starting transfers between devices, on_device(): others = [lax.ppermute(mine[n], 'c', SWAP) for n in range(4)]  8.95 us
    all_to_all x1, waiting for transfers between devices, on_device(): lax.all_to_all(tiles, ('zl', 'y'), split_axis=0, concat_axis=0, tiled=True)  7.65 us
    all_to_all x1, starting transfers between devices, on_device(): own = lax.all_to_all(own, MEM, split_axis=0, concat_axis=0, tiled=True)  7.64 us
  transfers between devices with their start and end apart: 10, of which 4 were waited for; matrix products, arithmetic and copies ran while one was open for 6% of the time, Pallas kernels for 0%

profile of v5, /device:TPU:1, one launch (start us, length us, event | category | flops | bytes accessed | tf_op | source)
XLA Modules:
  0.0 152.5 jit_solution(4248491472262305851)
XLA Ops:
  6.5 12.1 %collective-permute-start = (bf16[3,96,768]{2,1,0:T(8,128)(2,1)}, bf16[3,96,768]{2,1,0:T(8,128)(2,1)S(1)}, u32[]{:S(2)}, u32[]{:S(2)}) collective-permute-start(bf16[3,96,768]{2,1,0:T(8,128)(2,1)} %param.10), channel_id=1, source_target_pairs={{0,0},{1,64},{64,1},{65,65},{2,2},{3,66},{66,3},{67,67},{4,4},{5,6... | collective-permute-start | bytes 1327112 | tf_op jit(solution)/shard_map/ppermute | solution.py:120
  20.1 9.9 %all-to-all-start.2 = ((bf16[32,8,384]{2,1,0:T(8,128)(2,1)}), bf16[32,8,384]{2,1,0:T(8,128)(2,1)S(1)}, u32[]{:S(2)}, u32[]{:S(2)}) async-start(bf16[32,8,384]{2,1,0:T(8,128)(2,1)} %broadcast_in_dim.2), calls=%async_computation.2 | async-start | bytes 393216 | tf_op jit(solution)/shard_map/all_to_all | solution.py:123
  30.1 1.8 %collective-permute-start.1 = (f32[1]{0:T(128)}, f32[1]{0:T(128)}, u32[]{:S(2)}, u32[]{:S(2)}) collective-permute-start(f32[1]{0:T(128)} %param.8), channel_id=1, source_target_pairs={{0,0},{1,1},{2,2},{3,3},{4,4},{5,5},{6,6},{7,7},{64,8},{65,9},{66,... | collective-permute-start | bytes 20 | tf_op jit(solution)/shard_map/ppermute | solution.py:125
  31.9 7.6 %all-to-all-done.2.tiles = bf16[32,8,384]{2,1,0:T(8,128)(2,1)S(1)} async-done(((bf16[32,8,384]{2,1,0:T(8,128)(2,1)}), bf16[32,8,384]{2,1,0:T(8,128)(2,1)S(1)}, u32[]{:S(2)}, u32[]{:S(2)}) %all-to-all-start.2) | async-done | bytes 196640 | tf_op jit(solution)/shard_map/all_to_all | solution.py:123
  40.3 1.9 %shard_map.64 = bf16[384,768]{1,0:T(8,128)(2,1)} custom-call(bf16[288,768]{1,0:T(8,128)(2,1)} %bitcast.29, bf16[32,8,384]{2,1,0:T(8,128)(2,1)} %copy-done.6), custom_call_target="tpu_custom_call" | custom-call | flops 1000000 | bytes 2000000 | tf_op jit(solution)/shard_map/pallas_call | solution.py:30
  42.3 0.9 copy_bitcast_fusion
  43.1 7.6 %all-to-all-start = ((bf16[8,6,8,768]{3,2,1,0:T(8,128)(2,1)}), bf16[8,6,8,768]{3,2,1,0:T(8,128)(2,1)S(1)}, u32[]{:S(2)}, u32[]{:S(2)}) async-start(bf16[8,6,8,768]{3,2,1,0:T(8,128)(2,1)} %copy_bitcast_fusion), calls=%async_computation | async-start | bytes 1179648 | tf_op jit(solution)/shard_map/all_to_all | solution.py:119
  50.8 12.1 %all-to-all-done.own = bf16[8,6,8,768]{3,2,1,0:T(8,128)(2,1)S(1)} async-done(((bf16[8,6,8,768]{3,2,1,0:T(8,128)(2,1)}), bf16[8,6,8,768]{3,2,1,0:T(8,128)(2,1)S(1)}, u32[]{:S(2)}, u32[]{:S(2)}) %all-to-all-start) | async-done | bytes 589856 | tf_op jit(solution)/shard_map/all_to_all | solution.py:119
  63.8 1.2 reshape.25
  65.0 16.1 %all-to-all-start.1 = ((bf16[64,2,2304]{2,1,0:T(2,128)(2,1)}), bf16[64,2,2304]{2,1,0:T(2,128)(2,1)}, u32[]{:S(2)}, u32[]{:S(2)}) async-start(bf16[64,2,2304]{2,1,0:T(2,128)(2,1)} %reshape.25), calls=%async_computation.1 | async-start | bytes 1179648 | tf_op jit(solution)/shard_map/all_to_all | solution.py:133
  81.1 3.0 %all-gather.3.cloned.1.call-done = bf16[1536,768]{1,0:T(8,128)(2,1)} async-done(((bf16[384,768]{1,0:T(8,128)(2,1)}), bf16[1536,768]{1,0:T(8,128)(2,1)}) %all-gather.3.cloned.1.call-update) | async-done | bytes 2359312 | tf_op jit(solution)/shard_map/all_gather | solution.py:128
  84.1 3.3 %slice_bitcast_fusion = (bf16[384,768]{1,0:T(8,128)(2,1)}, bf16[384,768]{1,0:T(8,128)(2,1)}, bf16[384,768]{1,0:T(8,128)(2,1)}, bf16[384,768]{1,0:T(8,128)(2,1)}) fusion(bf16[4,384,768]{2,1,0:T(8,128)(2,1)} %bitcast.27), kind=kLoop, calls=%fused_computation.3 | loop fusion | bytes 4718592 | tf_op jit(solution)/shard_map/squeeze | solution.py:135
  87.4 2.7 %collective-permute-start.5 = (bf16[384,768]{1,0:T(8,128)(2,1)}, bf16[384,768]{1,0:T(8,128)(2,1)}, u32[]{:S(2)}, u32[]{:S(2)}) collective-permute-start(bf16[384,768]{1,0:T(8,128)(2,1)} %get-tuple-element.11), channel_id=1, source_target_pairs={{0,1},{1,0},{2,3},{3,2},{4,5},{5,4},{6,7},{7,6},{8,9},{9,8},{10,11... | collective-permute-start | bytes 1769480 | tf_op jit(solution)/shard_map/ppermute | solution.py:135
  90.1 1.9 %collective-permute-start.4 = (bf16[384,768]{1,0:T(8,128)(2,1)}, bf16[384,768]{1,0:T(8,128)(2,1)}, u32[]{:S(2)}, u32[]{:S(2)}) collective-permute-start(bf16[384,768]{1,0:T(8,128)(2,1)} %get-tuple-element.12), channel_id=1, source_target_pairs={{0,1},{1,0},{2,3},{3,2},{4,5},{5,4},{6,7},{7,6},{8,9},{9,8},{10,11... | collective-permute-start | bytes 1769480 | tf_op jit(solution)/shard_map/ppermute | solution.py:135
  92.0 2.4 %collective-permute-start.3 = (bf16[384,768]{1,0:T(8,128)(2,1)}, bf16[384,768]{1,0:T(8,128)(2,1)}, u32[]{:S(2)}, u32[]{:S(2)}) collective-permute-start(bf16[384,768]{1,0:T(8,128)(2,1)} %get-tuple-element.13), channel_id=1, source_target_pairs={{0,1},{1,0},{2,3},{3,2},{4,5},{5,4},{6,7},{7,6},{8,9},{9,8},{10,11... | collective-permute-start | bytes 1769480 | tf_op jit(solution)/shard_map/ppermute | solution.py:135
  94.4 1.9 %collective-permute-start.2 = (bf16[384,768]{1,0:T(8,128)(2,1)}, bf16[384,768]{1,0:T(8,128)(2,1)}, u32[]{:S(2)}, u32[]{:S(2)}) collective-permute-start(bf16[384,768]{1,0:T(8,128)(2,1)} %get-tuple-element.14), channel_id=1, source_target_pairs={{0,1},{1,0},{2,3},{3,2},{4,5},{5,4},{6,7},{7,6},{8,9},{9,8},{10,11... | collective-permute-start | bytes 1769480 | tf_op jit(solution)/shard_map/ppermute | solution.py:135
  96.4 3.7 %all-to-all-done.1 = bf16[64,2,2304]{2,1,0:T(2,128)(2,1)} async-done(((bf16[64,2,2304]{2,1,0:T(2,128)(2,1)}), bf16[64,2,2304]{2,1,0:T(2,128)(2,1)}, u32[]{:S(2)}, u32[]{:S(2)}) %all-to-all-start.1) | async-done | bytes 589856 | tf_op jit(solution)/shard_map/all_to_all | solution.py:133
  100.1 2.8 %reshape.26.field = bf16[384,768]{1,0:T(8,128)(2,1)} reshape(bf16[64,2,2304]{2,1,0:T(2,128)(2,1)} %all-to-all-done.1) | data formatting | bytes 1179648 | tf_op jit(solution)/shard_map/reshape | solution.py:133
  103.0 1.1 copy-done.2
  104.0 7.5 %shard_map.65 = bf16[384,768]{1,0:T(8,128)(2,1)S(1)} custom-call(s32[1]{0:T(128)} %bitcast.4.core, f32[3]{0:T(128)S(1)} %copy-done.4, f32[1]{0:T(128)} %collective-permute-done.1.member, bf16[384,768]{1,0:T(8,128)(2,1)S(1)} %copy-done.2, bf16[4,384,768]{2,1,0:T(8,128)(2,1)S(1)} %bitcast.28, bf16[384,768]{1,0:T(8,128)(2,1)} %collective-permute-done.2.rest_0_, ...), custom_call_target="tpu_custom_call" | custom-call | flops 2000000000 | bytes 5000000 | tf_op jit(solution)/shard_map/pallas_call | solution.py:77
  112.3 1.9 %reshape.28 = bf16[64,2,2304]{2,1,0:T(2,128)(2,1)S(1)} reshape(bf16[384,768]{1,0:T(8,128)(2,1)} %copy-done.3) | data formatting | bytes 1179648 | tf_op jit(solution)/shard_map/reshape | solution.py:137
  114.2 27.2 %all_to_all.20 = bf16[64,2,2304]{2,1,0:T(2,128)(2,1)S(1)} all-to-all(bf16[64,2,2304]{2,1,0:T(2,128)(2,1)S(1)} %reshape.28), channel_id=1, replica_groups=mesh['x'=4,'zh'=2,'zl'=4,'y'=8,'c'=2] {'c','zl','y'}, dimensions={0} | all-to-all | bytes 1179648 | tf_op jit(solution)/shard_map/all_to_all | solution.py:138
  141.4 1.3 reshape.29.back
  142.7 2.9 %shard_map.66 = f32[6,8,768]{2,1,0:T(8,128)} custom-call(bf16[8,6,8,768]{3,2,1,0:T(8,128)(2,1)} %copy-done.5, bf16[2,4,8,6,768]{4,3,2,1,0:T(8,128)(2,1)} %reshape.29.back), custom_call_target="tpu_custom_call" | custom-call | flops 1000000 | bytes 2000000 | tf_op jit(solution)/shard_map/pallas_call | solution.py:107
  (31 shorter events, 3.8 us)
Async XLA Ops:
  6.5 44.2 %copy-start = (f32[64,6,768]{2,0,1:T(8,128)S(1)}, f32[64,6,768]{2,0,1:T(8,128)}, u32[]{:S(2)}) copy-start(f32[64,6,768]{2,0,1:T(8,128)} %param.7) | copy-start | bytes 3538948
  6.5 25.4 %collective-permute-start = (bf16[3,96,768]{2,1,0:T(8,128)(2,1)}, bf16[3,96,768]{2,1,0:T(8,128)(2,1)S(1)}, u32[]{:S(2)}, u32[]{:S(2)}) collective-permute-start(bf16[3,96,768]{2,1,0:T(8,128)(2,1)} %param.10), channel_id=1, source_target_pairs={{0,0},{1,64},{64,1},{65,65},{2,2},{3,66},{66,3},{67,67},{4,4},{5,6... | collective-permute-start | bytes 1327112 | tf_op jit(solution)/shard_map/ppermute | solution.py:120
  19.4 22.9 %copy-start.7 = (bf16[1,64,6,768]{3,1,2,0:T(8,128)(2,1)S(1)}, bf16[1,64,6,768]{3,1,2,0:T(8,128)(2,1)}, u32[]{:S(2)}) copy-start(bf16[1,64,6,768]{3,1,2,0:T(8,128)(2,1)} %param.6) | copy-start | bytes 1769476
  20.1 19.5 %all-to-all-start.2 = ((bf16[32,8,384]{2,1,0:T(8,128)(2,1)}), bf16[32,8,384]{2,1,0:T(8,128)(2,1)S(1)}, u32[]{:S(2)}, u32[]{:S(2)}) async-start(bf16[32,8,384]{2,1,0:T(8,128)(2,1)} %broadcast_in_dim.2), calls=%async_computation.2 | async-start | bytes 393216 | tf_op jit(solution)/shard_map/all_to_all | solution.py:123
  30.1 54.1 %all-gather.3.cloned.1.call-start = ((), (), s32[]{:S(2)}) async-start(), calls=%async_computation.4 | async-start | bytes 2949120 | tf_op jit(solution)/shard_map/all_gather | solution.py:128
  30.1 1.8 %collective-permute-start.1 = (f32[1]{0:T(128)}, f32[1]{0:T(128)}, u32[]{:S(2)}, u32[]{:S(2)}) collective-permute-start(f32[1]{0:T(128)} %param.8), channel_id=1, source_target_pairs={{0,0},{1,1},{2,2},{3,3},{4,4},{5,5},{6,6},{7,7},{64,8},{65,9},{66,... | collective-permute-start | bytes 20 | tf_op jit(solution)/shard_map/ppermute | solution.py:125
  31.9 7.7 %copy-start.8 = (bf16[3,96,768]{2,1,0:T(8,128)(2,1)}, bf16[3,96,768]{2,1,0:T(8,128)(2,1)S(1)}, u32[]{:S(2)}) copy-start(bf16[3,96,768]{2,1,0:T(8,128)(2,1)S(1)} %collective-permute-done) | copy-start | bytes 1327108
  39.6 0.7 copy-start.6
  43.1 19.8 %all-to-all-start = ((bf16[8,6,8,768]{3,2,1,0:T(8,128)(2,1)}), bf16[8,6,8,768]{3,2,1,0:T(8,128)(2,1)S(1)}, u32[]{:S(2)}, u32[]{:S(2)}) async-start(bf16[8,6,8,768]{3,2,1,0:T(8,128)(2,1)} %copy_bitcast_fusion), calls=%async_computation | async-start | bytes 1179648 | tf_op jit(solution)/shard_map/all_to_all | solution.py:119
  62.9 0.8 copy-start.5
  65.0 35.1 %all-to-all-start.1 = ((bf16[64,2,2304]{2,1,0:T(2,128)(2,1)}), bf16[64,2,2304]{2,1,0:T(2,128)(2,1)}, u32[]{:S(2)}, u32[]{:S(2)}) async-start(bf16[64,2,2304]{2,1,0:T(2,128)(2,1)} %reshape.25), calls=%async_computation.1 | async-start | bytes 1179648 | tf_op jit(solution)/shard_map/all_to_all | solution.py:133
  84.1 18.8 %copy-start.1 = (bf16[1536,768]{1,0:T(8,128)(2,1)S(1)}, bf16[1536,768]{1,0:T(8,128)(2,1)}, u32[]{:S(2)}) copy-start(bf16[1536,768]{1,0:T(8,128)(2,1)} %all-gather.3.cloned.1.call-done) | copy-start | bytes 7077892
  87.4 15.6 %copy-start.4 = (f32[3]{0:T(128)S(1)}, f32[3]{0:T(128)}, u32[]{:S(2)}) copy-start(f32[3]{0:T(128)} %scale.1) | copy-start | bytes 40
  87.4 15.5 %collective-permute-start.5 = (bf16[384,768]{1,0:T(8,128)(2,1)}, bf16[384,768]{1,0:T(8,128)(2,1)}, u32[]{:S(2)}, u32[]{:S(2)}) collective-permute-start(bf16[384,768]{1,0:T(8,128)(2,1)} %get-tuple-element.11), channel_id=1, source_target_pairs={{0,1},{1,0},{2,3},{3,2},{4,5},{5,4},{6,7},{7,6},{8,9},{9,8},{10,11... | collective-permute-start | bytes 1769480 | tf_op jit(solution)/shard_map/ppermute | solution.py:135
  90.1 12.8 %collective-permute-start.4 = (bf16[384,768]{1,0:T(8,128)(2,1)}, bf16[384,768]{1,0:T(8,128)(2,1)}, u32[]{:S(2)}, u32[]{:S(2)}) collective-permute-start(bf16[384,768]{1,0:T(8,128)(2,1)} %get-tuple-element.12), channel_id=1, source_target_pairs={{0,1},{1,0},{2,3},{3,2},{4,5},{5,4},{6,7},{7,6},{8,9},{9,8},{10,11... | collective-permute-start | bytes 1769480 | tf_op jit(solution)/shard_map/ppermute | solution.py:135
  92.0 10.9 %collective-permute-start.3 = (bf16[384,768]{1,0:T(8,128)(2,1)}, bf16[384,768]{1,0:T(8,128)(2,1)}, u32[]{:S(2)}, u32[]{:S(2)}) collective-permute-start(bf16[384,768]{1,0:T(8,128)(2,1)} %get-tuple-element.13), channel_id=1, source_target_pairs={{0,1},{1,0},{2,3},{3,2},{4,5},{5,4},{6,7},{7,6},{8,9},{9,8},{10,11... | collective-permute-start | bytes 1769480 | tf_op jit(solution)/shard_map/ppermute | solution.py:135
  94.4 8.5 %collective-permute-start.2 = (bf16[384,768]{1,0:T(8,128)(2,1)}, bf16[384,768]{1,0:T(8,128)(2,1)}, u32[]{:S(2)}, u32[]{:S(2)}) collective-permute-start(bf16[384,768]{1,0:T(8,128)(2,1)} %get-tuple-element.14), channel_id=1, source_target_pairs={{0,1},{1,0},{2,3},{3,2},{4,5},{5,4},{6,7},{7,6},{8,9},{9,8},{10,11... | collective-permute-start | bytes 1769480 | tf_op jit(solution)/shard_map/ppermute | solution.py:135
  102.9 1.1 copy-start.2
  111.5 0.8 copy-start.3
Sparse Core Ops, SparseCore 0:
  42.4 41.7 all-gather.2

commit v6 on v4

--- a/solution.py
+++ b/solution.py
@@ -17,24 +17,21 @@
 HBM = pl.BlockSpec(memory_space=pltpu.MemorySpace.HBM)
 
 
-def pack_kernel(block, tiles, out, sem):
-    copy = pltpu.make_async_copy(block, out.at[pl.ds(0, 288)], sem)
-    copy.start()
+def pack_kernel(block, tiles, out):
+    out[pl.ds(0, 288), :] = block[...]
     for half in range(2):
         for part in range(4):
             first = 16 * half + 4 * part
             rows = [tiles[first + n, :6, :].astype(F32) for n in range(4)]
             out[pl.ds(288 + 24 * part, 24), pl.ds(384 * half, 384)] = jnp.concatenate(rows, axis=0).astype(BF16)
-    copy.wait()
 
 
 def pack(block, tiles):
     return pl.pallas_call(
         pack_kernel,
         out_shape=jax.ShapeDtypeStruct((384, 768), BF16),
-        in_specs=[ANY, VMEM],
+        in_specs=[VMEM, VMEM],
         out_specs=VMEM,
-        scratch_shapes=[pltpu.SemaphoreType.DMA],
         cost_estimate=pl.CostEstimate(flops=10**6, bytes_accessed=2 * 10**6, transcendentals=0),
     )(block, tiles)
 
@@ -88,7 +85,7 @@
             pltpu.SemaphoreType.DMA((2, 3, 4)),
             pltpu.SemaphoreType.DMA((2, 3, 2)),
         ],
-        compiler_params=pltpu.CompilerParams(vmem_limit_bytes=62 * 2**20),
+        compiler_params=pltpu.CompilerParams(vmem_limit_bytes=40 * 2**20),
         cost_estimate=pl.CostEstimate(flops=2 * 10**9, bytes_accessed=5 * 10**6, transcendentals=0),
     )(core, scale, member, field, mine, other)
 
@@ -119,16 +116,16 @@
     core = lax.axis_index("c")
     own = perturbations[0].transpose(1, 0, 2).reshape(6, 8, 8, 768).transpose(1, 0, 2, 3)
     own = lax.all_to_all(own, MEM, split_axis=0, concat_axis=0, tiled=True)
+    turn = [((c // 8) * 64 + m * 8 + c % 8, m * 64 + c) for m in range(8) for c in range(64)]
+    weight = lax.ppermute(member_weights, MEM + COL, turn)
     block = lax.ppermute(lon_filter, ("zh", "c"), [(0, 0), (1, 2), (2, 1), (3, 3)])
     rows = lax.dynamic_index_in_dim(lat_filter, jnp.minimum(lax.axis_index("x"), 2), 0, False)
     tiles = jnp.broadcast_to(jnp.pad(rows, ((0, 2), (0, 0)))[None], (32, 8, 384))
+    own, weight, block, tiles = lax.optimization_barrier((own, weight, block, tiles))
     tiles = lax.all_to_all(tiles, ("zl", "y"), split_axis=0, concat_axis=0, tiled=True)
     packed = pack(block.reshape(288, 768), tiles)
+    own, packed = lax.optimization_barrier((own, packed))
     mine = lax.all_gather(packed, "x", axis=0)
-    turn = [((c // 8) * 64 + m * 8 + c % 8, m * 64 + c) for m in range(8) for c in range(64)]
-    weight = lax.ppermute(member_weights, MEM + COL, turn)
-    own, weight = lax.optimization_barrier((own, weight))
-
     member = lax.axis_index(MEM)
     level = lax.dynamic_slice_in_dim(gradient.transpose(1, 0, 2), member * 8, 8, axis=1)
     schur = (own.astype(F32) * level[None]).astype(BF16)

time: 152 us -> 163 us (1.072)
  waiting for transfers between devices: 15 us -> 28.6 us
  starting transfers between devices: 20.6 us -> 26.1 us
  blocking collectives: 79.6 us -> 74.9 us
  Pallas kernels: 14.5 us -> 12.3 us
    ppermute x1, waiting for transfers between devices: 0.01 us -> 15.7 us  [on_device(): lax.ppermute(lon_filter, ('zh', 'c'), [(0, 0), (1, 2), (2, 1), (3, 3)])]
    all_to_all x1, blocking collectives: 35.3 us -> 23.2 us  [on_device(): lax.all_to_all(schur, COL, split_axis=0, concat_axis=0, tiled=True)]
    all_to_all x1, waiting for transfers between devices: 10.5 us -> 0.01 us  [on_device(): own = lax.all_to_all(own, MEM, split_axis=0, concat_axis=0, tiled=True)]
    all_to_all x1, starting transfers between devices: 4.02 us -> 13.3 us  [on_device(): own = lax.all_to_all(own, MEM, split_axis=0, concat_axis=0, tiled=True)]
    all_gather x1, waiting for transfers between devices: 0.01 us -> 8.35 us  [on_device(): mine = lax.all_gather(packed, 'x', axis=0)]
    all_to_all x1, blocking collectives: 24.8 us -> 30.2 us  [on_device(): lax.all_to_all(filtered, ('c', 'zl', 'y'), split_axis=0, concat_axis=0, t...]
    ppermute x1, starting transfers between devices: 12.1 us -> 8.35 us  [on_device(): lax.ppermute(lon_filter, ('zh', 'c'), [(0, 0), (1, 2), (2, 1), (3, 3)])]
    all_to_all x1, blocking collectives: 19.5 us -> 21.5 us  [on_device(): lax.all_to_all(tiles, ('zl', 'y'), split_axis=0, concat_axis=0, tiled=True)]
  transfers between devices with their start and end apart: 5 -> 5, of which waited for: 2 -> 3; matrix products, arithmetic and copies ran while one was open for 2% -> 1% of each run, Pallas kernels for 0% -> 0%
where the time goes in v6:
time: 163 us
  blocking collectives  74.9 us (46%)
  waiting for transfers between devices  28.6 us (18%)
  starting transfers between devices  26.1 us (16%)
  between operations  13.5 us (8%)
  Pallas kernels  12.3 us (8%)
  local copies, waits for them, and re-layouts  6.99 us (4%)
    all_to_all x1, blocking collectives, on_device(): lax.all_to_all(filtered, ('c', 'zl', 'y'), split_axis=0, concat_axis=0, t...  30.2 us
    all_to_all x1, blocking collectives, on_device(): lax.all_to_all(schur, COL, split_axis=0, concat_axis=0, tiled=True)  23.2 us
    all_to_all x1, blocking collectives, on_device(): lax.all_to_all(tiles, ('zl', 'y'), split_axis=0, concat_axis=0, tiled=True)  21.5 us
    ppermute x1, waiting for transfers between devices, on_device(): lax.ppermute(lon_filter, ('zh', 'c'), [(0, 0), (1, 2), (2, 1), (3, 3)])  15.7 us
    all_to_all x1, starting transfers between devices, on_device(): own = lax.all_to_all(own, MEM, split_axis=0, concat_axis=0, tiled=True)  13.3 us
    all_gather x1, waiting for transfers between devices, on_device(): mine = lax.all_gather(packed, 'x', axis=0)  8.35 us
    ppermute x1, starting transfers between devices, on_device(): lax.ppermute(lon_filter, ('zh', 'c'), [(0, 0), (1, 2), (2, 1), (3, 3)])  8.35 us
    pallas_call x1, Pallas kernels, filter_pair(): pl.pallas_call(filter_kernel, out_shape=jax.ShapeDtypeStruct((384, 768),...  7.45 us
  transfers between devices with their start and end apart: 5, of which 3 were waited for; matrix products, arithmetic and copies ran while one was open for 1% of the time, Pallas kernels for 0%

profile of v6, /device:TPU:1, one launch (start us, length us, event | category | flops | bytes accessed | tf_op | source)
XLA Modules:
  0.0 162.5 jit_solution(6048278370227129861)
XLA Ops:
  6.5 2.0 %copy_bitcast_fusion = bf16[8,6,8,768]{3,2,1,0:T(8,128)(2,1)} fusion(bf16[1,64,6,768]{3,1,2,0:T(8,128)(2,1)} %param.6), kind=kLoop, calls=%fused_computation.2 | loop fusion | bytes 1179648 | tf_op jit(solution)/shard_map/transpose | solution.py:117
  8.6 13.3 %all-to-all-start = ((bf16[8,6,8,768]{3,2,1,0:T(8,128)(2,1)}), bf16[8,6,8,768]{3,2,1,0:T(8,128)(2,1)S(1)}, u32[]{:S(2)}, u32[]{:S(2)}) async-start(bf16[8,6,8,768]{3,2,1,0:T(8,128)(2,1)} %copy_bitcast_fusion), calls=%async_computation | async-start | bytes 1179648 | tf_op jit(solution)/shard_map/all_to_all | solution.py:118
  21.9 0.0 all-gather.3.cloned.1.call-start
  21.9 8.4 %collective-permute-start.1 = (bf16[3,96,768]{2,1,0:T(8,128)(2,1)S(1)}, bf16[3,96,768]{2,1,0:T(8,128)(2,1)S(1)}, u32[]{:S(2)}, u32[]{:S(2)}) collective-permute-start(bf16[3,96,768]{2,1,0:T(8,128)(2,1)S(1)} %copy-done.5), channel_id=1, source_target_pairs={{0,0},{1,64},{64,1},{65,65},{2,2},{3,66},{66,3},{67,67},{4,4},{5,6... | collective-permute-start | bytes 1327112 | tf_op jit(solution)/shard_map/ppermute | solution.py:121
  30.3 1.8 %collective-permute-start = (f32[1]{0:T(128)}, f32[1]{0:T(128)}, u32[]{:S(2)}, u32[]{:S(2)}) collective-permute-start(f32[1]{0:T(128)} %param.8), channel_id=1, source_target_pairs={{0,0},{1,1},{2,2},{3,3},{4,4},{5,5},{6,6},{7,7},{64,8},{65,9},{66,... | collective-permute-start | bytes 20 | tf_op jit(solution)/shard_map/ppermute | solution.py:120
  32.1 0.7 dynamic-slice_bitcast_fusion.1
  32.8 15.7 %collective-permute-done.1 = bf16[3,96,768]{2,1,0:T(8,128)(2,1)S(1)} collective-permute-done((bf16[3,96,768]{2,1,0:T(8,128)(2,1)S(1)}, bf16[3,96,768]{2,1,0:T(8,128)(2,1)S(1)}, u32[]{:S(2)}, u32[]{:S(2)}) %collective-permute-start.1) | collective-permute-done | bytes 442400 | tf_op jit(solution)/shard_map/ppermute | solution.py:121
  48.6 21.5 %all_to_all.20.tiles = bf16[32,8,384]{2,1,0:T(8,128)(2,1)} all-to-all(bf16[32,8,384]{2,1,0:T(8,128)(2,1)S(1)} %broadcast_in_dim.2), channel_id=1, replica_groups=mesh['x'=4,'zh'=2,'zl'=4,'y'=8,'c'=2] {'zl','y'}, dimensions={0} | all-to-all | bytes 393216 | tf_op jit(solution)/shard_map/all_to_all | solution.py:125
  70.1 2.0 %shard_map.64 = bf16[384,768]{1,0:T(8,128)(2,1)} custom-call(bf16[288,768]{1,0:T(8,128)(2,1)} %bitcast.21, bf16[32,8,384]{2,1,0:T(8,128)(2,1)} %all_to_all.20.tiles), custom_call_target="tpu_custom_call" | custom-call | flops 1000000 | bytes 2000000 | tf_op jit(solution)/shard_map/pallas_call | solution.py:30
  72.0 0.0 all-gather.3.cloned.1.call-update
  72.1 0.1 fusion
  72.2 0.1 copy.8
  72.4 0.4 reshape.26
  72.8 23.2 %all_to_all.21 = bf16[64,2,2304]{2,1,0:T(2,128)(2,1)S(1)} all-to-all(bf16[64,2,2304]{2,1,0:T(2,128)(2,1)S(1)} %reshape.26), channel_id=1, replica_groups=mesh['x'=4,'zh'=2,'zl'=4,'y'=8,'c'=2] {'zl','y','c'}, dimensions={0} | all-to-all | bytes 1179648 | tf_op jit(solution)/shard_map/all_to_all | solution.py:133
  96.0 0.4 reshape.27.field
  96.4 8.4 %all-gather.3.cloned.1.call-done = bf16[1536,768]{1,0:T(8,128)(2,1)} async-done(((bf16[384,768]{1,0:T(8,128)(2,1)}), bf16[1536,768]{1,0:T(8,128)(2,1)}) %all-gather.3.cloned.1.call-update) | async-done | bytes 2359312 | tf_op jit(solution)/shard_map/all_gather | solution.py:128
  104.7 2.6 %collective-permute-start.2 = (bf16[4,384,768]{2,1,0:T(8,128)(2,1)}, bf16[4,384,768]{2,1,0:T(8,128)(2,1)}, u32[]{:S(2)}, u32[]{:S(2)}) collective-permute-start(bf16[4,384,768]{2,1,0:T(8,128)(2,1)} %bitcast.19), channel_id=1, source_target_pairs={{0,1},{1,0},{2,3},{3,2},{4,5},{5,4},{6,7},{7,6},{8,9},{9,8},{10,11... | collective-permute-start | bytes 7077896 | tf_op jit(solution)/shard_map/ppermute | solution.py:135
  107.3 4.5 %collective-permute-done.2.other = bf16[4,384,768]{2,1,0:T(8,128)(2,1)} collective-permute-done((bf16[4,384,768]{2,1,0:T(8,128)(2,1)}, bf16[4,384,768]{2,1,0:T(8,128)(2,1)}, u32[]{:S(2)}, u32[]{:S(2)}) %collective-permute-start.2) | collective-permute-done | bytes 2359328 | tf_op jit(solution)/shard_map/ppermute | solution.py:135
  111.8 1.7 %copy-done.1 = bf16[1536,768]{1,0:T(8,128)(2,1)S(1)} copy-done((bf16[1536,768]{1,0:T(8,128)(2,1)S(1)}, bf16[1536,768]{1,0:T(8,128)(2,1)}, u32[]{:S(2)}) %copy-start.1) | copy-done | bytes 2359320
  113.4 7.4 %shard_map.65 = bf16[384,768]{1,0:T(8,128)(2,1)S(1)} custom-call(s32[1]{0:T(128)} %bitcast.6.core, f32[3]{0:T(128)S(1)} %copy-done.2, f32[1]{0:T(128)} %collective-permute-done.member, bf16[384,768]{1,0:T(8,128)(2,1)S(1)} %reshape.27.field, bf16[4,384,768]{2,1,0:T(8,128)(2,1)S(1)} %bitcast.20, bf16[4,384,768]{2,1,0:T(8,128)(2,1)} %collective-permute-done.2.other), custom_call_target="tpu_custom_call" | custom-call | flops 2000000000 | bytes 5000000 | tf_op jit(solution)/shard_map/pallas_call | solution.py:76
  120.9 0.3 reshape.28
  121.2 30.2 %all_to_all.22 = bf16[64,2,2304]{2,1,0:T(2,128)(2,1)S(1)} all-to-all(bf16[64,2,2304]{2,1,0:T(2,128)(2,1)S(1)} %reshape.28), channel_id=1, replica_groups=mesh['x'=4,'zh'=2,'zl'=4,'y'=8,'c'=2] {'c','zl','y'}, dimensions={0} | all-to-all | bytes 1179648 | tf_op jit(solution)/shard_map/all_to_all | solution.py:138
  151.5 1.3 reshape.29.back
  152.7 2.9 %shard_map.66 = f32[6,8,768]{2,1,0:T(8,128)} custom-call(bf16[8,6,8,768]{3,2,1,0:T(8,128)(2,1)} %copy-done.3, bf16[2,4,8,6,768]{4,3,2,1,0:T(8,128)(2,1)} %reshape.29.back), custom_call_target="tpu_custom_call" | custom-call | flops 1000000 | bytes 2000000 | tf_op jit(solution)/shard_map/pallas_call | solution.py:106
  (16 shorter events, 0.1 us)
Async XLA Ops:
  6.5 65.5 %copy-start = (f32[64,6,768]{2,0,1:T(8,128)S(1)}, f32[64,6,768]{2,0,1:T(8,128)}, u32[]{:S(2)}) copy-start(f32[64,6,768]{2,0,1:T(8,128)} %param.7) | copy-start | bytes 3538948
  6.5 15.4 %copy-start.5 = (bf16[3,96,768]{2,1,0:T(8,128)(2,1)S(1)}, bf16[3,96,768]{2,1,0:T(8,128)(2,1)}, u32[]{:S(2)}) copy-start(bf16[3,96,768]{2,1,0:T(8,128)(2,1)} %param.10) | copy-start | bytes 1327108
  8.6 40.0 %all-to-all-start = ((bf16[8,6,8,768]{3,2,1,0:T(8,128)(2,1)}), bf16[8,6,8,768]{3,2,1,0:T(8,128)(2,1)S(1)}, u32[]{:S(2)}, u32[]{:S(2)}) async-start(bf16[8,6,8,768]{3,2,1,0:T(8,128)(2,1)} %copy_bitcast_fusion), calls=%async_computation | async-start | bytes 1179648 | tf_op jit(solution)/shard_map/all_to_all | solution.py:118
  21.9 82.8 %all-gather.3.cloned.1.call-start = ((), (), s32[]{:S(2)}) async-start(), calls=%async_computation.4 | async-start | bytes 2949120 | tf_op jit(solution)/shard_map/all_gather | solution.py:128
  21.9 26.6 %collective-permute-start.1 = (bf16[3,96,768]{2,1,0:T(8,128)(2,1)S(1)}, bf16[3,96,768]{2,1,0:T(8,128)(2,1)S(1)}, u32[]{:S(2)}, u32[]{:S(2)}) collective-permute-start(bf16[3,96,768]{2,1,0:T(8,128)(2,1)S(1)} %copy-done.5), channel_id=1, source_target_pairs={{0,0},{1,64},{64,1},{65,65},{2,2},{3,66},{66,3},{67,67},{4,4},{5,6... | collective-permute-start | bytes 1327112 | tf_op jit(solution)/shard_map/ppermute | solution.py:121
  30.3 2.5 %collective-permute-start = (f32[1]{0:T(128)}, f32[1]{0:T(128)}, u32[]{:S(2)}, u32[]{:S(2)}) collective-permute-start(f32[1]{0:T(128)} %param.8), channel_id=1, source_target_pairs={{0,0},{1,1},{2,2},{3,3},{4,4},{5,5},{6,6},{7,7},{64,8},{65,9},{66,... | collective-permute-start | bytes 20 | tf_op jit(solution)/shard_map/ppermute | solution.py:120
  48.5 21.5 %copy-start.4 = (bf16[3,96,768]{2,1,0:T(8,128)(2,1)}, bf16[3,96,768]{2,1,0:T(8,128)(2,1)S(1)}, u32[]{:S(2)}) copy-start(bf16[3,96,768]{2,1,0:T(8,128)(2,1)S(1)} %collective-permute-done.1) | copy-start | bytes 1327108
  48.5 23.5 %copy-start.3 = (bf16[8,6,8,768]{3,2,1,0:T(8,128)(2,1)}, bf16[8,6,8,768]{3,2,1,0:T(8,128)(2,1)S(1)}, u32[]{:S(2)}) copy-start(bf16[8,6,8,768]{3,2,1,0:T(8,128)(2,1)S(1)} %all-to-all-done.own) | copy-start | bytes 1769476
  72.8 39.0 %copy-start.2 = (f32[3]{0:T(128)S(1)}, f32[3]{0:T(128)}, u32[]{:S(2)}) copy-start(f32[3]{0:T(128)} %scale.1) | copy-start | bytes 40
  104.7 7.1 %collective-permute-start.2 = (bf16[4,384,768]{2,1,0:T(8,128)(2,1)}, bf16[4,384,768]{2,1,0:T(8,128)(2,1)}, u32[]{:S(2)}, u32[]{:S(2)}) collective-permute-start(bf16[4,384,768]{2,1,0:T(8,128)(2,1)} %bitcast.19), channel_id=1, source_target_pairs={{0,1},{1,0},{2,3},{3,2},{4,5},{5,4},{6,7},{7,6},{8,9},{9,8},{10,11... | collective-permute-start | bytes 7077896 | tf_op jit(solution)/shard_map/ppermute | solution.py:135
  111.8 1.7 %copy-start.1 = (bf16[1536,768]{1,0:T(8,128)(2,1)S(1)}, bf16[1536,768]{1,0:T(8,128)(2,1)}, u32[]{:S(2)}) copy-start(bf16[1536,768]{1,0:T(8,128)(2,1)} %all-gather.3.cloned.1.call-done) | copy-start | bytes 7077892
Sparse Core Ops, SparseCore 0:
  72.2 32.5 all-gather.2

commit v7 on v6

--- a/solution.py
+++ b/solution.py
@@ -90,53 +90,54 @@
     )(core, scale, member, field, mine, other)
 
 
-def final_kernel(own, back, out):
-    for r in range(6):
-        total = jnp.zeros((8, 768), F32)
-        for k in range(8):
-            parts = [
-                back[l % 2, k // 2, 4 * (k % 2) + l // 2, r, :].astype(F32).reshape(1, 768)
-                for l in range(8)
-            ]
-            total += own[k, r].astype(F32) * jnp.concatenate(parts, axis=0)
-        out[r] = total
+def final_kernel(side, own, back, keep, send):
+    for out, h in ((keep, side[0]), (send, 1 - side[0])):
+        for r in range(6):
+            total = jnp.zeros((8, 768), F32)
+            for x in range(4):
+                parts = [
+                    back[l % 2, x, 4 * h + l // 2, r, :].astype(F32).reshape(1, 768) for l in range(8)
+                ]
+                total += own[x, r, h].astype(F32) * jnp.concatenate(parts, axis=0)
+            out[r] = total.astype(out.dtype)
 
 
-def final_sum(own, back):
+def final_sum(side, own, back):
     return pl.pallas_call(
         final_kernel,
-        out_shape=jax.ShapeDtypeStruct((6, 8, 768), F32),
-        in_specs=[VMEM, VMEM],
-        out_specs=VMEM,
+        out_shape=(jax.ShapeDtypeStruct((6, 8, 768), F32), jax.ShapeDtypeStruct((6, 8, 768), BF16)),
+        in_specs=[SMEM, VMEM, VMEM],
+        out_specs=(VMEM, VMEM),
         cost_estimate=pl.CostEstimate(flops=10**6, bytes_accessed=2 * 10**6, transcendentals=0),
-    )(own, back)
+    )(side, own, back)
 
 
 def on_device(perturbations, gradient, member_weights, scale_weights, lon_filter, lat_filter):
-    core = lax.axis_index("c")
-    own = perturbations[0].transpose(1, 0, 2).reshape(6, 8, 8, 768).transpose(1, 0, 2, 3)
-    own = lax.all_to_all(own, MEM, split_axis=0, concat_axis=0, tiled=True)
-    turn = [((c // 8) * 64 + m * 8 + c % 8, m * 64 + c) for m in range(8) for c in range(64)]
-    weight = lax.ppermute(member_weights, MEM + COL, turn)
+    x, side, core = lax.axis_index("x"), lax.axis_index("zh"), lax.axis_index("c")
     block = lax.ppermute(lon_filter, ("zh", "c"), [(0, 0), (1, 2), (2, 1), (3, 3)])
-    rows = lax.dynamic_index_in_dim(lat_filter, jnp.minimum(lax.axis_index("x"), 2), 0, False)
+    rows = lax.dynamic_index_in_dim(lat_filter, jnp.minimum(x, 2), 0, False)
     tiles = jnp.broadcast_to(jnp.pad(rows, ((0, 2), (0, 0)))[None], (32, 8, 384))
-    own, weight, block, tiles = lax.optimization_barrier((own, weight, block, tiles))
     tiles = lax.all_to_all(tiles, ("zl", "y"), split_axis=0, concat_axis=0, tiled=True)
     packed = pack(block.reshape(288, 768), tiles)
-    own, packed = lax.optimization_barrier((own, packed))
     mine = lax.all_gather(packed, "x", axis=0)
-    member = lax.axis_index(MEM)
-    level = lax.dynamic_slice_in_dim(gradient.transpose(1, 0, 2), member * 8, 8, axis=1)
-    schur = (own.astype(F32) * level[None]).astype(BF16)
-    schur = schur.transpose(0, 2, 1, 3).reshape(64, 2, 2304)
+
+    own = perturbations[0].transpose(1, 0, 2).reshape(6, 4, 2, 8, 768).transpose(1, 0, 2, 3, 4)
+    own = lax.all_to_all(own, "x", split_axis=0, concat_axis=0, tiled=True)
+    turn = [(4 * a + b, 4 * b + a) for a in range(4) for b in range(4)]
+    weight = lax.ppermute(member_weights, ("x", "zl"), turn)
+    own, weight = lax.optimization_barrier((own, weight))
+    level = lax.dynamic_slice_in_dim(gradient.transpose(1, 0, 2), x * 16, 16, axis=1)
+    schur = (own.astype(F32) * level.reshape(1, 6, 2, 8, 768)).astype(BF16)
+    schur = schur.transpose(0, 2, 3, 1, 4).reshape(64, 2, 2304)
     field = lax.all_to_all(schur, COL, split_axis=0, concat_axis=0, tiled=True).reshape(384, 768)
     mine = lax.optimization_barrier((mine, field))[0]
     other = lax.ppermute(mine, "c", SWAP)
     core = core.reshape(1).astype(jnp.int32)
     filtered = filter_pair(core, scale_weights, weight, field, mine, other).reshape(64, 2, 2304)
     back = lax.all_to_all(filtered, ("c", "zl", "y"), split_axis=0, concat_axis=0, tiled=True)
-    return final_sum(own, back.reshape(2, 4, 8, 6, 768)).transpose(1, 0, 2)
+    keep, send = final_sum(side.reshape(1).astype(jnp.int32), own, back.reshape(2, 4, 8, 6, 768))
+    total = keep + lax.ppermute(send, "zh", SWAP).astype(F32)
+    return total.transpose(1, 0, 2)
 
 
 def solution(mesh):

time: 163 us -> 149 us (0.914)
  blocking collectives: 74.9 us -> 47.5 us
  starting transfers between devices: 26.1 us -> 32.4 us
  waiting for transfers between devices: 28.6 us -> 32.3 us
    all_to_all x1 -> x0, blocking collectives: 30.2 us -> none  [on_device(): lax.all_to_all(filtered, ('c', 'zl', 'y'), split_axis=0, concat_axis=0, t...]
    all_to_all x1 -> x2, waiting for transfers between devices: 0.01 us -> 24.8 us  [the longest x1 19.4 us: on_device(): lax.all_to_all(filtered, ('c', 'zl', 'y'), split_axis=0, concat_axis=0, t...]
    ppermute x1, waiting for transfers between devices: 15.7 us -> 0.01 us  [on_device(): lax.ppermute(lon_filter, ('zh', 'c'), [(0, 0), (1, 2), (2, 1), (3, 3)])]
    all_gather x1, waiting for transfers between devices: 8.35 us -> 0.02 us  [on_device(): mine = lax.all_gather(packed, 'x', axis=0)]
    ppermute x1 -> x2, starting transfers between devices: 1.84 us -> 8.16 us  [the longest x1 6.29 us: on_device(): total = keep + lax.ppermute(send, 'zh', SWAP).astype(F32)]
    all_to_all x1, blocking collectives: 23.2 us -> 28 us  [on_device(): lax.all_to_all(schur, COL, split_axis=0, concat_axis=0, tiled=True)]
    ppermute x1, starting transfers between devices: 8.35 us -> 12.1 us  [on_device(): lax.ppermute(lon_filter, ('zh', 'c'), [(0, 0), (1, 2), (2, 1), (3, 3)])]
    all_to_all x1 -> x2, starting transfers between devices: 13.3 us -> 9.57 us  [the longest x1 5.56 us: on_device(): lax.all_to_all(filtered, ('c', 'zl', 'y'), split_axis=0, concat_axis=0, t...]
  transfers between devices with their start and end apart: 5 -> 7, of which waited for: 3 -> 4; matrix products, arithmetic and copies ran while one was open for 1% -> 2% of each run, Pallas kernels for 0% -> 0%
where the time goes in v7:
time: 149 us; the launch traced here: 148 us
  blocking collectives  47.5 us (32%)
  starting transfers between devices  32.4 us (22%)
  waiting for transfers between devices  32.3 us (22%)
  between operations  13.5 us (9%)
  Pallas kernels  12.3 us (8%)
  local copies, waits for them, and re-layouts  7.96 us (5%)
  other arithmetic  1.7 us (1%)
    all_to_all x1, blocking collectives, on_device(): lax.all_to_all(schur, COL, split_axis=0, concat_axis=0, tiled=True)  28 us
    all_to_all x1, blocking collectives, on_device(): lax.all_to_all(tiles, ('zl', 'y'), split_axis=0, concat_axis=0, tiled=True)  19.5 us
    all_to_all x1, waiting for transfers between devices, on_device(): lax.all_to_all(filtered, ('c', 'zl', 'y'), split_axis=0, concat_axis=0, t...  19.4 us
    ppermute x1, starting transfers between devices, on_device(): lax.ppermute(lon_filter, ('zh', 'c'), [(0, 0), (1, 2), (2, 1), (3, 3)])  12.1 us
    pallas_call x1, Pallas kernels, filter_pair(): pl.pallas_call(filter_kernel, out_shape=jax.ShapeDtypeStruct((384, 768),...  7.45 us
    ppermute x1, starting transfers between devices, on_device(): total = keep + lax.ppermute(send, 'zh', SWAP).astype(F32)  6.29 us
    all_to_all x1, starting transfers between devices, on_device(): lax.all_to_all(filtered, ('c', 'zl', 'y'), split_axis=0, concat_axis=0, t...  5.56 us
    all_to_all x1, waiting for transfers between devices, on_device(): own = lax.all_to_all(own, 'x', split_axis=0, concat_axis=0, tiled=True)  5.38 us
  transfers between devices with their start and end apart: 7, of which 4 were waited for; matrix products, arithmetic and copies ran while one was open for 2% of the time, Pallas kernels for 0%

profile of v7, /device:TPU:1, one launch (start us, length us, event | category | flops | bytes accessed | tf_op | source)
XLA Modules:
  0.0 147.7 jit_solution(5055782140386931256)
XLA Ops:
  6.5 12.1 %collective-permute-start.1 = (bf16[3,96,768]{2,1,0:T(8,128)(2,1)}, bf16[3,96,768]{2,1,0:T(8,128)(2,1)S(1)}, u32[]{:S(2)}, u32[]{:S(2)}) collective-permute-start(bf16[3,96,768]{2,1,0:T(8,128)(2,1)} %param.10), channel_id=1, source_target_pairs={{0,0},{1,64},{64,1},{65,65},{2,2},{3,66},{66,3},{67,67},{4,4},{5,6... | collective-permute-start | bytes 1327112 | tf_op jit(solution)/shard_map/ppermute | solution.py:117
  18.7 0.7 dynamic-slice_bitcast_fusion.1
  19.4 19.5 %all_to_all.20.tiles = bf16[32,8,384]{2,1,0:T(8,128)(2,1)} all-to-all(bf16[32,8,384]{2,1,0:T(8,128)(2,1)S(1)} %broadcast_in_dim.2), channel_id=1, replica_groups=mesh['x'=4,'zh'=2,'zl'=4,'y'=8,'c'=2] {'zl','y'}, dimensions={0} | all-to-all | bytes 393216 | tf_op jit(solution)/shard_map/all_to_all | solution.py:120
  39.0 0.8 copy-done.5
  39.7 1.9 %shard_map.64 = bf16[384,768]{1,0:T(8,128)(2,1)} custom-call(bf16[288,768]{1,0:T(8,128)(2,1)} %bitcast.25, bf16[32,8,384]{2,1,0:T(8,128)(2,1)} %all_to_all.20.tiles), custom_call_target="tpu_custom_call" | custom-call | flops 1000000 | bytes 2000000 | tf_op jit(solution)/shard_map/pallas_call | solution.py:30
  41.7 0.9 copy.10
  42.6 4.0 %all-to-all-start = ((bf16[4,6,2,8,768]{4,3,2,1,0:T(8,128)(2,1)}), bf16[4,6,2,8,768]{4,3,2,1,0:T(8,128)(2,1)S(1)}, u32[]{:S(2)}, u32[]{:S(2)}) async-start(bf16[4,6,2,8,768]{4,3,2,1,0:T(8,128)(2,1)} %bitcast.21), calls=%async_computation | async-start | bytes 1179648 | tf_op jit(solution)/shard_map/all_to_all | solution.py:125
  46.6 1.9 %collective-permute-start = (f32[1]{0:T(128)}, f32[1]{0:T(128)}, u32[]{:S(2)}, u32[]{:S(2)}) collective-permute-start(f32[1]{0:T(128)} %param.8), channel_id=1, source_target_pairs={{0,0},{16,128},{32,256},{48,384},{128,16},{144,144},{160,272},{176... | collective-permute-start | bytes 20 | tf_op jit(solution)/shard_map/ppermute | solution.py:127
  48.5 5.4 %all-to-all-done.own = bf16[4,6,2,8,768]{4,3,2,1,0:T(8,128)(2,1)S(1)} async-done(((bf16[4,6,2,8,768]{4,3,2,1,0:T(8,128)(2,1)}), bf16[4,6,2,8,768]{4,3,2,1,0:T(8,128)(2,1)S(1)}, u32[]{:S(2)}, u32[]{:S(2)}) %all-to-all-start) | async-done | bytes 589856 | tf_op jit(solution)/shard_map/all_to_all | solution.py:125
  54.2 0.5 copy-done.3
  54.7 0.4 reshape.30
  55.1 28.0 %all_to_all.21 = bf16[64,2,2304]{2,1,0:T(2,128)(2,1)S(1)} all-to-all(bf16[64,2,2304]{2,1,0:T(2,128)(2,1)S(1)} %reshape.30), channel_id=1, replica_groups=mesh['x'=4,'zh'=2,'zl'=4,'y'=8,'c'=2] {'zl','y','c'}, dimensions={0} | all-to-all | bytes 1179648 | tf_op jit(solution)/shard_map/all_to_all | solution.py:132
  83.5 2.5 %collective-permute-start.2 = (bf16[4,384,768]{2,1,0:T(8,128)(2,1)}, bf16[4,384,768]{2,1,0:T(8,128)(2,1)}, u32[]{:S(2)}, u32[]{:S(2)}) collective-permute-start(bf16[4,384,768]{2,1,0:T(8,128)(2,1)} %bitcast.22), channel_id=1, source_target_pairs={{0,1},{1,0},{2,3},{3,2},{4,5},{5,4},{6,7},{7,6},{8,9},{9,8},{10,11... | collective-permute-start | bytes 7077896 | tf_op jit(solution)/shard_map/ppermute | solution.py:134
  86.1 4.5 %collective-permute-done.2.other = bf16[4,384,768]{2,1,0:T(8,128)(2,1)} collective-permute-done((bf16[4,384,768]{2,1,0:T(8,128)(2,1)}, bf16[4,384,768]{2,1,0:T(8,128)(2,1)}, u32[]{:S(2)}, u32[]{:S(2)}) %collective-permute-start.2) | collective-permute-done | bytes 2359328 | tf_op jit(solution)/shard_map/ppermute | solution.py:134
  90.6 1.7 %copy-done.1 = bf16[1536,768]{1,0:T(8,128)(2,1)S(1)} copy-done((bf16[1536,768]{1,0:T(8,128)(2,1)S(1)}, bf16[1536,768]{1,0:T(8,128)(2,1)}, u32[]{:S(2)}) %copy-start.1) | copy-done | bytes 2359320
  92.2 7.4 %shard_map.65 = bf16[384,768]{1,0:T(8,128)(2,1)S(1)} custom-call(s32[1]{0:T(128)} %bitcast.5.core, f32[3]{0:T(128)S(1)} %copy-done.2, f32[1]{0:T(128)} %collective-permute-done.member, bf16[384,768]{1,0:T(8,128)(2,1)S(1)} %reshape.31.field, bf16[4,384,768]{2,1,0:T(8,128)(2,1)S(1)} %bitcast.23, bf16[4,384,768]{2,1,0:T(8,128)(2,1)} %collective-permute-done.2.other), custom_call_target="tpu_custom_call" | custom-call | flops 2000000000 | bytes 5000000 | tf_op jit(solution)/shard_map/pallas_call | solution.py:76
  99.7 1.1 reshape.33
  100.8 5.6 %all-to-all-start.3 = ((bf16[64,2,2304]{2,1,0:T(2,128)(2,1)}), bf16[64,2,2304]{2,1,0:T(2,128)(2,1)S(1)}, u32[]{:S(2)}, u32[]{:S(2)}) async-start(bf16[64,2,2304]{2,1,0:T(2,128)(2,1)} %reshape.33), calls=%async_computation.3 | async-start | bytes 1179648 | tf_op jit(solution)/shard_map/all_to_all | solution.py:137
  106.4 19.4 %all-to-all-done.3 = bf16[64,2,2304]{2,1,0:T(2,128)(2,1)S(1)} async-done(((bf16[64,2,2304]{2,1,0:T(2,128)(2,1)}), bf16[64,2,2304]{2,1,0:T(2,128)(2,1)S(1)}, u32[]{:S(2)}, u32[]{:S(2)}) %all-to-all-start.3) | async-done | bytes 589856 | tf_op jit(solution)/shard_map/all_to_all | solution.py:137
  125.8 1.3 reshape.34.back
  127.1 2.9 %shard_map.66 = (f32[6,8,768]{2,1,0:T(8,128)}, bf16[6,8,768]{2,1,0:T(8,128)(2,1)}) custom-call(s32[1]{0:T(128)} %bitcast.side, bf16[4,6,2,8,768]{4,3,2,1,0:T(8,128)(2,1)} %copy-done.3, bf16[2,4,8,6,768]{4,3,2,1,0:T(8,128)(2,1)} %reshape.34.back), custom_call_target="tpu_custom_call" | custom-call | flops 1000000 | bytes 2000000 | tf_op jit(solution)/shard_map/pallas_call | solution.py:106
  130.0 6.3 %collective-permute-start.3 = (bf16[6,8,768]{2,1,0:T(8,128)(2,1)}, bf16[6,8,768]{2,1,0:T(8,128)(2,1)S(1)}, u32[]{:S(2)}, u32[]{:S(2)}) collective-permute-start(bf16[6,8,768]{2,1,0:T(8,128)(2,1)} %get-tuple-element.14), channel_id=1, source_target_pairs={{0,64},{64,0},{1,65},{65,1},{2,66},{66,2},{3,67},{67,3},{4,68},{68... | collective-permute-start | bytes 221192 | tf_op jit(solution)/shard_map/ppermute | solution.py:139
  136.3 3.0 %collective-permute-done.3 = bf16[6,8,768]{2,1,0:T(8,128)(2,1)S(1)} collective-permute-done((bf16[6,8,768]{2,1,0:T(8,128)(2,1)}, bf16[6,8,768]{2,1,0:T(8,128)(2,1)S(1)}, u32[]{:S(2)}, u32[]{:S(2)}) %collective-permute-start.3) | collective-permute-done | bytes 73760 | tf_op jit(solution)/shard_map/ppermute | solution.py:139
  139.3 1.6 %add_bitcast_fusion = f32[8,6,768]{2,0,1:T(8,128)} fusion(f32[6,8,768]{2,1,0:T(8,128)} %get-tuple-element.13, bf16[6,8,768]{2,1,0:T(8,128)(2,1)S(1)} %collective-permute-done.3), kind=kLoop, calls=%fused_computation.4 | loop fusion | flops 73728 | bytes 368640 | tf_op jit(solution)/shard_map/transpose | solution.py:140
  (20 shorter events, 0.8 us)
Async XLA Ops:
  6.5 41.9 %copy-start = (f32[64,6,768]{2,0,1:T(8,128)S(1)}, f32[64,6,768]{2,0,1:T(8,128)}, u32[]{:S(2)}) copy-start(f32[64,6,768]{2,0,1:T(8,128)} %param.7) | copy-start | bytes 3538948
  6.5 77.0 %all-gather.3.cloned.1.call-start = ((), (), s32[]{:S(2)}) async-start(), calls=%async_computation.4 | async-start | bytes 2949120 | tf_op jit(solution)/shard_map/all_gather | solution.py:122
  6.5 32.4 %collective-permute-start.1 = (bf16[3,96,768]{2,1,0:T(8,128)(2,1)}, bf16[3,96,768]{2,1,0:T(8,128)(2,1)S(1)}, u32[]{:S(2)}, u32[]{:S(2)}) collective-permute-start(bf16[3,96,768]{2,1,0:T(8,128)(2,1)} %param.10), channel_id=1, source_target_pairs={{0,0},{1,64},{64,1},{65,65},{2,2},{3,66},{66,3},{67,67},{4,4},{5,6... | collective-permute-start | bytes 1327112 | tf_op jit(solution)/shard_map/ppermute | solution.py:117
  19.4 22.3 %copy-start.4 = (bf16[1,64,6,768]{3,1,2,0:T(8,128)(2,1)S(1)}, bf16[1,64,6,768]{3,1,2,0:T(8,128)(2,1)}, u32[]{:S(2)}) copy-start(bf16[1,64,6,768]{3,1,2,0:T(8,128)(2,1)} %param.6) | copy-start | bytes 1769476
  39.0 0.8 copy-start.5
  42.6 11.3 %all-to-all-start = ((bf16[4,6,2,8,768]{4,3,2,1,0:T(8,128)(2,1)}), bf16[4,6,2,8,768]{4,3,2,1,0:T(8,128)(2,1)S(1)}, u32[]{:S(2)}, u32[]{:S(2)}) async-start(bf16[4,6,2,8,768]{4,3,2,1,0:T(8,128)(2,1)} %bitcast.21), calls=%async_computation | async-start | bytes 1179648 | tf_op jit(solution)/shard_map/all_to_all | solution.py:125
  46.6 1.9 %collective-permute-start = (f32[1]{0:T(128)}, f32[1]{0:T(128)}, u32[]{:S(2)}, u32[]{:S(2)}) collective-permute-start(f32[1]{0:T(128)} %param.8), channel_id=1, source_target_pairs={{0,0},{16,128},{32,256},{48,384},{128,16},{144,144},{160,272},{176... | collective-permute-start | bytes 20 | tf_op jit(solution)/shard_map/ppermute | solution.py:127
  53.9 0.8 copy-start.3
  55.1 35.5 %copy-start.2 = (f32[3]{0:T(128)S(1)}, f32[3]{0:T(128)}, u32[]{:S(2)}) copy-start(f32[3]{0:T(128)} %scale.1) | copy-start | bytes 40
  83.5 7.0 %collective-permute-start.2 = (bf16[4,384,768]{2,1,0:T(8,128)(2,1)}, bf16[4,384,768]{2,1,0:T(8,128)(2,1)}, u32[]{:S(2)}, u32[]{:S(2)}) collective-permute-start(bf16[4,384,768]{2,1,0:T(8,128)(2,1)} %bitcast.22), channel_id=1, source_target_pairs={{0,1},{1,0},{2,3},{3,2},{4,5},{5,4},{6,7},{7,6},{8,9},{9,8},{10,11... | collective-permute-start | bytes 7077896 | tf_op jit(solution)/shard_map/ppermute | solution.py:134
  90.6 1.7 %copy-start.1 = (bf16[1536,768]{1,0:T(8,128)(2,1)S(1)}, bf16[1536,768]{1,0:T(8,128)(2,1)}, u32[]{:S(2)}) copy-start(bf16[1536,768]{1,0:T(8,128)(2,1)} %all-gather.3.cloned.1.call-done) | copy-start | bytes 7077892
  100.8 25.0 %all-to-all-start.3 = ((bf16[64,2,2304]{2,1,0:T(2,128)(2,1)}), bf16[64,2,2304]{2,1,0:T(2,128)(2,1)S(1)}, u32[]{:S(2)}, u32[]{:S(2)}) async-start(bf16[64,2,2304]{2,1,0:T(2,128)(2,1)} %reshape.33), calls=%async_computation.3 | async-start | bytes 1179648 | tf_op jit(solution)/shard_map/all_to_all | solution.py:137
  130.0 9.3 %collective-permute-start.3 = (bf16[6,8,768]{2,1,0:T(8,128)(2,1)}, bf16[6,8,768]{2,1,0:T(8,128)(2,1)S(1)}, u32[]{:S(2)}, u32[]{:S(2)}) collective-permute-start(bf16[6,8,768]{2,1,0:T(8,128)(2,1)} %get-tuple-element.14), channel_id=1, source_target_pairs={{0,64},{64,0},{1,65},{65,1},{2,66},{66,2},{3,67},{67,3},{4,68},{68... | collective-permute-start | bytes 221192 | tf_op jit(solution)/shard_map/ppermute | solution.py:139
Sparse Core Ops, SparseCore 0:
  41.8 33.8 all-gather.2

commit v8 on v7

v8 whole, which is shorter than its diff:
```python
import jax
import jax.numpy as jnp
from jax import lax
from jax.experimental import pallas as pl
from jax.experimental.pallas import tpu as pltpu
from jax.sharding import Mesh, PartitionSpec as P

MEM = ("x", "zh")
COL = ("zl", "y", "c")
SWAP = [(0, 1), (1, 0)]
F32, BF16 = jnp.float32, jnp.bfloat16


VMEM = pl.BlockSpec(memory_space=pltpu.VMEM)
SMEM = pl.BlockSpec(memory_space=pltpu.SMEM)
ANY = pl.BlockSpec(memory_space=pl.ANY)
HBM = pl.BlockSpec(memory_space=pltpu.MemorySpace.HBM)


def rows_kernel(tiles, out):
    for part in range(16):
        rows = [tiles[4 * part + n, :6, :].astype(F32) for n in range(4)]
        out[pl.ds(24 * part, 24), :] = jnp.concatenate(rows, axis=0).astype(BF16)


def join_rows(tiles):
    return pl.pallas_call(
        rows_kernel,
        out_shape=jax.ShapeDtypeStruct((384, 384), BF16),
        in_specs=[VMEM],
        out_specs=VMEM,
        cost_estimate=pl.CostEstimate(flops=10**6, bytes_accessed=6 * 10**5, transcendentals=0),
    )(tiles)


def filter_kernel(place, scale, member, field, *rest):
    rows, mine, others = rest[:4], rest[4:8], rest[8:12]
    out, lon, lat, mid, lon_sems, lat_sems = rest[12:]
    x, core = place[0], place[1]
    lon_copies, lat_copies = [], []
    for d in range(4):
        copy = pltpu.make_async_copy(rows[d], lat.at[lax.rem(x + 4 - d, 4)], lat_sems.at[d])
        copy.start()
        lat_copies.append(copy)
    for m, (part, half) in enumerate(((mine, core), (others, 1 - core))):
        for n in range(4):
            to = pl.ds(pl.multiple_of((2 * n + half) * 96, 32), 96)
            copy = pltpu.make_async_copy(part[n], lon.at[:, to, :], lon_sems.at[m, n])
            copy.start()
            lon_copies.append(copy)
    for copy in lat_copies:
        copy.wait()
    for s in range(3):
        across = jnp.dot(lat[s], field[...], preferred_element_type=F32)
        mid[s] = (scale[s] * member[0] * across).astype(BF16)
    for copy in lon_copies:
        copy.wait()
    total = jnp.zeros(out.shape, F32)
    for s in range(3):
        total += lax.dot_general(
            mid[s], lon[s], (((1,), (1,)), ((), ())), preferred_element_type=F32
        )
    out[...] = total.astype(BF16)


def filter_pair(place, scale, member, field, rows, mine, others):
    return pl.pallas_call(
        filter_kernel,
        out_shape=jax.ShapeDtypeStruct((384, 768), BF16),
        in_specs=[SMEM, SMEM, SMEM, VMEM] + [ANY] * 12,
        out_specs=VMEM,
        scratch_shapes=[
            pltpu.VMEM((3, 768, 768), BF16),
            pltpu.VMEM((4, 384, 384), BF16),
            pltpu.VMEM((3, 384, 768), BF16),
            pltpu.SemaphoreType.DMA((2, 4)),
            pltpu.SemaphoreType.DMA((4,)),
        ],
        compiler_params=pltpu.CompilerParams(vmem_limit_bytes=40 * 2**20),
        cost_estimate=pl.CostEstimate(flops=2 * 10**9, bytes_accessed=5 * 10**6, transcendentals=0),
    )(place, scale, member, field, *rows, *mine, *others)


def final_kernel(side, own, back, keep, send):
    for out, h in ((keep, side[0]), (send, 1 - side[0])):
        for r in range(6):
            total = jnp.zeros((8, 768), F32)
            for x in range(4):
                parts = [
                    back[x, 4 * h + l // 2, l % 2, r, :].astype(F32).reshape(1, 768) for l in range(8)
                ]
                total += own[x, r, h].astype(F32) * jnp.concatenate(parts, axis=0)
            out[r] = total.astype(out.dtype)


def final_sum(side, own, back):
    return pl.pallas_call(
        final_kernel,
        out_shape=(jax.ShapeDtypeStruct((6, 8, 768), F32), jax.ShapeDtypeStruct((6, 8, 768), BF16)),
        in_specs=[SMEM, VMEM, VMEM],
        out_specs=(VMEM, VMEM),
        cost_estimate=pl.CostEstimate(flops=10**6, bytes_accessed=2 * 10**6, transcendentals=0),
    )(side, own, back)


def on_device(perturbations, gradient, member_weights, scale_weights, lon_filter, lat_filter):
    x, side, core = lax.axis_index("x"), lax.axis_index("zh"), lax.axis_index("c")
    block = lax.ppermute(lon_filter, ("zh", "c"), [(0, 0), (1, 2), (2, 1), (3, 3)])
    rows = lax.dynamic_index_in_dim(lat_filter, jnp.minimum(x, 2), 0, False)
    tiles = jnp.broadcast_to(jnp.pad(rows, ((0, 2), (0, 0)))[None], (64, 8, 384))
    rows = join_rows(lax.all_to_all(tiles, COL, split_axis=0, concat_axis=0, tiled=True))
    rows = [rows] + [
        lax.ppermute(rows, "x", [(i, (i + d) % 4) for i in range(4)]) for d in (1, 2, 3)
    ]

    own = perturbations[0].transpose(1, 0, 2).reshape(6, 4, 2, 8, 768).transpose(1, 0, 2, 3, 4)
    own = lax.all_to_all(own, "x", split_axis=0, concat_axis=0, tiled=True)
    turn = [(4 * a + b, 4 * b + a) for a in range(4) for b in range(4)]
    weight = lax.ppermute(member_weights, ("x", "zl"), turn)
    own, weight, block = lax.optimization_barrier((own, weight, block))
    mine = lax.all_gather(block, "x", axis=0)
    level = lax.dynamic_slice_in_dim(gradient.transpose(1, 0, 2), x * 16, 16, axis=1)
    schur = (own.astype(F32) * level.reshape(1, 6, 2, 8, 768)).astype(BF16)
    schur = schur.transpose(0, 2, 3, 1, 4).reshape(64, 2, 2304)
    field = lax.all_to_all(schur, COL, split_axis=0, concat_axis=0, tiled=True).reshape(384, 768)
    mine = lax.optimization_barrier((mine, schur))[0]
    mine = [mine[n] for n in range(4)]
    others = [lax.ppermute(part, "c", SWAP) for part in mine]
    place = jnp.stack([x, core]).astype(jnp.int32)
    filtered = filter_pair(place, scale_weights, weight, field, rows, mine, others)
    back = lax.all_to_all(filtered.reshape(64, 2, 2304), COL, split_axis=0, concat_axis=0, tiled=True)
    keep, send = final_sum(side.reshape(1).astype(jnp.int32), own, back.reshape(4, 8, 2, 6, 768))
    total = keep + lax.ppermute(send, "zh", SWAP).astype(F32)
    return total.transpose(1, 0, 2)


def solution(mesh):
    fine = Mesh(mesh.devices.reshape(4, 2, 4, 8, 2), MEM + COL)
    placed = (
        P(MEM, None, COL, None),
        P(None, COL, None),
        P(MEM),
        P(),
        P(None, MEM, None),
        P(None, COL, None),
    )
    return jax.shard_map(
        on_device, mesh=fine, in_specs=placed, out_specs=P(MEM, COL, None), check_vma=False
    )
```

time: 149 us -> 164 us (1.10)
  blocking collectives: 47.5 us -> 0 us
  starting transfers between devices: 32.4 us -> 73.7 us
  waiting for transfers between devices: 32.3 us -> 45.8 us
  local copies, waits for them, and re-layouts: 7.96 us -> 16.1 us
  Pallas kernels: 12.3 us -> 10.5 us
    all_to_all x2 -> x0, blocking collectives: 47.5 us -> none  [the longest x1 28 us: on_device(): lax.all_to_all(schur, COL, split_axis=0, concat_axis=0, tiled=True)]
    all_to_all x1 -> x3, starting transfers between devices: 5.56 us -> 29.6 us  [the longest x1 12.2 us: on_device(): lax.all_to_all(tiles, COL, split_axis=0, concat_axis=0, tiled=True)]
    ppermute x1 -> x7, starting transfers between devices: 2.54 us -> 20.1 us  [the longest x3 10.7 us: on_device(): lax.ppermute(rows, 'x', [(i, (i + d) % 4) for i in range(4)])]
    all_to_all x1 -> x3, waiting for transfers between devices: 19.4 us -> 32.2 us  [the longest x1 19 us: on_device(): lax.all_to_all(filtered.reshape(64, 2, 2304), COL, split_axis=0, concat_a...]
    squeeze x0 -> x1, local copies, waits for them, and re-layouts: none -> 2.33 us  [on_device(): mine = [mine[n] for n in range(4)]]
    reshape x1, local copies, waits for them, and re-layouts: 0.37 us -> 2.12 us  [on_device(): lax.all_to_all(schur, COL, split_axis=0, concat_axis=0, tiled=True)]
    pallas_call x1, Pallas kernels: 7.45 us -> 5.8 us  [filter_pair(): pl.pallas_call(filter_kernel, out_shape=jax.ShapeDtypeStruct((384, 768),...]
    unnamed x12 -> x24, local copies, waits for them, and re-layouts: 2.95 us -> 4.36 us
  transfers between devices with their start and end apart: 7 -> 15, of which waited for: 4 -> 5; matrix products, arithmetic and copies ran while one was open for 2% -> 6% of each run, Pallas kernels for 0% -> 1%
where the time goes in v8:
time: 164 us; the launch traced here: 162 us
  starting transfers between devices  73.7 us (45%)
  waiting for transfers between devices  45.8 us (28%)
  local copies, waits for them, and re-layouts  16.1 us (10%)
  between operations  13.7 us (8%)
  Pallas kernels  10.5 us (6%)
  other arithmetic  1.77 us (1%)
    all_to_all x1, waiting for transfers between devices, on_device(): lax.all_to_all(filtered.reshape(64, 2, 2304), COL, split_axis=0, concat_a...  19 us
    all_to_all x1, waiting for transfers between devices, on_device(): lax.all_to_all(tiles, COL, split_axis=0, concat_axis=0, tiled=True)  13.2 us
    all_to_all x1, starting transfers between devices, on_device(): lax.all_to_all(tiles, COL, split_axis=0, concat_axis=0, tiled=True)  12.2 us
    ppermute x1, starting transfers between devices, on_device(): lax.ppermute(lon_filter, ('zh', 'c'), [(0, 0), (1, 2), (2, 1), (3, 3)])  12.1 us
    all_to_all x1, starting transfers between devices, on_device(): lax.all_to_all(filtered.reshape(64, 2, 2304), COL, split_axis=0, concat_a...  11.6 us
    ppermute x3, starting transfers between devices, on_device(): lax.ppermute(rows, 'x', [(i, (i + d) % 4) for i in range(4)])  10.7 us
    ppermute x4, starting transfers between devices, on_device(): others = [lax.ppermute(part, 'c', SWAP) for part in mine]  9.35 us
    ppermute x1, starting transfers between devices, on_device(): total = keep + lax.ppermute(send, 'zh', SWAP).astype(F32)  6.03 us
  transfers between devices with their start and end apart: 15, of which 5 were waited for; matrix products, arithmetic and copies ran while one was open for 6% of the time, Pallas kernels for 1%

profile of v8, /device:TPU:1, one launch (start us, length us, event | category | flops | bytes accessed | tf_op | source)
XLA Modules:
  0.0 161.6 jit_solution(2502165375822156457)
XLA Ops:
  6.5 12.1 %collective-permute-start.1 = (bf16[3,96,768]{2,1,0:T(8,128)(2,1)}, bf16[3,96,768]{2,1,0:T(8,128)(2,1)S(1)}, u32[]{:S(2)}, u32[]{:S(2)}) collective-permute-start(bf16[3,96,768]{2,1,0:T(8,128)(2,1)} %param.10), channel_id=1, source_target_pairs={{0,0},{1,64},{64,1},{65,65},{2,2},{3,66},{66,3},{67,67},{4,4},{5,6... | collective-permute-start | bytes 1327112 | tf_op jit(solution)/shard_map/ppermute | solution.py:108
  18.7 1.9 %copy.12 = bf16[6,4,2,8,768]{4,3,2,0,1:T(8,128)(2,1)} copy(bf16[6,4,2,8,768]{4,3,2,1,0:T(8,128)(2,1)} %bitcast.31) | data formatting | bytes 1179648 | tf_op jit(solution)/shard_map/reshape | solution.py:116
  20.6 4.0 %all-to-all-start = ((bf16[4,6,2,8,768]{4,3,2,1,0:T(8,128)(2,1)}), bf16[4,6,2,8,768]{4,3,2,1,0:T(8,128)(2,1)S(1)}, u32[]{:S(2)}, u32[]{:S(2)}) async-start(bf16[4,6,2,8,768]{4,3,2,1,0:T(8,128)(2,1)} %bitcast.29), calls=%async_computation | async-start | bytes 1179648 | tf_op jit(solution)/shard_map/all_to_all | solution.py:117
  24.6 1.8 %collective-permute-start = (f32[1]{0:T(128)}, f32[1]{0:T(128)}, u32[]{:S(2)}, u32[]{:S(2)}) collective-permute-start(f32[1]{0:T(128)} %param.8), channel_id=1, source_target_pairs={{0,0},{16,128},{32,256},{48,384},{128,16},{144,144},{160,272},{176... | collective-permute-start | bytes 20 | tf_op jit(solution)/shard_map/ppermute | solution.py:119
  26.5 5.5 %all-to-all-done.own = bf16[4,6,2,8,768]{4,3,2,1,0:T(8,128)(2,1)S(1)} async-done(((bf16[4,6,2,8,768]{4,3,2,1,0:T(8,128)(2,1)}), bf16[4,6,2,8,768]{4,3,2,1,0:T(8,128)(2,1)S(1)}, u32[]{:S(2)}, u32[]{:S(2)}) %all-to-all-start) | async-done | bytes 589856 | tf_op jit(solution)/shard_map/all_to_all | solution.py:117
  33.5 12.2 %all-to-all-start.2 = ((bf16[64,8,384]{2,1,0:T(8,128)(2,1)}), bf16[64,8,384]{2,1,0:T(8,128)(2,1)S(1)}, u32[]{:S(2)}, u32[]{:S(2)}) async-start(bf16[64,8,384]{2,1,0:T(8,128)(2,1)} %broadcast_in_dim.2), calls=%async_computation.2 | async-start | bytes 786432 | tf_op jit(solution)/shard_map/all_to_all | solution.py:111
  47.3 13.2 %all-to-all-done.2.tiles = bf16[64,8,384]{2,1,0:T(8,128)(2,1)S(1)} async-done(((bf16[64,8,384]{2,1,0:T(8,128)(2,1)}), bf16[64,8,384]{2,1,0:T(8,128)(2,1)S(1)}, u32[]{:S(2)}, u32[]{:S(2)}) %all-to-all-start.2) | async-done | bytes 393248 | tf_op jit(solution)/shard_map/all_to_all | solution.py:111
  60.5 5.8 %all-to-all-start.1 = ((bf16[64,2,2304]{2,1,0:T(2,128)(2,1)}), bf16[64,2,2304]{2,1,0:T(2,128)(2,1)}, u32[]{:S(2)}, u32[]{:S(2)}) async-start(bf16[64,2,2304]{2,1,0:T(2,128)(2,1)} %reshape.23), calls=%async_computation.1 | async-start | bytes 1179648 | tf_op jit(solution)/shard_map/all_to_all | solution.py:125
  68.2 2.1 %collective-permute-start.4 = (bf16[384,384]{1,0:T(8,128)(2,1)}, bf16[384,384]{1,0:T(8,128)(2,1)S(1)}, u32[]{:S(2)}, u32[]{:S(2)}) collective-permute-start(bf16[384,384]{1,0:T(8,128)(2,1)} %shard_map.64.rest_0_), channel_id=1, source_target_pairs={{0,384},{128,0},{256,128},{384,256},{1,385},{129,1},{257,129},{385... | collective-permute-start | bytes 884744 | tf_op jit(solution)/shard_map/ppermute | solution.py:113
  70.4 4.3 %collective-permute-start.3 = (bf16[384,384]{1,0:T(8,128)(2,1)}, bf16[384,384]{1,0:T(8,128)(2,1)S(1)}, u32[]{:S(2)}, u32[]{:S(2)}) collective-permute-start(bf16[384,384]{1,0:T(8,128)(2,1)} %shard_map.64.rest_0_), channel_id=1, source_target_pairs={{0,256},{128,384},{256,0},{384,128},{1,257},{129,385},{257,1},{385... | collective-permute-start | bytes 884744 | tf_op jit(solution)/shard_map/ppermute | solution.py:113
  74.7 2.3 %slice_bitcast_fusion = (bf16[3,96,768]{2,1,0:T(8,128)(2,1)S(1)}, bf16[3,96,768]{2,1,0:T(8,128)(2,1)S(1)}, bf16[3,96,768]{2,1,0:T(8,128)(2,1)S(1)}, bf16[3,96,768]{2,1,0:T(8,128)(2,1)}) fusion(bf16[4,3,96,768]{3,2,1,0:T(8,128)(2,1)} %bitcast.30), kind=kLoop, calls=%fused_computation.3 | loop fusion | bytes 3538944 | tf_op jit(solution)/shard_map/squeeze | solution.py:127
  77.0 3.1 %collective-permute-start.8 = (bf16[3,96,768]{2,1,0:T(8,128)(2,1)S(1)}, bf16[3,96,768]{2,1,0:T(8,128)(2,1)}, u32[]{:S(2)}, u32[]{:S(2)}) collective-permute-start(bf16[3,96,768]{2,1,0:T(8,128)(2,1)S(1)} %get-tuple-element.17.rest_7_), channel_id=1, source_target_pairs={{0,1},{1,0},{2,3},{3,2},{4,5},{5,4},{6,7},{7,6},{8,9},{9,8},{10,11... | collective-permute-start | bytes 1327112 | tf_op jit(solution)/shard_map/ppermute | solution.py:128
  80.2 1.9 %collective-permute-start.7 = (bf16[3,96,768]{2,1,0:T(8,128)(2,1)S(1)}, bf16[3,96,768]{2,1,0:T(8,128)(2,1)}, u32[]{:S(2)}, u32[]{:S(2)}) collective-permute-start(bf16[3,96,768]{2,1,0:T(8,128)(2,1)S(1)} %get-tuple-element.18.rest_6_), channel_id=1, source_target_pairs={{0,1},{1,0},{2,3},{3,2},{4,5},{5,4},{6,7},{7,6},{8,9},{9,8},{10,11... | collective-permute-start | bytes 1327112 | tf_op jit(solution)/shard_map/ppermute | solution.py:128
  82.1 2.4 %collective-permute-start.6 = (bf16[3,96,768]{2,1,0:T(8,128)(2,1)S(1)}, bf16[3,96,768]{2,1,0:T(8,128)(2,1)}, u32[]{:S(2)}, u32[]{:S(2)}) collective-permute-start(bf16[3,96,768]{2,1,0:T(8,128)(2,1)S(1)} %get-tuple-element.19.rest_5_), channel_id=1, source_target_pairs={{0,1},{1,0},{2,3},{3,2},{4,5},{5,4},{6,7},{7,6},{8,9},{9,8},{10,11... | collective-permute-start | bytes 1327112 | tf_op jit(solution)/shard_map/ppermute | solution.py:128
  85.2 1.9 %collective-permute-start.5 = (bf16[3,96,768]{2,1,0:T(8,128)(2,1)}, bf16[3,96,768]{2,1,0:T(8,128)(2,1)}, u32[]{:S(2)}, u32[]{:S(2)}) collective-permute-start(bf16[3,96,768]{2,1,0:T(8,128)(2,1)} %get-tuple-element.20.rest_4_), channel_id=1, source_target_pairs={{0,1},{1,0},{2,3},{3,2},{4,5},{5,4},{6,7},{7,6},{8,9},{9,8},{10,11... | collective-permute-start | bytes 1327112 | tf_op jit(solution)/shard_map/ppermute | solution.py:128
  87.9 4.3 %collective-permute-start.2 = (bf16[384,384]{1,0:T(8,128)(2,1)S(1)}, bf16[384,384]{1,0:T(8,128)(2,1)}, u32[]{:S(2)}, u32[]{:S(2)}) collective-permute-start(bf16[384,384]{1,0:T(8,128)(2,1)S(1)} %copy-done.3), channel_id=1, source_target_pairs={{0,128},{128,256},{256,384},{384,0},{1,129},{129,257},{257,385},{3... | collective-permute-start | bytes 884744 | tf_op jit(solution)/shard_map/ppermute | solution.py:113
  92.2 2.1 %reshape.24.field = bf16[384,768]{1,0:T(8,128)(2,1)S(1)} reshape(bf16[64,2,2304]{2,1,0:T(2,128)(2,1)} %all-to-all-done.1) | data formatting | bytes 1179648 | tf_op jit(solution)/shard_map/reshape | solution.py:125
  94.3 4.8 %collective-permute-done.2.rest_1_ = bf16[384,384]{1,0:T(8,128)(2,1)} collective-permute-done((bf16[384,384]{1,0:T(8,128)(2,1)S(1)}, bf16[384,384]{1,0:T(8,128)(2,1)}, u32[]{:S(2)}, u32[]{:S(2)}) %collective-permute-start.2) | collective-permute-done | bytes 294944 | tf_op jit(solution)/shard_map/ppermute | solution.py:113
  102.1 5.8 %shard_map.65 = bf16[384,768]{1,0:T(8,128)(2,1)S(1)} custom-call(s32[2]{0:T(128)S(1)} %pad_add_fusion.place, f32[3]{0:T(128)S(1)} %copy-done.8, f32[1]{0:T(128)} %collective-permute-done.member, bf16[384,768]{1,0:T(8,128)(2,1)S(1)} %reshape.24.field, bf16[384,384]{1,0:T(8,128)(2,1)S(1)} %copy-done.3, bf16[384,384]{1,0:T(8,128)(2,1)} %collective-permute-done.2.rest_1_, ...), custom_call_target="tpu_custom_call" | custom-call | flops 2000000000 | bytes 5000000 | tf_op jit(solution)/shard_map/pallas_call | solution.py:67
  109.1 11.6 %all-to-all-start.3 = ((bf16[64,2,2304]{2,1,0:T(2,128)(2,1)}), bf16[64,2,2304]{2,1,0:T(2,128)(2,1)S(1)}, u32[]{:S(2)}, u32[]{:S(2)}) async-start(bf16[64,2,2304]{2,1,0:T(2,128)(2,1)} %reshape.25), calls=%async_computation.3 | async-start | bytes 1179648 | tf_op jit(solution)/shard_map/all_to_all | solution.py:131
  120.6 19.0 %all-to-all-done.3 = bf16[64,2,2304]{2,1,0:T(2,128)(2,1)S(1)} async-done(((bf16[64,2,2304]{2,1,0:T(2,128)(2,1)}), bf16[64,2,2304]{2,1,0:T(2,128)(2,1)S(1)}, u32[]{:S(2)}, u32[]{:S(2)}) %all-to-all-start.3) | async-done | bytes 589856 | tf_op jit(solution)/shard_map/all_to_all | solution.py:131
  140.9 2.9 %shard_map.66 = (f32[6,8,768]{2,1,0:T(8,128)}, bf16[6,8,768]{2,1,0:T(8,128)(2,1)}) custom-call(s32[1]{0:T(128)} %bitcast.side, bf16[4,6,2,8,768]{4,3,2,1,0:T(8,128)(2,1)} %copy-done.9, bf16[4,8,2,6,768]{4,3,2,1,0:T(8,128)(2,1)} %reshape.26.back), custom_call_target="tpu_custom_call" | custom-call | flops 1000000 | bytes 2000000 | tf_op jit(solution)/shard_map/pallas_call | solution.py:97
  143.8 6.0 %collective-permute-start.9 = (bf16[6,8,768]{2,1,0:T(8,128)(2,1)}, bf16[6,8,768]{2,1,0:T(8,128)(2,1)S(1)}, u32[]{:S(2)}, u32[]{:S(2)}) collective-permute-start(bf16[6,8,768]{2,1,0:T(8,128)(2,1)} %get-tuple-element.16), channel_id=1, source_target_pairs={{0,64},{64,0},{1,65},{65,1},{2,66},{66,2},{3,67},{67,3},{4,68},{68... | collective-permute-start | bytes 221192 | tf_op jit(solution)/shard_map/ppermute | solution.py:133
  149.9 3.3 %collective-permute-done.9 = bf16[6,8,768]{2,1,0:T(8,128)(2,1)S(1)} collective-permute-done((bf16[6,8,768]{2,1,0:T(8,128)(2,1)}, bf16[6,8,768]{2,1,0:T(8,128)(2,1)S(1)}, u32[]{:S(2)}, u32[]{:S(2)}) %collective-permute-start.9) | collective-permute-done | bytes 73760 | tf_op jit(solution)/shard_map/ppermute | solution.py:133
  (48 shorter events, 13.4 us)
Async XLA Ops:
  6.5 39.2 %copy-start = (f32[64,6,768]{2,0,1:T(8,128)S(1)}, f32[64,6,768]{2,0,1:T(8,128)}, u32[]{:S(2)}) copy-start(f32[64,6,768]{2,0,1:T(8,128)} %param.7) | copy-start | bytes 3538948
  6.5 19.9 %collective-permute-start.1 = (bf16[3,96,768]{2,1,0:T(8,128)(2,1)}, bf16[3,96,768]{2,1,0:T(8,128)(2,1)S(1)}, u32[]{:S(2)}, u32[]{:S(2)}) collective-permute-start(bf16[3,96,768]{2,1,0:T(8,128)(2,1)} %param.10), channel_id=1, source_target_pairs={{0,0},{1,64},{64,1},{65,65},{2,2},{3,66},{66,3},{67,67},{4,4},{5,6... | collective-permute-start | bytes 1327112 | tf_op jit(solution)/shard_map/ppermute | solution.py:108
  20.6 11.3 %all-to-all-start = ((bf16[4,6,2,8,768]{4,3,2,1,0:T(8,128)(2,1)}), bf16[4,6,2,8,768]{4,3,2,1,0:T(8,128)(2,1)S(1)}, u32[]{:S(2)}, u32[]{:S(2)}) async-start(bf16[4,6,2,8,768]{4,3,2,1,0:T(8,128)(2,1)} %bitcast.29), calls=%async_computation | async-start | bytes 1179648 | tf_op jit(solution)/shard_map/all_to_all | solution.py:117
  24.6 50.0 %all-gather.3.cloned.1.call-start = ((), (), s32[]{:S(2)}) async-start(), calls=%async_computation.4 | async-start | bytes 2211840 | tf_op jit(solution)/shard_map/all_gather | solution.py:121
  24.6 1.8 %collective-permute-start = (f32[1]{0:T(128)}, f32[1]{0:T(128)}, u32[]{:S(2)}, u32[]{:S(2)}) collective-permute-start(f32[1]{0:T(128)} %param.8), channel_id=1, source_target_pairs={{0,0},{16,128},{32,256},{48,384},{128,16},{144,144},{160,272},{176... | collective-permute-start | bytes 20 | tf_op jit(solution)/shard_map/ppermute | solution.py:119
  26.4 5.5 %copy-start.11 = (bf16[3,96,768]{2,1,0:T(8,128)(2,1)}, bf16[3,96,768]{2,1,0:T(8,128)(2,1)S(1)}, u32[]{:S(2)}) copy-start(bf16[3,96,768]{2,1,0:T(8,128)(2,1)S(1)} %collective-permute-done.1) | copy-start | bytes 1327108
  31.9 14.0 %copy-start.9 = (bf16[4,6,2,8,768]{4,3,2,1,0:T(8,128)(2,1)}, bf16[4,6,2,8,768]{4,3,2,1,0:T(8,128)(2,1)S(1)}, u32[]{:S(2)}) copy-start(bf16[4,6,2,8,768]{4,3,2,1,0:T(8,128)(2,1)S(1)} %all-to-all-done.own) | copy-start | bytes 1769476
  33.5 27.1 %all-to-all-start.2 = ((bf16[64,8,384]{2,1,0:T(8,128)(2,1)}), bf16[64,8,384]{2,1,0:T(8,128)(2,1)S(1)}, u32[]{:S(2)}, u32[]{:S(2)}) async-start(bf16[64,8,384]{2,1,0:T(8,128)(2,1)} %broadcast_in_dim.2), calls=%async_computation.2 | async-start | bytes 786432 | tf_op jit(solution)/shard_map/all_to_all | solution.py:111
  60.5 5.8 %copy-start.10 = (bf16[64,8,384]{2,1,0:T(8,128)(2,1)}, bf16[64,8,384]{2,1,0:T(8,128)(2,1)S(1)}, u32[]{:S(2)}) copy-start(bf16[64,8,384]{2,1,0:T(8,128)(2,1)S(1)} %all-to-all-done.2.tiles) | copy-start | bytes 1179652
  60.5 31.7 %all-to-all-start.1 = ((bf16[64,2,2304]{2,1,0:T(2,128)(2,1)}), bf16[64,2,2304]{2,1,0:T(2,128)(2,1)}, u32[]{:S(2)}, u32[]{:S(2)}) async-start(bf16[64,2,2304]{2,1,0:T(2,128)(2,1)} %reshape.23), calls=%async_computation.1 | async-start | bytes 1179648 | tf_op jit(solution)/shard_map/all_to_all | solution.py:125
  68.2 16.3 %collective-permute-start.4 = (bf16[384,384]{1,0:T(8,128)(2,1)}, bf16[384,384]{1,0:T(8,128)(2,1)S(1)}, u32[]{:S(2)}, u32[]{:S(2)}) collective-permute-start(bf16[384,384]{1,0:T(8,128)(2,1)} %shard_map.64.rest_0_), channel_id=1, source_target_pairs={{0,384},{128,0},{256,128},{384,256},{1,385},{129,1},{257,129},{385... | collective-permute-start | bytes 884744 | tf_op jit(solution)/shard_map/ppermute | solution.py:113
  70.4 16.8 %collective-permute-start.3 = (bf16[384,384]{1,0:T(8,128)(2,1)}, bf16[384,384]{1,0:T(8,128)(2,1)S(1)}, u32[]{:S(2)}, u32[]{:S(2)}) collective-permute-start(bf16[384,384]{1,0:T(8,128)(2,1)} %shard_map.64.rest_0_), channel_id=1, source_target_pairs={{0,256},{128,384},{256,0},{384,128},{1,257},{129,385},{257,1},{385... | collective-permute-start | bytes 884744 | tf_op jit(solution)/shard_map/ppermute | solution.py:113
  74.7 13.2 %copy-start.3 = (bf16[384,384]{1,0:T(8,128)(2,1)S(1)}, bf16[384,384]{1,0:T(8,128)(2,1)}, u32[]{:S(2)}) copy-start(bf16[384,384]{1,0:T(8,128)(2,1)} %shard_map.64.rest_0_) | copy-start | bytes 884740
  77.0 22.1 %copy-start.1 = (bf16[3,96,768]{2,1,0:T(8,128)(2,1)}, bf16[3,96,768]{2,1,0:T(8,128)(2,1)S(1)}, u32[]{:S(2)}) copy-start(bf16[3,96,768]{2,1,0:T(8,128)(2,1)S(1)} %get-tuple-element.19.rest_5_) | copy-start | bytes 1327108
  77.0 22.1 %copy-start.8 = (f32[3]{0:T(128)S(1)}, f32[3]{0:T(128)}, u32[]{:S(2)}) copy-start(f32[3]{0:T(128)} %scale.1) | copy-start | bytes 40
  77.0 22.1 %collective-permute-start.8 = (bf16[3,96,768]{2,1,0:T(8,128)(2,1)S(1)}, bf16[3,96,768]{2,1,0:T(8,128)(2,1)}, u32[]{:S(2)}, u32[]{:S(2)}) collective-permute-start(bf16[3,96,768]{2,1,0:T(8,128)(2,1)S(1)} %get-tuple-element.17.rest_7_), channel_id=1, source_target_pairs={{0,1},{1,0},{2,3},{3,2},{4,5},{5,4},{6,7},{7,6},{8,9},{9,8},{10,11... | collective-permute-start | bytes 1327112 | tf_op jit(solution)/shard_map/ppermute | solution.py:128
  80.2 19.0 %collective-permute-start.7 = (bf16[3,96,768]{2,1,0:T(8,128)(2,1)S(1)}, bf16[3,96,768]{2,1,0:T(8,128)(2,1)}, u32[]{:S(2)}, u32[]{:S(2)}) collective-permute-start(bf16[3,96,768]{2,1,0:T(8,128)(2,1)S(1)} %get-tuple-element.18.rest_6_), channel_id=1, source_target_pairs={{0,1},{1,0},{2,3},{3,2},{4,5},{5,4},{6,7},{7,6},{8,9},{9,8},{10,11... | collective-permute-start | bytes 1327112 | tf_op jit(solution)/shard_map/ppermute | solution.py:128
  82.1 17.1 %collective-permute-start.6 = (bf16[3,96,768]{2,1,0:T(8,128)(2,1)S(1)}, bf16[3,96,768]{2,1,0:T(8,128)(2,1)}, u32[]{:S(2)}, u32[]{:S(2)}) collective-permute-start(bf16[3,96,768]{2,1,0:T(8,128)(2,1)S(1)} %get-tuple-element.19.rest_5_), channel_id=1, source_target_pairs={{0,1},{1,0},{2,3},{3,2},{4,5},{5,4},{6,7},{7,6},{8,9},{9,8},{10,11... | collective-permute-start | bytes 1327112 | tf_op jit(solution)/shard_map/ppermute | solution.py:128
  85.2 13.9 %collective-permute-start.5 = (bf16[3,96,768]{2,1,0:T(8,128)(2,1)}, bf16[3,96,768]{2,1,0:T(8,128)(2,1)}, u32[]{:S(2)}, u32[]{:S(2)}) collective-permute-start(bf16[3,96,768]{2,1,0:T(8,128)(2,1)} %get-tuple-element.20.rest_4_), channel_id=1, source_target_pairs={{0,1},{1,0},{2,3},{3,2},{4,5},{5,4},{6,7},{7,6},{8,9},{9,8},{10,11... | collective-permute-start | bytes 1327112 | tf_op jit(solution)/shard_map/ppermute | solution.py:128
  87.9 11.3 %collective-permute-start.2 = (bf16[384,384]{1,0:T(8,128)(2,1)S(1)}, bf16[384,384]{1,0:T(8,128)(2,1)}, u32[]{:S(2)}, u32[]{:S(2)}) collective-permute-start(bf16[384,384]{1,0:T(8,128)(2,1)S(1)} %copy-done.3), channel_id=1, source_target_pairs={{0,128},{128,256},{256,384},{384,0},{1,129},{129,257},{257,385},{3... | collective-permute-start | bytes 884744 | tf_op jit(solution)/shard_map/ppermute | solution.py:113
  99.2 1.0 copy-start.2
  100.2 1.0 copy-start.5
  109.1 30.6 %all-to-all-start.3 = ((bf16[64,2,2304]{2,1,0:T(2,128)(2,1)}), bf16[64,2,2304]{2,1,0:T(2,128)(2,1)S(1)}, u32[]{:S(2)}, u32[]{:S(2)}) async-start(bf16[64,2,2304]{2,1,0:T(2,128)(2,1)} %reshape.25), calls=%async_computation.3 | async-start | bytes 1179648 | tf_op jit(solution)/shard_map/all_to_all | solution.py:131
  143.8 9.3 %collective-permute-start.9 = (bf16[6,8,768]{2,1,0:T(8,128)(2,1)}, bf16[6,8,768]{2,1,0:T(8,128)(2,1)S(1)}, u32[]{:S(2)}, u32[]{:S(2)}) collective-permute-start(bf16[6,8,768]{2,1,0:T(8,128)(2,1)} %get-tuple-element.16), channel_id=1, source_target_pairs={{0,64},{64,0},{1,65},{65,1},{2,66},{66,2},{3,67},{67,3},{4,68},{68... | collective-permute-start | bytes 221192 | tf_op jit(solution)/shard_map/ppermute | solution.py:133
  (3 other events, 2.4 us)
Sparse Core Ops, SparseCore 0:
  32.1 32.8 all-gather.2

commit v9 on v7

--- a/solution.py
+++ b/solution.py
@@ -32,6 +32,7 @@
         out_shape=jax.ShapeDtypeStruct((384, 768), BF16),
         in_specs=[VMEM, VMEM],
         out_specs=VMEM,
+        compiler_params=pltpu.CompilerParams(vmem_limit_bytes=16 * 2**20),
         cost_estimate=pl.CostEstimate(flops=10**6, bytes_accessed=2 * 10**6, transcendentals=0),
     )(block, tiles)
 
@@ -53,7 +54,7 @@
             for x in range(4):
                 to = pl.ds(pl.multiple_of((2 * x + half) * 96, 32), 96)
                 copy = pltpu.make_async_copy(
-                    part.at[x, pl.ds(96 * s, 96), :], lon.at[s, to, :], lon_sems.at[m, s, x]
+                    part.at[x, pl.ds(96 * s, 96), :], lon.at[to, pl.ds(768 * s, 768)], lon_sems.at[m, s, x]
                 )
                 copy.start()
                 lon_copies.append(copy)
@@ -61,14 +62,12 @@
         copy.wait()
     for s in range(3):
         across = jnp.dot(lat[s], field[...], preferred_element_type=F32)
-        mid[s] = (scale[s] * member[0] * across).astype(BF16)
+        mid[:, pl.ds(768 * s, 768)] = (scale[s] * member[0] * across).astype(BF16)
     for copy in lon_copies:
         copy.wait()
-    total = jnp.zeros(out.shape, F32)
-    for s in range(3):
-        total += lax.dot_general(
-            mid[s], lon[s], (((1,), (1,)), ((), ())), preferred_element_type=F32
-        )
+    total = lax.dot_general(
+        mid[...], lon[...], (((1,), (1,)), ((), ())), preferred_element_type=F32
+    )
     out[...] = total.astype(BF16)
 
 
@@ -79,9 +78,9 @@
         in_specs=[SMEM, SMEM, SMEM, VMEM, HBM, HBM],
         out_specs=VMEM,
         scratch_shapes=[
-            pltpu.VMEM((3, 768, 768), BF16),
+            pltpu.VMEM((768, 2304), BF16),
             pltpu.VMEM((3, 384, 384), BF16),
-            pltpu.VMEM((3, 384, 768), BF16),
+            pltpu.VMEM((384, 2304), BF16),
             pltpu.SemaphoreType.DMA((2, 3, 4)),
             pltpu.SemaphoreType.DMA((2, 3, 2)),
         ],
@@ -90,31 +89,50 @@
     )(core, scale, member, field, mine, other)
 
 
-def final_kernel(side, own, back, keep, send):
-    for out, h in ((keep, side[0]), (send, 1 - side[0])):
-        for r in range(6):
-            total = jnp.zeros((8, 768), F32)
-            for x in range(4):
-                parts = [
-                    back[l % 2, x, 4 * h + l // 2, r, :].astype(F32).reshape(1, 768) for l in range(8)
-                ]
-                total += own[x, r, h].astype(F32) * jnp.concatenate(parts, axis=0)
-            out[r] = total.astype(out.dtype)
+def member_sum(own, back, h, r):
+    total = jnp.zeros((8, 768), F32)
+    for x in range(4):
+        parts = [back[l % 2, x, 4 * h + l // 2, r, :].astype(F32).reshape(1, 768) for l in range(8)]
+        total += own[x, r, h].astype(F32) * jnp.concatenate(parts, axis=0)
+    return total
+
+
+def send_kernel(side, own, back, out):
+    for r in range(6):
+        out[r] = member_sum(own, back, 1 - side[0], r).astype(out.dtype)
+
+
+def keep_kernel(side, own, back, other, out):
+    for r in range(6):
+        out[r] = member_sum(own, back, side[0], r) + other[r].astype(F32)
 
 
 def final_sum(side, own, back):
+    common = dict(
+        compiler_params=pltpu.CompilerParams(vmem_limit_bytes=16 * 2**20),
+        cost_estimate=pl.CostEstimate(flops=10**6, bytes_accessed=10**6, transcendentals=0),
+    )
+    send = pl.pallas_call(
+        send_kernel,
+        out_shape=jax.ShapeDtypeStruct((6, 8, 768), BF16),
+        in_specs=[SMEM, VMEM, VMEM],
+        out_specs=VMEM,
+        **common,
+    )(side, own, back)
     return pl.pallas_call(
-        final_kernel,
-        out_shape=(jax.ShapeDtypeStruct((6, 8, 768), F32), jax.ShapeDtypeStruct((6, 8, 768), BF16)),
-        in_specs=[SMEM, VMEM, VMEM],
-        out_specs=(VMEM, VMEM),
-        cost_estimate=pl.CostEstimate(flops=10**6, bytes_accessed=2 * 10**6, transcendentals=0),
-    )(side, own, back)
+        keep_kernel,
+        out_shape=jax.ShapeDtypeStruct((6, 8, 768), F32),
+        in_specs=[SMEM, VMEM, VMEM, VMEM],
+        out_specs=VMEM,
+        **common,
+    )(side, own, back, lax.ppermute(send, "zh", SWAP))
 
 
 def on_device(perturbations, gradient, member_weights, scale_weights, lon_filter, lat_filter):
     x, side, core = lax.axis_index("x"), lax.axis_index("zh"), lax.axis_index("c")
-    block = lax.ppermute(lon_filter, ("zh", "c"), [(0, 0), (1, 2), (2, 1), (3, 3)])
+    pairs = [(8 * h + 2 * z + h, 8 * h + 2 * z + h) for h in range(2) for z in range(4)]
+    pairs += [(8 * h + 2 * z + 1 - h, 8 * (1 - h) + 2 * (3 - z) + h) for h in range(2) for z in range(4)]
+    block = lax.ppermute(lon_filter, ("zh", "zl", "c"), pairs)
     rows = lax.dynamic_index_in_dim(lat_filter, jnp.minimum(x, 2), 0, False)
     tiles = jnp.broadcast_to(jnp.pad(rows, ((0, 2), (0, 0)))[None], (32, 8, 384))
     tiles = lax.all_to_all(tiles, ("zl", "y"), split_axis=0, concat_axis=0, tiled=True)
@@ -135,8 +153,7 @@
     core = core.reshape(1).astype(jnp.int32)
     filtered = filter_pair(core, scale_weights, weight, field, mine, other).reshape(64, 2, 2304)
     back = lax.all_to_all(filtered, ("c", "zl", "y"), split_axis=0, concat_axis=0, tiled=True)
-    keep, send = final_sum(side.reshape(1).astype(jnp.int32), own, back.reshape(2, 4, 8, 6, 768))
-    total = keep + lax.ppermute(send, "zh", SWAP).astype(F32)
+    total = final_sum(side.reshape(1).astype(jnp.int32), own, back.reshape(2, 4, 8, 6, 768))
     return total.transpose(1, 0, 2)
 
 

time: 149 us -> 139 us (0.933); the launches traced: 148 us -> 136 us
  blocking collectives: 47.5 us -> 40.7 us
  Pallas kernels: 12.3 us -> 8.71 us
  local copies, waits for them, and re-layouts: 7.96 us -> 5.78 us
  waiting for transfers between devices: 32.3 us -> 33.9 us
  other arithmetic: 1.7 us -> 0.1 us
    all_to_all x1, blocking collectives: 28 us -> 23 us  [on_device(): lax.all_to_all(schur, COL, split_axis=0, concat_axis=0, tiled=True)]
    all_to_all x1, blocking collectives: 19.5 us -> 17.7 us  [on_device(): lax.all_to_all(tiles, ('zl', 'y'), split_axis=0, concat_axis=0, tiled=True)]
    all_to_all x1, starting transfers between devices: 5.56 us -> 7.28 us  [on_device(): lax.all_to_all(filtered, ('c', 'zl', 'y'), split_axis=0, concat_axis=0, t...]
    transpose x1 -> x0, other arithmetic: 1.59 us -> none  [on_device(): return total.transpose(1, 0, 2)]
where the time goes in v9:
time: 139 us; the launch traced here: 136 us
  blocking collectives  40.7 us (29%)
  waiting for transfers between devices  33.9 us (24%)
  starting transfers between devices  33.2 us (24%)
  between operations  13.5 us (10%)
  Pallas kernels  8.71 us (6%)
  local copies, waits for them, and re-layouts  5.78 us (4%)
    all_to_all x1, blocking collectives, on_device(): lax.all_to_all(schur, COL, split_axis=0, concat_axis=0, tiled=True)  23 us
    all_to_all x1, waiting for transfers between devices, on_device(): lax.all_to_all(filtered, ('c', 'zl', 'y'), split_axis=0, concat_axis=0, t...  19.4 us
    all_to_all x1, blocking collectives, on_device(): lax.all_to_all(tiles, ('zl', 'y'), split_axis=0, concat_axis=0, tiled=True)  17.7 us
    ppermute x1, starting transfers between devices, on_device(): block = lax.ppermute(lon_filter, ('zh', 'zl', 'c'), pairs)  12.2 us
    all_to_all x1, starting transfers between devices, on_device(): lax.all_to_all(filtered, ('c', 'zl', 'y'), split_axis=0, concat_axis=0, t...  7.28 us
    all_to_all x1, waiting for transfers between devices, on_device(): own = lax.all_to_all(own, 'x', split_axis=0, concat_axis=0, tiled=True)  6.23 us
    pallas_call x1, Pallas kernels, filter_pair(): pl.pallas_call(filter_kernel, out_shape=jax.ShapeDtypeStruct((384, 768),...  6.19 us
    ppermute x1, starting transfers between devices, final_sum(): lax.ppermute(send, 'zh', SWAP)  5.33 us
  transfers between devices with their start and end apart: 7, of which 4 were waited for; matrix products, arithmetic and copies ran while one was open for 2% of the time, Pallas kernels for 0%

profile of v9, /device:TPU:1, one launch (start us, length us, event | category | flops | bytes accessed | tf_op | source)
XLA Modules:
  0.0 136.0 jit_solution(9432811644604589671)
XLA Ops:
  6.5 12.2 %collective-permute-start.1 = (bf16[3,96,768]{2,1,0:T(8,128)(2,1)}, bf16[3,96,768]{2,1,0:T(8,128)(2,1)S(1)}, u32[]{:S(2)}, u32[]{:S(2)}) collective-permute-start(bf16[3,96,768]{2,1,0:T(8,128)(2,1)} %param.10), channel_id=1, source_target_pairs={{0,0},{16,16},{32,32},{48,48},{65,65},{81,81},{97,97},{113,113},{1... | collective-permute-start | bytes 1327112 | tf_op jit(solution)/shard_map/ppermute | solution.py:135
  18.7 0.7 dynamic-slice_bitcast_fusion.1
  19.5 17.7 %all_to_all.20.tiles = bf16[32,8,384]{2,1,0:T(8,128)(2,1)S(1)} all-to-all(bf16[32,8,384]{2,1,0:T(8,128)(2,1)S(1)} %broadcast_in_dim.2), channel_id=1, replica_groups=mesh['x'=4,'zh'=2,'zl'=4,'y'=8,'c'=2] {'zl','y'}, dimensions={0} | all-to-all | bytes 393216 | tf_op jit(solution)/shard_map/all_to_all | solution.py:138
  37.1 0.9 shard_map.64
  38.1 0.9 copy.10
  38.9 4.0 %all-to-all-start = ((bf16[4,6,2,8,768]{4,3,2,1,0:T(8,128)(2,1)}), bf16[4,6,2,8,768]{4,3,2,1,0:T(8,128)(2,1)S(1)}, u32[]{:S(2)}, u32[]{:S(2)}) async-start(bf16[4,6,2,8,768]{4,3,2,1,0:T(8,128)(2,1)} %bitcast.20), calls=%async_computation | async-start | bytes 1179648 | tf_op jit(solution)/shard_map/all_to_all | solution.py:143
  42.9 1.9 %collective-permute-start = (f32[1]{0:T(128)}, f32[1]{0:T(128)}, u32[]{:S(2)}, u32[]{:S(2)}) collective-permute-start(f32[1]{0:T(128)} %param.8), channel_id=1, source_target_pairs={{0,0},{16,128},{32,256},{48,384},{128,16},{144,144},{160,272},{176... | collective-permute-start | bytes 20 | tf_op jit(solution)/shard_map/ppermute | solution.py:145
  44.9 6.2 %all-to-all-done.own = bf16[4,6,2,8,768]{4,3,2,1,0:T(8,128)(2,1)S(1)} async-done(((bf16[4,6,2,8,768]{4,3,2,1,0:T(8,128)(2,1)}), bf16[4,6,2,8,768]{4,3,2,1,0:T(8,128)(2,1)S(1)}, u32[]{:S(2)}, u32[]{:S(2)}) %all-to-all-start) | async-done | bytes 589856 | tf_op jit(solution)/shard_map/all_to_all | solution.py:143
  51.2 0.2 copy.8
  51.4 0.4 reshape.30
  51.8 23.0 %all_to_all.21 = bf16[64,2,2304]{2,1,0:T(2,128)(2,1)S(1)} all-to-all(bf16[64,2,2304]{2,1,0:T(2,128)(2,1)S(1)} %reshape.30), channel_id=1, replica_groups=mesh['x'=4,'zh'=2,'zl'=4,'y'=8,'c'=2] {'zl','y','c'}, dimensions={0} | all-to-all | bytes 1179648 | tf_op jit(solution)/shard_map/all_to_all | solution.py:150
  74.8 0.4 reshape.31.field
  75.2 2.5 %collective-permute-start.2 = (bf16[4,384,768]{2,1,0:T(8,128)(2,1)}, bf16[4,384,768]{2,1,0:T(8,128)(2,1)}, u32[]{:S(2)}, u32[]{:S(2)}) collective-permute-start(bf16[4,384,768]{2,1,0:T(8,128)(2,1)} %bitcast.22), channel_id=1, source_target_pairs={{0,1},{1,0},{2,3},{3,2},{4,5},{5,4},{6,7},{7,6},{8,9},{9,8},{10,11... | collective-permute-start | bytes 7077896 | tf_op jit(solution)/shard_map/ppermute | solution.py:152
  77.8 4.5 %collective-permute-done.2.other = bf16[4,384,768]{2,1,0:T(8,128)(2,1)} collective-permute-done((bf16[4,384,768]{2,1,0:T(8,128)(2,1)}, bf16[4,384,768]{2,1,0:T(8,128)(2,1)}, u32[]{:S(2)}, u32[]{:S(2)}) %collective-permute-start.2) | collective-permute-done | bytes 2359328 | tf_op jit(solution)/shard_map/ppermute | solution.py:152
  82.3 1.7 %copy-done.1 = bf16[1536,768]{1,0:T(8,128)(2,1)S(1)} copy-done((bf16[1536,768]{1,0:T(8,128)(2,1)S(1)}, bf16[1536,768]{1,0:T(8,128)(2,1)}, u32[]{:S(2)}) %copy-start.1) | copy-done | bytes 2359320
  84.0 6.2 %shard_map.65 = bf16[384,768]{1,0:T(8,128)(2,1)S(1)} custom-call(s32[1]{0:T(128)} %bitcast.5.core, f32[3]{0:T(128)S(1)} %copy-done.2, f32[1]{0:T(128)} %collective-permute-done.member, bf16[384,768]{1,0:T(8,128)(2,1)S(1)} %reshape.31.field, bf16[4,384,768]{2,1,0:T(8,128)(2,1)S(1)} %bitcast.23, bf16[4,384,768]{2,1,0:T(8,128)(2,1)} %collective-permute-done.2.other), custom_call_target="tpu_custom_call" | custom-call | flops 2000000000 | bytes 5000000 | tf_op jit(solution)/shard_map/pallas_call | solution.py:75
  90.1 1.1 reshape.33
  91.3 7.3 %all-to-all-start.3 = ((bf16[64,2,2304]{2,1,0:T(2,128)(2,1)}), bf16[64,2,2304]{2,1,0:T(2,128)(2,1)S(1)}, u32[]{:S(2)}, u32[]{:S(2)}) async-start(bf16[64,2,2304]{2,1,0:T(2,128)(2,1)} %reshape.33), calls=%async_computation.3 | async-start | bytes 1179648 | tf_op jit(solution)/shard_map/all_to_all | solution.py:155
  98.6 19.4 %all-to-all-done.3 = bf16[64,2,2304]{2,1,0:T(2,128)(2,1)S(1)} async-done(((bf16[64,2,2304]{2,1,0:T(2,128)(2,1)}), bf16[64,2,2304]{2,1,0:T(2,128)(2,1)S(1)}, u32[]{:S(2)}, u32[]{:S(2)}) %all-to-all-start.3) | async-done | bytes 589856 | tf_op jit(solution)/shard_map/all_to_all | solution.py:155
  118.0 0.4 reshape.34.back
  118.4 0.5 shard_map.66
  118.9 5.3 %collective-permute-start.3 = (bf16[6,8,768]{2,1,0:T(8,128)(2,1)S(1)}, bf16[6,8,768]{2,1,0:T(8,128)(2,1)S(1)}, u32[]{:S(2)}, u32[]{:S(2)}) collective-permute-start(bf16[6,8,768]{2,1,0:T(8,128)(2,1)S(1)} %shard_map.66), channel_id=1, source_target_pairs={{0,64},{64,0},{1,65},{65,1},{2,66},{66,2},{3,67},{67,3},{4,68},{68... | collective-permute-start | bytes 221192 | tf_op jit(solution)/shard_map/ppermute | solution.py:128
  124.2 3.8 %collective-permute-done.3.other = bf16[6,8,768]{2,1,0:T(8,128)(2,1)S(1)} collective-permute-done((bf16[6,8,768]{2,1,0:T(8,128)(2,1)S(1)}, bf16[6,8,768]{2,1,0:T(8,128)(2,1)S(1)}, u32[]{:S(2)}, u32[]{:S(2)}) %collective-permute-start.3) | collective-permute-done | bytes 73760 | tf_op jit(solution)/shard_map/ppermute | solution.py:128
  128.0 1.1 shard_map.67
  (16 shorter events, 0.2 us)
Async XLA Ops:
  6.5 38.3 %copy-start = (f32[64,6,768]{2,0,1:T(8,128)S(1)}, f32[64,6,768]{2,0,1:T(8,128)}, u32[]{:S(2)}) copy-start(f32[64,6,768]{2,0,1:T(8,128)} %param.7) | copy-start | bytes 3538948
  6.5 68.7 %all-gather.3.cloned.1.call-start = ((), (), s32[]{:S(2)}) async-start(), calls=%async_computation.4 | async-start | bytes 2949120 | tf_op jit(solution)/shard_map/all_gather | solution.py:140
  6.5 30.6 %collective-permute-start.1 = (bf16[3,96,768]{2,1,0:T(8,128)(2,1)}, bf16[3,96,768]{2,1,0:T(8,128)(2,1)S(1)}, u32[]{:S(2)}, u32[]{:S(2)}) collective-permute-start(bf16[3,96,768]{2,1,0:T(8,128)(2,1)} %param.10), channel_id=1, source_target_pairs={{0,0},{16,16},{32,32},{48,48},{65,65},{81,81},{97,97},{113,113},{1... | collective-permute-start | bytes 1327112 | tf_op jit(solution)/shard_map/ppermute | solution.py:135
  19.4 18.6 %copy-start.3 = (bf16[1,64,6,768]{3,1,2,0:T(8,128)(2,1)S(1)}, bf16[1,64,6,768]{3,1,2,0:T(8,128)(2,1)}, u32[]{:S(2)}) copy-start(bf16[1,64,6,768]{3,1,2,0:T(8,128)(2,1)} %param.6) | copy-start | bytes 1769476
  38.9 12.2 %all-to-all-start = ((bf16[4,6,2,8,768]{4,3,2,1,0:T(8,128)(2,1)}), bf16[4,6,2,8,768]{4,3,2,1,0:T(8,128)(2,1)S(1)}, u32[]{:S(2)}, u32[]{:S(2)}) async-start(bf16[4,6,2,8,768]{4,3,2,1,0:T(8,128)(2,1)} %bitcast.20), calls=%async_computation | async-start | bytes 1179648 | tf_op jit(solution)/shard_map/all_to_all | solution.py:143
  42.9 1.9 %collective-permute-start = (f32[1]{0:T(128)}, f32[1]{0:T(128)}, u32[]{:S(2)}, u32[]{:S(2)}) collective-permute-start(f32[1]{0:T(128)} %param.8), channel_id=1, source_target_pairs={{0,0},{16,128},{32,256},{48,384},{128,16},{144,144},{160,272},{176... | collective-permute-start | bytes 20 | tf_op jit(solution)/shard_map/ppermute | solution.py:145
  51.8 30.5 %copy-start.2 = (f32[3]{0:T(128)S(1)}, f32[3]{0:T(128)}, u32[]{:S(2)}) copy-start(f32[3]{0:T(128)} %scale.1) | copy-start | bytes 40
  75.2 7.0 %collective-permute-start.2 = (bf16[4,384,768]{2,1,0:T(8,128)(2,1)}, bf16[4,384,768]{2,1,0:T(8,128)(2,1)}, u32[]{:S(2)}, u32[]{:S(2)}) collective-permute-start(bf16[4,384,768]{2,1,0:T(8,128)(2,1)} %bitcast.22), channel_id=1, source_target_pairs={{0,1},{1,0},{2,3},{3,2},{4,5},{5,4},{6,7},{7,6},{8,9},{9,8},{10,11... | collective-permute-start | bytes 7077896 | tf_op jit(solution)/shard_map/ppermute | solution.py:152
  82.3 1.7 %copy-start.1 = (bf16[1536,768]{1,0:T(8,128)(2,1)S(1)}, bf16[1536,768]{1,0:T(8,128)(2,1)}, u32[]{:S(2)}) copy-start(bf16[1536,768]{1,0:T(8,128)(2,1)} %all-gather.3.cloned.1.call-done) | copy-start | bytes 7077892
  91.3 26.7 %all-to-all-start.3 = ((bf16[64,2,2304]{2,1,0:T(2,128)(2,1)}), bf16[64,2,2304]{2,1,0:T(2,128)(2,1)S(1)}, u32[]{:S(2)}, u32[]{:S(2)}) async-start(bf16[64,2,2304]{2,1,0:T(2,128)(2,1)} %reshape.33), calls=%async_computation.3 | async-start | bytes 1179648 | tf_op jit(solution)/shard_map/all_to_all | solution.py:155
  118.9 9.1 %collective-permute-start.3 = (bf16[6,8,768]{2,1,0:T(8,128)(2,1)S(1)}, bf16[6,8,768]{2,1,0:T(8,128)(2,1)S(1)}, u32[]{:S(2)}, u32[]{:S(2)}) collective-permute-start(bf16[6,8,768]{2,1,0:T(8,128)(2,1)S(1)} %shard_map.66), channel_id=1, source_target_pairs={{0,64},{64,0},{1,65},{65,1},{2,66},{66,2},{3,67},{67,3},{4,68},{68... | collective-permute-start | bytes 221192 | tf_op jit(solution)/shard_map/ppermute | solution.py:128
Sparse Core Ops, SparseCore 0:
  38.2 33.2 all-gather.2

commit v10 on v9

--- a/solution.py
+++ b/solution.py
@@ -17,8 +17,9 @@
 HBM = pl.BlockSpec(memory_space=pltpu.MemorySpace.HBM)
 
 
-def pack_kernel(block, tiles, out):
-    out[pl.ds(0, 288), :] = block[...]
+def pack_kernel(one, two, three, tiles, out):
+    for s, block in enumerate((one, two, three)):
+        out[pl.ds(96 * s, 96), :] = block[...]
     for half in range(2):
         for part in range(4):
             first = 16 * half + 4 * part
@@ -26,15 +27,15 @@
             out[pl.ds(288 + 24 * part, 24), pl.ds(384 * half, 384)] = jnp.concatenate(rows, axis=0).astype(BF16)
 
 
-def pack(block, tiles):
+def pack(blocks, tiles):
     return pl.pallas_call(
         pack_kernel,
         out_shape=jax.ShapeDtypeStruct((384, 768), BF16),
-        in_specs=[VMEM, VMEM],
+        in_specs=[VMEM] * 4,
         out_specs=VMEM,
         compiler_params=pltpu.CompilerParams(vmem_limit_bytes=16 * 2**20),
         cost_estimate=pl.CostEstimate(flops=10**6, bytes_accessed=2 * 10**6, transcendentals=0),
-    )(block, tiles)
+    )(*blocks, tiles)
 
 
 def filter_kernel(core, scale, member, field, mine, other, out, lon, lat, mid, lon_sems, lat_sems):
@@ -130,30 +131,31 @@
 
 def on_device(perturbations, gradient, member_weights, scale_weights, lon_filter, lat_filter):
     x, side, core = lax.axis_index("x"), lax.axis_index("zh"), lax.axis_index("c")
+    rows = lax.dynamic_index_in_dim(lat_filter, jnp.minimum(x, 2), 0, False)
+    tiles = jnp.broadcast_to(jnp.pad(rows, ((0, 2), (0, 0)))[None], (32, 8, 384))
+    tiles, lon_filter = lax.optimization_barrier((tiles, lon_filter))
     pairs = [(8 * h + 2 * z + h, 8 * h + 2 * z + h) for h in range(2) for z in range(4)]
     pairs += [(8 * h + 2 * z + 1 - h, 8 * (1 - h) + 2 * (3 - z) + h) for h in range(2) for z in range(4)]
-    block = lax.ppermute(lon_filter, ("zh", "zl", "c"), pairs)
-    rows = lax.dynamic_index_in_dim(lat_filter, jnp.minimum(x, 2), 0, False)
-    tiles = jnp.broadcast_to(jnp.pad(rows, ((0, 2), (0, 0)))[None], (32, 8, 384))
+    blocks = [lax.ppermute(lon_filter[s], ("zh", "zl", "c"), pairs) for s in range(3)]
     tiles = lax.all_to_all(tiles, ("zl", "y"), split_axis=0, concat_axis=0, tiled=True)
-    packed = pack(block.reshape(288, 768), tiles)
+    packed = pack(blocks, tiles)
     mine = lax.all_gather(packed, "x", axis=0)
 
     own = perturbations[0].transpose(1, 0, 2).reshape(6, 4, 2, 8, 768).transpose(1, 0, 2, 3, 4)
     own = lax.all_to_all(own, "x", split_axis=0, concat_axis=0, tiled=True)
     turn = [(4 * a + b, 4 * b + a) for a in range(4) for b in range(4)]
     weight = lax.ppermute(member_weights, ("x", "zl"), turn)
-    own, weight = lax.optimization_barrier((own, weight))
+    core, side = core.reshape(1).astype(jnp.int32), side.reshape(1).astype(jnp.int32)
+    own, weight, core, side = lax.optimization_barrier((own, weight, core, side))
     level = lax.dynamic_slice_in_dim(gradient.transpose(1, 0, 2), x * 16, 16, axis=1)
     schur = (own.astype(F32) * level.reshape(1, 6, 2, 8, 768)).astype(BF16)
     schur = schur.transpose(0, 2, 3, 1, 4).reshape(64, 2, 2304)
     field = lax.all_to_all(schur, COL, split_axis=0, concat_axis=0, tiled=True).reshape(384, 768)
     mine = lax.optimization_barrier((mine, field))[0]
     other = lax.ppermute(mine, "c", SWAP)
-    core = core.reshape(1).astype(jnp.int32)
     filtered = filter_pair(core, scale_weights, weight, field, mine, other).reshape(64, 2, 2304)
     back = lax.all_to_all(filtered, ("c", "zl", "y"), split_axis=0, concat_axis=0, tiled=True)
-    total = final_sum(side.reshape(1).astype(jnp.int32), own, back.reshape(2, 4, 8, 6, 768))
+    total = final_sum(side, own, back.reshape(2, 4, 8, 6, 768))
     return total.transpose(1, 0, 2)
 
 

time: 139 us -> 147 us (1.058)
  waiting for transfers between devices: 33.9 us -> 18.7 us
  blocking collectives: 40.7 us -> 53.7 us
  starting transfers between devices: 33.2 us -> 43.9 us
    all_to_all x1, waiting for transfers between devices: 19.4 us -> 0.01 us  [on_device(): lax.all_to_all(tiles, ('zl', 'y'), split_axis=0, concat_axis=0, tiled=True)]
    all_to_all x1, blocking collectives: 17.7 us -> 26.3 us  [on_device(): lax.all_to_all(filtered, ('c', 'zl', 'y'), split_axis=0, concat_axis=0, t...]
    all_to_all x1, starting transfers between devices: 7.28 us -> 13.5 us  [on_device(): lax.all_to_all(tiles, ('zl', 'y'), split_axis=0, concat_axis=0, tiled=True)]
    ppermute x1 -> x3, waiting for transfers between devices: 0.01 us -> 6.09 us  [on_device(): lax.ppermute(lon_filter[s], ('zh', 'zl', 'c'), pairs)]
    all_to_all x1, blocking collectives: 23 us -> 27.4 us  [on_device(): lax.all_to_all(schur, COL, split_axis=0, concat_axis=0, tiled=True)]
    ppermute x1 -> x3, starting transfers between devices: 12.2 us -> 15.9 us  [on_device(): lax.ppermute(lon_filter[s], ('zh', 'zl', 'c'), pairs)]
  transfers between devices with their start and end apart: 7 -> 9, of which waited for: 4 -> 5; matrix products, arithmetic and copies ran while one was open for 2% -> 2% of each run, Pallas kernels for 0% -> 0%
where the time goes in v10:
time: 147 us; the launch traced here: 145 us
  blocking collectives  53.7 us (37%)
  starting transfers between devices  43.9 us (30%)
  waiting for transfers between devices  18.7 us (13%)
  between operations  13.6 us (9%)
  Pallas kernels  8.07 us (5%)
  local copies, waits for them, and re-layouts  6.87 us (5%)
    all_to_all x1, blocking collectives, on_device(): lax.all_to_all(schur, COL, split_axis=0, concat_axis=0, tiled=True)  27.4 us
    all_to_all x1, blocking collectives, on_device(): lax.all_to_all(filtered, ('c', 'zl', 'y'), split_axis=0, concat_axis=0, t...  26.3 us
    ppermute x3, starting transfers between devices, on_device(): lax.ppermute(lon_filter[s], ('zh', 'zl', 'c'), pairs)  15.9 us
    all_to_all x1, starting transfers between devices, on_device(): lax.all_to_all(tiles, ('zl', 'y'), split_axis=0, concat_axis=0, tiled=True)  13.5 us
    ppermute x1, starting transfers between devices, final_sum(): lax.ppermute(send, 'zh', SWAP)  6.28 us
    ppermute x3, waiting for transfers between devices, on_device(): lax.ppermute(lon_filter[s], ('zh', 'zl', 'c'), pairs)  6.09 us
    pallas_call x1, Pallas kernels, filter_pair(): pl.pallas_call(filter_kernel, out_shape=jax.ShapeDtypeStruct((384, 768),...  5.54 us
    all_to_all x1, waiting for transfers between devices, on_device(): own = lax.all_to_all(own, 'x', split_axis=0, concat_axis=0, tiled=True)  5.43 us
  transfers between devices with their start and end apart: 9, of which 5 were waited for; matrix products, arithmetic and copies ran while one was open for 2% of the time, Pallas kernels for 0%

profile of v10, /device:TPU:1, one launch (start us, length us, event | category | flops | bytes accessed | tf_op | source)
XLA Modules:
  0.0 144.9 jit_solution(11523495382234336370)
XLA Ops:
  6.5 0.8 dynamic-slice_bitcast_fusion.1
  7.3 0.7 broadcast_in_dim.2
  8.0 13.5 %all-to-all-start.2 = ((bf16[32,8,384]{2,1,0:T(8,128)(2,1)}), bf16[32,8,384]{2,1,0:T(8,128)(2,1)S(1)}, u32[]{:S(2)}, u32[]{:S(2)}) async-start(bf16[32,8,384]{2,1,0:T(8,128)(2,1)} %broadcast_in_dim.2), calls=%async_computation.2 | async-start | bytes 393216 | tf_op jit(solution)/shard_map/all_to_all | solution.py:140
  21.6 1.1 slice_bitcast_fusion
  22.7 9.2 %collective-permute-start.3 = (bf16[96,768]{1,0:T(8,128)(2,1)S(1)}, bf16[96,768]{1,0:T(8,128)(2,1)S(1)}, u32[]{:S(2)}, u32[]{:S(2)}) collective-permute-start(bf16[96,768]{1,0:T(8,128)(2,1)S(1)} %get-tuple-element.19), channel_id=1, source_target_pairs={{0,0},{16,16},{32,32},{48,48},{65,65},{81,81},{97,97},{113,113},{1... | collective-permute-start | bytes 442376 | tf_op jit(solution)/shard_map/ppermute | solution.py:139
  31.9 1.9 %collective-permute-start.2 = (bf16[96,768]{1,0:T(8,128)(2,1)S(1)}, bf16[96,768]{1,0:T(8,128)(2,1)S(1)}, u32[]{:S(2)}, u32[]{:S(2)}) collective-permute-start(bf16[96,768]{1,0:T(8,128)(2,1)S(1)} %get-tuple-element.20), channel_id=1, source_target_pairs={{0,0},{16,16},{32,32},{48,48},{65,65},{81,81},{97,97},{113,113},{1... | collective-permute-start | bytes 442376 | tf_op jit(solution)/shard_map/ppermute | solution.py:139
  33.8 4.9 %collective-permute-start.1 = (bf16[96,768]{1,0:T(8,128)(2,1)S(1)}, bf16[96,768]{1,0:T(8,128)(2,1)S(1)}, u32[]{:S(2)}, u32[]{:S(2)}) collective-permute-start(bf16[96,768]{1,0:T(8,128)(2,1)S(1)} %get-tuple-element.21), channel_id=1, source_target_pairs={{0,0},{16,16},{32,32},{48,48},{65,65},{81,81},{97,97},{113,113},{1... | collective-permute-start | bytes 442376 | tf_op jit(solution)/shard_map/ppermute | solution.py:139
  38.7 0.9 collective-permute-done.2.two
  39.5 5.2 %collective-permute-done.1.one = bf16[96,768]{1,0:T(8,128)(2,1)S(1)} collective-permute-done((bf16[96,768]{1,0:T(8,128)(2,1)S(1)}, bf16[96,768]{1,0:T(8,128)(2,1)S(1)}, u32[]{:S(2)}, u32[]{:S(2)}) %collective-permute-start.1) | collective-permute-done | bytes 147488 | tf_op jit(solution)/shard_map/ppermute | solution.py:139
  44.7 0.9 shard_map.64
  45.7 0.9 copy.10
  46.5 3.9 %all-to-all-start = ((bf16[4,6,2,8,768]{4,3,2,1,0:T(8,128)(2,1)}), bf16[4,6,2,8,768]{4,3,2,1,0:T(8,128)(2,1)S(1)}, u32[]{:S(2)}, u32[]{:S(2)}) async-start(bf16[4,6,2,8,768]{4,3,2,1,0:T(8,128)(2,1)} %bitcast.25), calls=%async_computation | async-start | bytes 1179648 | tf_op jit(solution)/shard_map/all_to_all | solution.py:145
  50.4 1.8 %collective-permute-start = (f32[1]{0:T(128)}, f32[1]{0:T(128)}, u32[]{:S(2)}, u32[]{:S(2)}) collective-permute-start(f32[1]{0:T(128)} %param.8), channel_id=1, source_target_pairs={{0,0},{16,128},{32,256},{48,384},{128,16},{144,144},{160,272},{176... | collective-permute-start | bytes 20 | tf_op jit(solution)/shard_map/ppermute | solution.py:147
  52.3 5.4 %all-to-all-done.own = bf16[4,6,2,8,768]{4,3,2,1,0:T(8,128)(2,1)S(1)} async-done(((bf16[4,6,2,8,768]{4,3,2,1,0:T(8,128)(2,1)}), bf16[4,6,2,8,768]{4,3,2,1,0:T(8,128)(2,1)S(1)}, u32[]{:S(2)}, u32[]{:S(2)}) %all-to-all-start) | async-done | bytes 589856 | tf_op jit(solution)/shard_map/all_to_all | solution.py:145
  58.4 27.4 %all_to_all.20 = bf16[64,2,2304]{2,1,0:T(2,128)(2,1)S(1)} all-to-all(bf16[64,2,2304]{2,1,0:T(2,128)(2,1)S(1)} %reshape.27), channel_id=1, replica_groups=mesh['x'=4,'zh'=2,'zl'=4,'y'=8,'c'=2] {'zl','y','c'}, dimensions={0} | all-to-all | bytes 1179648 | tf_op jit(solution)/shard_map/all_to_all | solution.py:153
  86.2 2.5 %collective-permute-start.4 = (bf16[4,384,768]{2,1,0:T(8,128)(2,1)}, bf16[4,384,768]{2,1,0:T(8,128)(2,1)S(1)}, u32[]{:S(2)}, u32[]{:S(2)}) collective-permute-start(bf16[4,384,768]{2,1,0:T(8,128)(2,1)} %bitcast.26), channel_id=1, source_target_pairs={{0,1},{1,0},{2,3},{3,2},{4,5},{5,4},{6,7},{7,6},{8,9},{9,8},{10,11... | collective-permute-start | bytes 7077896 | tf_op jit(solution)/shard_map/ppermute | solution.py:155
  88.8 4.3 %collective-permute-done.4.other = bf16[4,384,768]{2,1,0:T(8,128)(2,1)S(1)} collective-permute-done((bf16[4,384,768]{2,1,0:T(8,128)(2,1)}, bf16[4,384,768]{2,1,0:T(8,128)(2,1)S(1)}, u32[]{:S(2)}, u32[]{:S(2)}) %collective-permute-start.4) | collective-permute-done | bytes 2359328 | tf_op jit(solution)/shard_map/ppermute | solution.py:155
  93.1 1.7 %copy-done.1 = bf16[1536,768]{1,0:T(8,128)(2,1)S(1)} copy-done((bf16[1536,768]{1,0:T(8,128)(2,1)S(1)}, bf16[1536,768]{1,0:T(8,128)(2,1)}, u32[]{:S(2)}) %copy-start.1) | copy-done | bytes 2359320
  94.8 5.5 %shard_map.65 = bf16[384,768]{1,0:T(8,128)(2,1)S(1)} custom-call(s32[1]{0:T(128)} %bitcast.4.core, f32[3]{0:T(128)S(1)} %copy-done.2, f32[1]{0:T(128)} %collective-permute-done.member, bf16[384,768]{1,0:T(8,128)(2,1)S(1)} %reshape.28.field, bf16[4,384,768]{2,1,0:T(8,128)(2,1)S(1)} %bitcast.27, bf16[4,384,768]{2,1,0:T(8,128)(2,1)S(1)} %collective-permute-done.4.other), custom_call_target="tpu_custom_call" | custom-call | flops 2000000000 | bytes 5000000 | tf_op jit(solution)/shard_map/pallas_call | solution.py:76
  100.7 26.3 %all_to_all.21 = bf16[64,2,2304]{2,1,0:T(2,128)(2,1)S(1)} all-to-all(bf16[64,2,2304]{2,1,0:T(2,128)(2,1)S(1)} %reshape.29), channel_id=1, replica_groups=mesh['x'=4,'zh'=2,'zl'=4,'y'=8,'c'=2] {'c','zl','y'}, dimensions={0} | all-to-all | bytes 1179648 | tf_op jit(solution)/shard_map/all_to_all | solution.py:157
  127.4 0.5 shard_map.66
  127.8 6.3 %collective-permute-start.5 = (bf16[6,8,768]{2,1,0:T(8,128)(2,1)S(1)}, bf16[6,8,768]{2,1,0:T(8,128)(2,1)S(1)}, u32[]{:S(2)}, u32[]{:S(2)}) collective-permute-start(bf16[6,8,768]{2,1,0:T(8,128)(2,1)S(1)} %shard_map.66), channel_id=1, source_target_pairs={{0,64},{64,0},{1,65},{65,1},{2,66},{66,2},{3,67},{67,3},{4,68},{68... | collective-permute-start | bytes 221192 | tf_op jit(solution)/shard_map/ppermute | solution.py:129
  134.1 2.8 %collective-permute-done.5.other = bf16[6,8,768]{2,1,0:T(8,128)(2,1)S(1)} collective-permute-done((bf16[6,8,768]{2,1,0:T(8,128)(2,1)S(1)}, bf16[6,8,768]{2,1,0:T(8,128)(2,1)S(1)}, u32[]{:S(2)}, u32[]{:S(2)}) %collective-permute-start.5) | collective-permute-done | bytes 73760 | tf_op jit(solution)/shard_map/ppermute | solution.py:129
  137.0 1.1 shard_map.67
  (21 shorter events, 1.9 us)
Async XLA Ops:
  6.5 45.7 %copy-start = (f32[64,6,768]{2,0,1:T(8,128)S(1)}, f32[64,6,768]{2,0,1:T(8,128)}, u32[]{:S(2)}) copy-start(f32[64,6,768]{2,0,1:T(8,128)} %param.7) | copy-start | bytes 3538948
  8.0 36.7 %all-to-all-start.2 = ((bf16[32,8,384]{2,1,0:T(8,128)(2,1)}), bf16[32,8,384]{2,1,0:T(8,128)(2,1)S(1)}, u32[]{:S(2)}, u32[]{:S(2)}) async-start(bf16[32,8,384]{2,1,0:T(8,128)(2,1)} %broadcast_in_dim.2), calls=%async_computation.2 | async-start | bytes 393216 | tf_op jit(solution)/shard_map/all_to_all | solution.py:140
  21.5 24.2 %copy-start.3 = (bf16[1,64,6,768]{3,1,2,0:T(8,128)(2,1)S(1)}, bf16[1,64,6,768]{3,1,2,0:T(8,128)(2,1)}, u32[]{:S(2)}) copy-start(bf16[1,64,6,768]{3,1,2,0:T(8,128)(2,1)} %param.6) | copy-start | bytes 1769476
  21.5 64.7 %all-gather.3.cloned.1.call-start = ((), (), s32[]{:S(2)}) async-start(), calls=%async_computation.4 | async-start | bytes 2949120 | tf_op jit(solution)/shard_map/all_gather | solution.py:142
  22.7 16.0 %collective-permute-start.3 = (bf16[96,768]{1,0:T(8,128)(2,1)S(1)}, bf16[96,768]{1,0:T(8,128)(2,1)S(1)}, u32[]{:S(2)}, u32[]{:S(2)}) collective-permute-start(bf16[96,768]{1,0:T(8,128)(2,1)S(1)} %get-tuple-element.19), channel_id=1, source_target_pairs={{0,0},{16,16},{32,32},{48,48},{65,65},{81,81},{97,97},{113,113},{1... | collective-permute-start | bytes 442376 | tf_op jit(solution)/shard_map/ppermute | solution.py:139
  31.9 7.7 %collective-permute-start.2 = (bf16[96,768]{1,0:T(8,128)(2,1)S(1)}, bf16[96,768]{1,0:T(8,128)(2,1)S(1)}, u32[]{:S(2)}, u32[]{:S(2)}) collective-permute-start(bf16[96,768]{1,0:T(8,128)(2,1)S(1)} %get-tuple-element.20), channel_id=1, source_target_pairs={{0,0},{16,16},{32,32},{48,48},{65,65},{81,81},{97,97},{113,113},{1... | collective-permute-start | bytes 442376 | tf_op jit(solution)/shard_map/ppermute | solution.py:139
  33.8 11.0 %collective-permute-start.1 = (bf16[96,768]{1,0:T(8,128)(2,1)S(1)}, bf16[96,768]{1,0:T(8,128)(2,1)S(1)}, u32[]{:S(2)}, u32[]{:S(2)}) collective-permute-start(bf16[96,768]{1,0:T(8,128)(2,1)S(1)} %get-tuple-element.21), channel_id=1, source_target_pairs={{0,0},{16,16},{32,32},{48,48},{65,65},{81,81},{97,97},{113,113},{1... | collective-permute-start | bytes 442376 | tf_op jit(solution)/shard_map/ppermute | solution.py:139
  46.5 11.1 %all-to-all-start = ((bf16[4,6,2,8,768]{4,3,2,1,0:T(8,128)(2,1)}), bf16[4,6,2,8,768]{4,3,2,1,0:T(8,128)(2,1)S(1)}, u32[]{:S(2)}, u32[]{:S(2)}) async-start(bf16[4,6,2,8,768]{4,3,2,1,0:T(8,128)(2,1)} %bitcast.25), calls=%async_computation | async-start | bytes 1179648 | tf_op jit(solution)/shard_map/all_to_all | solution.py:145
  50.4 1.8 %collective-permute-start = (f32[1]{0:T(128)}, f32[1]{0:T(128)}, u32[]{:S(2)}, u32[]{:S(2)}) collective-permute-start(f32[1]{0:T(128)} %param.8), channel_id=1, source_target_pairs={{0,0},{16,128},{32,256},{48,384},{128,16},{144,144},{160,272},{176... | collective-permute-start | bytes 20 | tf_op jit(solution)/shard_map/ppermute | solution.py:147
  58.4 34.7 %copy-start.2 = (f32[3]{0:T(128)S(1)}, f32[3]{0:T(128)}, u32[]{:S(2)}) copy-start(f32[3]{0:T(128)} %scale.1) | copy-start | bytes 40
  86.2 6.9 %collective-permute-start.4 = (bf16[4,384,768]{2,1,0:T(8,128)(2,1)}, bf16[4,384,768]{2,1,0:T(8,128)(2,1)S(1)}, u32[]{:S(2)}, u32[]{:S(2)}) collective-permute-start(bf16[4,384,768]{2,1,0:T(8,128)(2,1)} %bitcast.26), channel_id=1, source_target_pairs={{0,1},{1,0},{2,3},{3,2},{4,5},{5,4},{6,7},{7,6},{8,9},{9,8},{10,11... | collective-permute-start | bytes 7077896 | tf_op jit(solution)/shard_map/ppermute | solution.py:155
  93.1 1.7 %copy-start.1 = (bf16[1536,768]{1,0:T(8,128)(2,1)S(1)}, bf16[1536,768]{1,0:T(8,128)(2,1)}, u32[]{:S(2)}) copy-start(bf16[1536,768]{1,0:T(8,128)(2,1)} %all-gather.3.cloned.1.call-done) | copy-start | bytes 7077892
  127.8 9.1 %collective-permute-start.5 = (bf16[6,8,768]{2,1,0:T(8,128)(2,1)S(1)}, bf16[6,8,768]{2,1,0:T(8,128)(2,1)S(1)}, u32[]{:S(2)}, u32[]{:S(2)}) collective-permute-start(bf16[6,8,768]{2,1,0:T(8,128)(2,1)S(1)} %shard_map.66), channel_id=1, source_target_pairs={{0,64},{64,0},{1,65},{65,1},{2,66},{66,2},{3,67},{67,3},{4,68},{68... | collective-permute-start | bytes 221192 | tf_op jit(solution)/shard_map/ppermute | solution.py:129
Sparse Core Ops, SparseCore 0:
  45.8 36.4 all-gather.2

commit v11 on v9

--- a/solution.py
+++ b/solution.py
@@ -141,19 +141,20 @@
 
     own = perturbations[0].transpose(1, 0, 2).reshape(6, 4, 2, 8, 768).transpose(1, 0, 2, 3, 4)
     own = lax.all_to_all(own, "x", split_axis=0, concat_axis=0, tiled=True)
+    core, side = core.reshape(1).astype(jnp.int32), side.reshape(1).astype(jnp.int32)
+    own, core, side = lax.optimization_barrier((own, core, side))
     turn = [(4 * a + b, 4 * b + a) for a in range(4) for b in range(4)]
-    weight = lax.ppermute(member_weights, ("x", "zl"), turn)
-    own, weight = lax.optimization_barrier((own, weight))
+    weight = lax.optimization_barrier((member_weights, own))[0]
+    weight = lax.ppermute(weight, ("x", "zl"), turn)
     level = lax.dynamic_slice_in_dim(gradient.transpose(1, 0, 2), x * 16, 16, axis=1)
     schur = (own.astype(F32) * level.reshape(1, 6, 2, 8, 768)).astype(BF16)
     schur = schur.transpose(0, 2, 3, 1, 4).reshape(64, 2, 2304)
     field = lax.all_to_all(schur, COL, split_axis=0, concat_axis=0, tiled=True).reshape(384, 768)
     mine = lax.optimization_barrier((mine, field))[0]
     other = lax.ppermute(mine, "c", SWAP)
-    core = core.reshape(1).astype(jnp.int32)
     filtered = filter_pair(core, scale_weights, weight, field, mine, other).reshape(64, 2, 2304)
     back = lax.all_to_all(filtered, ("c", "zl", "y"), split_axis=0, concat_axis=0, tiled=True)
-    total = final_sum(side.reshape(1).astype(jnp.int32), own, back.reshape(2, 4, 8, 6, 768))
+    total = final_sum(side, own, back.reshape(2, 4, 8, 6, 768))
     return total.transpose(1, 0, 2)
 
 

time: 139 us -> 142 us (1.022)
  blocking collectives: 40.7 us -> 72.1 us
  waiting for transfers between devices: 33.9 us -> 14.5 us
  starting transfers between devices: 33.2 us -> 25.9 us
    all_to_all x0 -> x1, blocking collectives: none -> 31.4 us  [on_device(): lax.all_to_all(filtered, ('c', 'zl', 'y'), split_axis=0, concat_axis=0, t...]
    all_to_all x1 -> x0, waiting for transfers between devices: 19.4 us -> none  [on_device(): lax.all_to_all(filtered, ('c', 'zl', 'y'), split_axis=0, concat_axis=0, t...]
    all_to_all x1 -> x0, starting transfers between devices: 7.28 us -> none  [on_device(): lax.all_to_all(filtered, ('c', 'zl', 'y'), split_axis=0, concat_axis=0, t...]
    ppermute x1, waiting for transfers between devices: 4.48 us -> 2.51 us  [on_device(): other = lax.ppermute(mine, 'c', SWAP)]
    all_to_all x1, waiting for transfers between devices: 6.23 us -> 8.12 us  [on_device(): own = lax.all_to_all(own, 'x', split_axis=0, concat_axis=0, tiled=True)]
  transfers between devices with their start and end apart: 7 -> 6, of which waited for: 4 -> 3; matrix products, arithmetic and copies ran while one was open for 2% -> 2% of each run, Pallas kernels for 0% -> 0%
where the time goes in v11:
time: 142 us; the launch traced here: 139 us
  blocking collectives  72.1 us (51%)
  starting transfers between devices  25.9 us (18%)
  waiting for transfers between devices  14.5 us (10%)
  between operations  13.5 us (10%)
  Pallas kernels  8.13 us (6%)
  local copies, waits for them, and re-layouts  4.96 us (3%)
    all_to_all x1, blocking collectives, on_device(): lax.all_to_all(filtered, ('c', 'zl', 'y'), split_axis=0, concat_axis=0, t...  31.4 us
    all_to_all x1, blocking collectives, on_device(): lax.all_to_all(schur, COL, split_axis=0, concat_axis=0, tiled=True)  22.9 us
    all_to_all x1, blocking collectives, on_device(): lax.all_to_all(tiles, ('zl', 'y'), split_axis=0, concat_axis=0, tiled=True)  17.7 us
    ppermute x1, starting transfers between devices, on_device(): block = lax.ppermute(lon_filter, ('zh', 'zl', 'c'), pairs)  12.2 us
    all_to_all x1, waiting for transfers between devices, on_device(): own = lax.all_to_all(own, 'x', split_axis=0, concat_axis=0, tiled=True)  8.12 us
    pallas_call x1, Pallas kernels, filter_pair(): pl.pallas_call(filter_kernel, out_shape=jax.ShapeDtypeStruct((384, 768),...  5.6 us
    ppermute x1, starting transfers between devices, final_sum(): lax.ppermute(send, 'zh', SWAP)  5.32 us
    all_to_all x1, starting transfers between devices, on_device(): own = lax.all_to_all(own, 'x', split_axis=0, concat_axis=0, tiled=True)  4.01 us
  transfers between devices with their start and end apart: 6, of which 3 were waited for; matrix products, arithmetic and copies ran while one was open for 2% of the time, Pallas kernels for 0%

profile of v11, /device:TPU:1, one launch (start us, length us, event | category | flops | bytes accessed | tf_op | source)
XLA Modules:
  0.0 139.1 jit_solution(1916903075115411568)
XLA Ops:
  6.5 12.2 %collective-permute-start.1 = (bf16[3,96,768]{2,1,0:T(8,128)(2,1)}, bf16[3,96,768]{2,1,0:T(8,128)(2,1)S(1)}, u32[]{:S(2)}, u32[]{:S(2)}) collective-permute-start(bf16[3,96,768]{2,1,0:T(8,128)(2,1)} %param.10), channel_id=1, source_target_pairs={{0,0},{16,16},{32,32},{48,48},{65,65},{81,81},{97,97},{113,113},{1... | collective-permute-start | bytes 1327112 | tf_op jit(solution)/shard_map/ppermute | solution.py:135
  18.7 0.7 dynamic-slice_bitcast_fusion.1
  19.5 17.7 %all_to_all.20.tiles = bf16[32,8,384]{2,1,0:T(8,128)(2,1)S(1)} all-to-all(bf16[32,8,384]{2,1,0:T(8,128)(2,1)S(1)} %broadcast_in_dim.2), channel_id=1, replica_groups=mesh['x'=4,'zh'=2,'zl'=4,'y'=8,'c'=2] {'zl','y'}, dimensions={0} | all-to-all | bytes 393216 | tf_op jit(solution)/shard_map/all_to_all | solution.py:138
  37.1 0.9 shard_map.64
  38.1 0.9 copy.10
  38.9 4.0 %all-to-all-start = ((bf16[4,6,2,8,768]{4,3,2,1,0:T(8,128)(2,1)}), bf16[4,6,2,8,768]{4,3,2,1,0:T(8,128)(2,1)S(1)}, u32[]{:S(2)}, u32[]{:S(2)}) async-start(bf16[4,6,2,8,768]{4,3,2,1,0:T(8,128)(2,1)} %bitcast.20), calls=%async_computation | async-start | bytes 1179648 | tf_op jit(solution)/shard_map/all_to_all | solution.py:143
  43.0 8.1 %all-to-all-done.own = bf16[4,6,2,8,768]{4,3,2,1,0:T(8,128)(2,1)S(1)} async-done(((bf16[4,6,2,8,768]{4,3,2,1,0:T(8,128)(2,1)}), bf16[4,6,2,8,768]{4,3,2,1,0:T(8,128)(2,1)S(1)}, u32[]{:S(2)}, u32[]{:S(2)}) %all-to-all-start) | async-done | bytes 589856 | tf_op jit(solution)/shard_map/all_to_all | solution.py:143
  51.1 0.1 fusion
  51.2 0.2 copy.8
  51.4 0.4 reshape.30
  51.8 22.9 %all_to_all.21 = bf16[64,2,2304]{2,1,0:T(2,128)(2,1)S(1)} all-to-all(bf16[64,2,2304]{2,1,0:T(2,128)(2,1)S(1)} %reshape.30), channel_id=1, replica_groups=mesh['x'=4,'zh'=2,'zl'=4,'y'=8,'c'=2] {'zl','y','c'}, dimensions={0} | all-to-all | bytes 1179648 | tf_op jit(solution)/shard_map/all_to_all | solution.py:152
  74.8 0.4 reshape.31.field
  75.2 2.5 %collective-permute-start.2 = (bf16[4,384,768]{2,1,0:T(8,128)(2,1)}, bf16[4,384,768]{2,1,0:T(8,128)(2,1)S(1)}, u32[]{:S(2)}, u32[]{:S(2)}) collective-permute-start(bf16[4,384,768]{2,1,0:T(8,128)(2,1)} %bitcast.22), channel_id=1, source_target_pairs={{0,1},{1,0},{2,3},{3,2},{4,5},{5,4},{6,7},{7,6},{8,9},{9,8},{10,11... | collective-permute-start | bytes 7077896 | tf_op jit(solution)/shard_map/ppermute | solution.py:154
  77.7 1.8 %collective-permute-start = (f32[1]{0:T(128)}, f32[1]{0:T(128)}, u32[]{:S(2)}, u32[]{:S(2)}) collective-permute-start(f32[1]{0:T(128)} %param.8), channel_id=1, source_target_pairs={{0,0},{16,128},{32,256},{48,384},{128,16},{144,144},{160,272},{176... | collective-permute-start | bytes 20 | tf_op jit(solution)/shard_map/ppermute | solution.py:148
  79.6 2.5 %collective-permute-done.2.other = bf16[4,384,768]{2,1,0:T(8,128)(2,1)S(1)} collective-permute-done((bf16[4,384,768]{2,1,0:T(8,128)(2,1)}, bf16[4,384,768]{2,1,0:T(8,128)(2,1)S(1)}, u32[]{:S(2)}, u32[]{:S(2)}) %collective-permute-start.2) | collective-permute-done | bytes 2359328 | tf_op jit(solution)/shard_map/ppermute | solution.py:154
  82.1 1.7 %copy-done.1 = bf16[1536,768]{1,0:T(8,128)(2,1)S(1)} copy-done((bf16[1536,768]{1,0:T(8,128)(2,1)S(1)}, bf16[1536,768]{1,0:T(8,128)(2,1)}, u32[]{:S(2)}) %copy-start.1) | copy-done | bytes 2359320
  83.8 5.6 %shard_map.65 = bf16[384,768]{1,0:T(8,128)(2,1)S(1)} custom-call(s32[1]{0:T(128)} %bitcast.4.core, f32[3]{0:T(128)S(1)} %copy-done.2, f32[1]{0:T(128)} %collective-permute-done.member, bf16[384,768]{1,0:T(8,128)(2,1)S(1)} %reshape.31.field, bf16[4,384,768]{2,1,0:T(8,128)(2,1)S(1)} %bitcast.23, bf16[4,384,768]{2,1,0:T(8,128)(2,1)S(1)} %collective-permute-done.2.other), custom_call_target="tpu_custom_call" | custom-call | flops 2000000000 | bytes 5000000 | tf_op jit(solution)/shard_map/pallas_call | solution.py:75
  89.4 0.3 reshape.33
  89.7 31.4 %all_to_all.22 = bf16[64,2,2304]{2,1,0:T(2,128)(2,1)S(1)} all-to-all(bf16[64,2,2304]{2,1,0:T(2,128)(2,1)S(1)} %reshape.33), channel_id=1, replica_groups=mesh['x'=4,'zh'=2,'zl'=4,'y'=8,'c'=2] {'c','zl','y'}, dimensions={0} | all-to-all | bytes 1179648 | tf_op jit(solution)/shard_map/all_to_all | solution.py:156
  121.1 0.4 reshape.34.back
  121.5 0.5 shard_map.66
  122.0 5.3 %collective-permute-start.3 = (bf16[6,8,768]{2,1,0:T(8,128)(2,1)S(1)}, bf16[6,8,768]{2,1,0:T(8,128)(2,1)S(1)}, u32[]{:S(2)}, u32[]{:S(2)}) collective-permute-start(bf16[6,8,768]{2,1,0:T(8,128)(2,1)S(1)} %shard_map.66), channel_id=1, source_target_pairs={{0,64},{64,0},{1,65},{65,1},{2,66},{66,2},{3,67},{67,3},{4,68},{68... | collective-permute-start | bytes 221192 | tf_op jit(solution)/shard_map/ppermute | solution.py:128
  127.3 3.8 %collective-permute-done.3.other = bf16[6,8,768]{2,1,0:T(8,128)(2,1)S(1)} collective-permute-done((bf16[6,8,768]{2,1,0:T(8,128)(2,1)S(1)}, bf16[6,8,768]{2,1,0:T(8,128)(2,1)S(1)}, u32[]{:S(2)}, u32[]{:S(2)}) %collective-permute-start.3) | collective-permute-done | bytes 73760 | tf_op jit(solution)/shard_map/ppermute | solution.py:128
  131.1 1.1 shard_map.67
  (15 shorter events, 0.1 us)
Async XLA Ops:
  6.5 36.4 %copy-start = (f32[64,6,768]{2,0,1:T(8,128)S(1)}, f32[64,6,768]{2,0,1:T(8,128)}, u32[]{:S(2)}) copy-start(f32[64,6,768]{2,0,1:T(8,128)} %param.7) | copy-start | bytes 3538948
  6.5 68.7 %all-gather.3.cloned.1.call-start = ((), (), s32[]{:S(2)}) async-start(), calls=%async_computation.4 | async-start | bytes 2949120 | tf_op jit(solution)/shard_map/all_gather | solution.py:140
  6.5 30.6 %collective-permute-start.1 = (bf16[3,96,768]{2,1,0:T(8,128)(2,1)}, bf16[3,96,768]{2,1,0:T(8,128)(2,1)S(1)}, u32[]{:S(2)}, u32[]{:S(2)}) collective-permute-start(bf16[3,96,768]{2,1,0:T(8,128)(2,1)} %param.10), channel_id=1, source_target_pairs={{0,0},{16,16},{32,32},{48,48},{65,65},{81,81},{97,97},{113,113},{1... | collective-permute-start | bytes 1327112 | tf_op jit(solution)/shard_map/ppermute | solution.py:135
  19.4 18.6 %copy-start.3 = (bf16[1,64,6,768]{3,1,2,0:T(8,128)(2,1)S(1)}, bf16[1,64,6,768]{3,1,2,0:T(8,128)(2,1)}, u32[]{:S(2)}) copy-start(bf16[1,64,6,768]{3,1,2,0:T(8,128)(2,1)} %param.6) | copy-start | bytes 1769476
  38.9 12.2 %all-to-all-start = ((bf16[4,6,2,8,768]{4,3,2,1,0:T(8,128)(2,1)}), bf16[4,6,2,8,768]{4,3,2,1,0:T(8,128)(2,1)S(1)}, u32[]{:S(2)}, u32[]{:S(2)}) async-start(bf16[4,6,2,8,768]{4,3,2,1,0:T(8,128)(2,1)} %bitcast.20), calls=%async_computation | async-start | bytes 1179648 | tf_op jit(solution)/shard_map/all_to_all | solution.py:143
  51.8 30.3 %copy-start.2 = (f32[3]{0:T(128)S(1)}, f32[3]{0:T(128)}, u32[]{:S(2)}) copy-start(f32[3]{0:T(128)} %scale.1) | copy-start | bytes 40
  75.2 6.9 %collective-permute-start.2 = (bf16[4,384,768]{2,1,0:T(8,128)(2,1)}, bf16[4,384,768]{2,1,0:T(8,128)(2,1)S(1)}, u32[]{:S(2)}, u32[]{:S(2)}) collective-permute-start(bf16[4,384,768]{2,1,0:T(8,128)(2,1)} %bitcast.22), channel_id=1, source_target_pairs={{0,1},{1,0},{2,3},{3,2},{4,5},{5,4},{6,7},{7,6},{8,9},{9,8},{10,11... | collective-permute-start | bytes 7077896 | tf_op jit(solution)/shard_map/ppermute | solution.py:154
  77.7 1.8 %collective-permute-start = (f32[1]{0:T(128)}, f32[1]{0:T(128)}, u32[]{:S(2)}, u32[]{:S(2)}) collective-permute-start(f32[1]{0:T(128)} %param.8), channel_id=1, source_target_pairs={{0,0},{16,128},{32,256},{48,384},{128,16},{144,144},{160,272},{176... | collective-permute-start | bytes 20 | tf_op jit(solution)/shard_map/ppermute | solution.py:148
  82.1 1.7 %copy-start.1 = (bf16[1536,768]{1,0:T(8,128)(2,1)S(1)}, bf16[1536,768]{1,0:T(8,128)(2,1)}, u32[]{:S(2)}) copy-start(bf16[1536,768]{1,0:T(8,128)(2,1)} %all-gather.3.cloned.1.call-done) | copy-start | bytes 7077892
  122.0 9.1 %collective-permute-start.3 = (bf16[6,8,768]{2,1,0:T(8,128)(2,1)S(1)}, bf16[6,8,768]{2,1,0:T(8,128)(2,1)S(1)}, u32[]{:S(2)}, u32[]{:S(2)}) collective-permute-start(bf16[6,8,768]{2,1,0:T(8,128)(2,1)S(1)} %shard_map.66), channel_id=1, source_target_pairs={{0,64},{64,0},{1,65},{65,1},{2,66},{66,2},{3,67},{67,3},{4,68},{68... | collective-permute-start | bytes 221192 | tf_op jit(solution)/shard_map/ppermute | solution.py:128
Sparse Core Ops, SparseCore 0:
  38.2 33.2 all-gather.2

commit v12 on v9

--- a/solution.py
+++ b/solution.py
@@ -143,17 +143,17 @@
     own = lax.all_to_all(own, "x", split_axis=0, concat_axis=0, tiled=True)
     turn = [(4 * a + b, 4 * b + a) for a in range(4) for b in range(4)]
     weight = lax.ppermute(member_weights, ("x", "zl"), turn)
-    own, weight = lax.optimization_barrier((own, weight))
+    core, side = core.reshape(1).astype(jnp.int32), side.reshape(1).astype(jnp.int32)
+    own, weight, core, side = lax.optimization_barrier((own, weight, core, side))
     level = lax.dynamic_slice_in_dim(gradient.transpose(1, 0, 2), x * 16, 16, axis=1)
     schur = (own.astype(F32) * level.reshape(1, 6, 2, 8, 768)).astype(BF16)
     schur = schur.transpose(0, 2, 3, 1, 4).reshape(64, 2, 2304)
     field = lax.all_to_all(schur, COL, split_axis=0, concat_axis=0, tiled=True).reshape(384, 768)
     mine = lax.optimization_barrier((mine, field))[0]
     other = lax.ppermute(mine, "c", SWAP)
-    core = core.reshape(1).astype(jnp.int32)
     filtered = filter_pair(core, scale_weights, weight, field, mine, other).reshape(64, 2, 2304)
     back = lax.all_to_all(filtered, ("c", "zl", "y"), split_axis=0, concat_axis=0, tiled=True)
-    total = final_sum(side.reshape(1).astype(jnp.int32), own, back.reshape(2, 4, 8, 6, 768))
+    total = final_sum(side, own, back.reshape(2, 4, 8, 6, 768))
     return total.transpose(1, 0, 2)
 
 

time: 139 us -> 137 us (0.986)
  blocking collectives: 40.7 us -> 67.2 us
  waiting for transfers between devices: 33.9 us -> 14.5 us
  starting transfers between devices: 33.2 us -> 25.9 us
    all_to_all x0 -> x1, blocking collectives: none -> 26.6 us  [on_device(): lax.all_to_all(filtered, ('c', 'zl', 'y'), split_axis=0, concat_axis=0, t...]
    all_to_all x1 -> x0, waiting for transfers between devices: 19.4 us -> none  [on_device(): lax.all_to_all(filtered, ('c', 'zl', 'y'), split_axis=0, concat_axis=0, t...]
    all_to_all x1 -> x0, starting transfers between devices: 7.28 us -> none  [on_device(): lax.all_to_all(filtered, ('c', 'zl', 'y'), split_axis=0, concat_axis=0, t...]
  transfers between devices with their start and end apart: 7 -> 6, of which waited for: 4 -> 3; matrix products, arithmetic and copies ran while one was open for 2% -> 2% of each run, Pallas kernels for 0% -> 0%
where the time goes in v12:
time: 137 us; the launch traced here: 134 us
  blocking collectives  67.2 us (49%)
  starting transfers between devices  25.9 us (19%)
  waiting for transfers between devices  14.5 us (11%)
  between operations  13.5 us (10%)
  Pallas kernels  8.05 us (6%)
  local copies, waits for them, and re-layouts  4.96 us (4%)
    all_to_all x1, blocking collectives, on_device(): lax.all_to_all(filtered, ('c', 'zl', 'y'), split_axis=0, concat_axis=0, t...  26.6 us
    all_to_all x1, blocking collectives, on_device(): lax.all_to_all(schur, COL, split_axis=0, concat_axis=0, tiled=True)  23 us
    all_to_all x1, blocking collectives, on_device(): lax.all_to_all(tiles, ('zl', 'y'), split_axis=0, concat_axis=0, tiled=True)  17.7 us
    ppermute x1, starting transfers between devices, on_device(): block = lax.ppermute(lon_filter, ('zh', 'zl', 'c'), pairs)  12.2 us
    all_to_all x1, waiting for transfers between devices, on_device(): own = lax.all_to_all(own, 'x', split_axis=0, concat_axis=0, tiled=True)  6.33 us
    pallas_call x1, Pallas kernels, filter_pair(): pl.pallas_call(filter_kernel, out_shape=jax.ShapeDtypeStruct((384, 768),...  5.51 us
    ppermute x1, starting transfers between devices, final_sum(): lax.ppermute(send, 'zh', SWAP)  5.37 us
    ppermute x1, waiting for transfers between devices, on_device(): other = lax.ppermute(mine, 'c', SWAP)  4.35 us
  transfers between devices with their start and end apart: 6, of which 3 were waited for; matrix products, arithmetic and copies ran while one was open for 2% of the time, Pallas kernels for 0%

profile of v12, /device:TPU:1, one launch (start us, length us, event | category | flops | bytes accessed | tf_op | source)
XLA Modules:
  0.0 134.2 jit_solution(2508621053031425000)
XLA Ops:
  6.5 12.2 %collective-permute-start.1 = (bf16[3,96,768]{2,1,0:T(8,128)(2,1)}, bf16[3,96,768]{2,1,0:T(8,128)(2,1)S(1)}, u32[]{:S(2)}, u32[]{:S(2)}) collective-permute-start(bf16[3,96,768]{2,1,0:T(8,128)(2,1)} %param.10), channel_id=1, source_target_pairs={{0,0},{16,16},{32,32},{48,48},{65,65},{81,81},{97,97},{113,113},{1... | collective-permute-start | bytes 1327112 | tf_op jit(solution)/shard_map/ppermute | solution.py:135
  18.7 0.7 dynamic-slice_bitcast_fusion.1
  19.5 17.7 %all_to_all.20.tiles = bf16[32,8,384]{2,1,0:T(8,128)(2,1)S(1)} all-to-all(bf16[32,8,384]{2,1,0:T(8,128)(2,1)S(1)} %broadcast_in_dim.2), channel_id=1, replica_groups=mesh['x'=4,'zh'=2,'zl'=4,'y'=8,'c'=2] {'zl','y'}, dimensions={0} | all-to-all | bytes 393216 | tf_op jit(solution)/shard_map/all_to_all | solution.py:138
  37.1 0.9 shard_map.64
  38.1 0.9 copy.10
  38.9 4.0 %all-to-all-start = ((bf16[4,6,2,8,768]{4,3,2,1,0:T(8,128)(2,1)}), bf16[4,6,2,8,768]{4,3,2,1,0:T(8,128)(2,1)S(1)}, u32[]{:S(2)}, u32[]{:S(2)}) async-start(bf16[4,6,2,8,768]{4,3,2,1,0:T(8,128)(2,1)} %bitcast.20), calls=%async_computation | async-start | bytes 1179648 | tf_op jit(solution)/shard_map/all_to_all | solution.py:143
  43.0 1.8 %collective-permute-start = (f32[1]{0:T(128)}, f32[1]{0:T(128)}, u32[]{:S(2)}, u32[]{:S(2)}) collective-permute-start(f32[1]{0:T(128)} %param.8), channel_id=1, source_target_pairs={{0,0},{16,128},{32,256},{48,384},{128,16},{144,144},{160,272},{176... | collective-permute-start | bytes 20 | tf_op jit(solution)/shard_map/ppermute | solution.py:145
  44.8 6.3 %all-to-all-done.own = bf16[4,6,2,8,768]{4,3,2,1,0:T(8,128)(2,1)S(1)} async-done(((bf16[4,6,2,8,768]{4,3,2,1,0:T(8,128)(2,1)}), bf16[4,6,2,8,768]{4,3,2,1,0:T(8,128)(2,1)S(1)}, u32[]{:S(2)}, u32[]{:S(2)}) %all-to-all-start) | async-done | bytes 589856 | tf_op jit(solution)/shard_map/all_to_all | solution.py:143
  51.1 0.1 fusion
  51.2 0.2 copy.8
  51.4 0.4 reshape.30
  51.8 23.0 %all_to_all.21 = bf16[64,2,2304]{2,1,0:T(2,128)(2,1)S(1)} all-to-all(bf16[64,2,2304]{2,1,0:T(2,128)(2,1)S(1)} %reshape.30), channel_id=1, replica_groups=mesh['x'=4,'zh'=2,'zl'=4,'y'=8,'c'=2] {'zl','y','c'}, dimensions={0} | all-to-all | bytes 1179648 | tf_op jit(solution)/shard_map/all_to_all | solution.py:151
  74.8 0.4 reshape.31.field
  75.2 2.5 %collective-permute-start.2 = (bf16[4,384,768]{2,1,0:T(8,128)(2,1)}, bf16[4,384,768]{2,1,0:T(8,128)(2,1)S(1)}, u32[]{:S(2)}, u32[]{:S(2)}) collective-permute-start(bf16[4,384,768]{2,1,0:T(8,128)(2,1)} %bitcast.22), channel_id=1, source_target_pairs={{0,1},{1,0},{2,3},{3,2},{4,5},{5,4},{6,7},{7,6},{8,9},{9,8},{10,11... | collective-permute-start | bytes 7077896 | tf_op jit(solution)/shard_map/ppermute | solution.py:153
  77.8 4.3 %collective-permute-done.2.other = bf16[4,384,768]{2,1,0:T(8,128)(2,1)S(1)} collective-permute-done((bf16[4,384,768]{2,1,0:T(8,128)(2,1)}, bf16[4,384,768]{2,1,0:T(8,128)(2,1)S(1)}, u32[]{:S(2)}, u32[]{:S(2)}) %collective-permute-start.2) | collective-permute-done | bytes 2359328 | tf_op jit(solution)/shard_map/ppermute | solution.py:153
  82.1 1.7 %copy-done.1 = bf16[1536,768]{1,0:T(8,128)(2,1)S(1)} copy-done((bf16[1536,768]{1,0:T(8,128)(2,1)S(1)}, bf16[1536,768]{1,0:T(8,128)(2,1)}, u32[]{:S(2)}) %copy-start.1) | copy-done | bytes 2359320
  83.8 5.5 %shard_map.65 = bf16[384,768]{1,0:T(8,128)(2,1)S(1)} custom-call(s32[1]{0:T(128)} %bitcast.4.core, f32[3]{0:T(128)S(1)} %copy-done.2, f32[1]{0:T(128)} %collective-permute-done.member, bf16[384,768]{1,0:T(8,128)(2,1)S(1)} %reshape.31.field, bf16[4,384,768]{2,1,0:T(8,128)(2,1)S(1)} %bitcast.23, bf16[4,384,768]{2,1,0:T(8,128)(2,1)S(1)} %collective-permute-done.2.other), custom_call_target="tpu_custom_call" | custom-call | flops 2000000000 | bytes 5000000 | tf_op jit(solution)/shard_map/pallas_call | solution.py:75
  89.3 0.3 reshape.33
  89.6 26.6 %all_to_all.22 = bf16[64,2,2304]{2,1,0:T(2,128)(2,1)S(1)} all-to-all(bf16[64,2,2304]{2,1,0:T(2,128)(2,1)S(1)} %reshape.33), channel_id=1, replica_groups=mesh['x'=4,'zh'=2,'zl'=4,'y'=8,'c'=2] {'c','zl','y'}, dimensions={0} | all-to-all | bytes 1179648 | tf_op jit(solution)/shard_map/all_to_all | solution.py:155
  116.2 0.4 reshape.34.back
  116.6 0.5 shard_map.66
  117.1 5.4 %collective-permute-start.3 = (bf16[6,8,768]{2,1,0:T(8,128)(2,1)S(1)}, bf16[6,8,768]{2,1,0:T(8,128)(2,1)S(1)}, u32[]{:S(2)}, u32[]{:S(2)}) collective-permute-start(bf16[6,8,768]{2,1,0:T(8,128)(2,1)S(1)} %shard_map.66), channel_id=1, source_target_pairs={{0,64},{64,0},{1,65},{65,1},{2,66},{66,2},{3,67},{67,3},{4,68},{68... | collective-permute-start | bytes 221192 | tf_op jit(solution)/shard_map/ppermute | solution.py:128
  122.4 3.7 %collective-permute-done.3.other = bf16[6,8,768]{2,1,0:T(8,128)(2,1)S(1)} collective-permute-done((bf16[6,8,768]{2,1,0:T(8,128)(2,1)S(1)}, bf16[6,8,768]{2,1,0:T(8,128)(2,1)S(1)}, u32[]{:S(2)}, u32[]{:S(2)}) %collective-permute-start.3) | collective-permute-done | bytes 73760 | tf_op jit(solution)/shard_map/ppermute | solution.py:128
  126.2 1.1 shard_map.67
  (15 shorter events, 0.1 us)
Async XLA Ops:
  6.5 38.2 %copy-start = (f32[64,6,768]{2,0,1:T(8,128)S(1)}, f32[64,6,768]{2,0,1:T(8,128)}, u32[]{:S(2)}) copy-start(f32[64,6,768]{2,0,1:T(8,128)} %param.7) | copy-start | bytes 3538948
  6.5 68.7 %all-gather.3.cloned.1.call-start = ((), (), s32[]{:S(2)}) async-start(), calls=%async_computation.4 | async-start | bytes 2949120 | tf_op jit(solution)/shard_map/all_gather | solution.py:140
  6.5 30.6 %collective-permute-start.1 = (bf16[3,96,768]{2,1,0:T(8,128)(2,1)}, bf16[3,96,768]{2,1,0:T(8,128)(2,1)S(1)}, u32[]{:S(2)}, u32[]{:S(2)}) collective-permute-start(bf16[3,96,768]{2,1,0:T(8,128)(2,1)} %param.10), channel_id=1, source_target_pairs={{0,0},{16,16},{32,32},{48,48},{65,65},{81,81},{97,97},{113,113},{1... | collective-permute-start | bytes 1327112 | tf_op jit(solution)/shard_map/ppermute | solution.py:135
  19.4 18.6 %copy-start.3 = (bf16[1,64,6,768]{3,1,2,0:T(8,128)(2,1)S(1)}, bf16[1,64,6,768]{3,1,2,0:T(8,128)(2,1)}, u32[]{:S(2)}) copy-start(bf16[1,64,6,768]{3,1,2,0:T(8,128)(2,1)} %param.6) | copy-start | bytes 1769476
  38.9 12.2 %all-to-all-start = ((bf16[4,6,2,8,768]{4,3,2,1,0:T(8,128)(2,1)}), bf16[4,6,2,8,768]{4,3,2,1,0:T(8,128)(2,1)S(1)}, u32[]{:S(2)}, u32[]{:S(2)}) async-start(bf16[4,6,2,8,768]{4,3,2,1,0:T(8,128)(2,1)} %bitcast.20), calls=%async_computation | async-start | bytes 1179648 | tf_op jit(solution)/shard_map/all_to_all | solution.py:143
  43.0 1.8 %collective-permute-start = (f32[1]{0:T(128)}, f32[1]{0:T(128)}, u32[]{:S(2)}, u32[]{:S(2)}) collective-permute-start(f32[1]{0:T(128)} %param.8), channel_id=1, source_target_pairs={{0,0},{16,128},{32,256},{48,384},{128,16},{144,144},{160,272},{176... | collective-permute-start | bytes 20 | tf_op jit(solution)/shard_map/ppermute | solution.py:145
  51.8 30.3 %copy-start.2 = (f32[3]{0:T(128)S(1)}, f32[3]{0:T(128)}, u32[]{:S(2)}) copy-start(f32[3]{0:T(128)} %scale.1) | copy-start | bytes 40
  75.2 6.9 %collective-permute-start.2 = (bf16[4,384,768]{2,1,0:T(8,128)(2,1)}, bf16[4,384,768]{2,1,0:T(8,128)(2,1)S(1)}, u32[]{:S(2)}, u32[]{:S(2)}) collective-permute-start(bf16[4,384,768]{2,1,0:T(8,128)(2,1)} %bitcast.22), channel_id=1, source_target_pairs={{0,1},{1,0},{2,3},{3,2},{4,5},{5,4},{6,7},{7,6},{8,9},{9,8},{10,11... | collective-permute-start | bytes 7077896 | tf_op jit(solution)/shard_map/ppermute | solution.py:153
  82.1 1.7 %copy-start.1 = (bf16[1536,768]{1,0:T(8,128)(2,1)S(1)}, bf16[1536,768]{1,0:T(8,128)(2,1)}, u32[]{:S(2)}) copy-start(bf16[1536,768]{1,0:T(8,128)(2,1)} %all-gather.3.cloned.1.call-done) | copy-start | bytes 7077892
  117.1 9.1 %collective-permute-start.3 = (bf16[6,8,768]{2,1,0:T(8,128)(2,1)S(1)}, bf16[6,8,768]{2,1,0:T(8,128)(2,1)S(1)}, u32[]{:S(2)}, u32[]{:S(2)}) collective-permute-start(bf16[6,8,768]{2,1,0:T(8,128)(2,1)S(1)} %shard_map.66), channel_id=1, source_target_pairs={{0,64},{64,0},{1,65},{65,1},{2,66},{66,2},{3,67},{67,3},{4,68},{68... | collective-permute-start | bytes 221192 | tf_op jit(solution)/shard_map/ppermute | solution.py:128
Sparse Core Ops, SparseCore 0:
  38.2 33.2 all-gather.2

commit v13 on v12

--- a/solution.py
+++ b/solution.py
@@ -14,7 +14,6 @@
 VMEM = pl.BlockSpec(memory_space=pltpu.VMEM)
 SMEM = pl.BlockSpec(memory_space=pltpu.SMEM)
 ANY = pl.BlockSpec(memory_space=pl.ANY)
-HBM = pl.BlockSpec(memory_space=pltpu.MemorySpace.HBM)
 
 
 def pack_kernel(block, tiles, out):
@@ -37,20 +36,45 @@
     )(block, tiles)
 
 
-def filter_kernel(core, scale, member, field, mine, other, out, lon, lat, mid, lon_sems, lat_sems):
-    lon_copies, lat_copies = [], []
-    sides = ((mine, core[0]), (other, 1 - core[0]))
-    for m, (part, half) in enumerate(sides):
-        for s in range(3):
-            for h in range(2):
-                to = pl.ds(pl.multiple_of(half * 192 + 96 * h, 32), 96)
-                copy = pltpu.make_async_copy(
-                    part.at[s, pl.ds(288, 96), pl.ds(384 * h, 384)], lat.at[s, to, :], lat_sems.at[m, s, h]
-                )
-                copy.start()
-                lat_copies.append(copy)
+def copy_rows(part, lat, sems):
+    copies = []
     for s in range(3):
-        for m, (part, half) in enumerate(sides):
+        for h in range(2):
+            copy = pltpu.make_async_copy(
+                part.at[s, pl.ds(288, 96), pl.ds(384 * h, 384)], lat.at[s, pl.ds(96 * h, 96), :], sems.at[s, h]
+            )
+            copy.start()
+            copies.append(copy)
+    return copies
+
+
+def first_kernel(scale, member, field, mine, out, lat, sems):
+    for copy in copy_rows(mine, lat, sems):
+        copy.wait()
+    for s in range(3):
+        across = jnp.dot(lat[s], field[...], preferred_element_type=F32)
+        out[:, pl.ds(768 * s, 768)] = (scale[s] * member[0] * across).astype(BF16)
+
+
+def filter_first(scale, member, field, mine):
+    return pl.pallas_call(
+        first_kernel,
+        out_shape=jax.ShapeDtypeStruct((192, 2304), BF16),
+        in_specs=[SMEM, SMEM, VMEM, ANY],
+        out_specs=VMEM,
+        scratch_shapes=[pltpu.VMEM((3, 192, 384), BF16), pltpu.SemaphoreType.DMA((3, 2))],
+        compiler_params=pltpu.CompilerParams(vmem_limit_bytes=24 * 2**20),
+        cost_estimate=pl.CostEstimate(flops=4 * 10**8, bytes_accessed=2 * 10**6, transcendentals=0),
+    )(scale, member, field, mine)
+
+
+def filter_kernel(core, scale, member, field, first, mine, other, out, lon, lat, mid, lon_sems, lat_sems, sem):
+    lat_copies = copy_rows(other, lat, lat_sems)
+    rows = pl.ds(pl.multiple_of(core[0] * 192, 64), 192)
+    lon_copies = [pltpu.make_async_copy(first, mid.at[rows, :], sem)]
+    lon_copies[0].start()
+    for s in range(3):
+        for m, (part, half) in enumerate(((mine, core[0]), (other, 1 - core[0]))):
             for x in range(4):
                 to = pl.ds(pl.multiple_of((2 * x + half) * 96, 32), 96)
                 copy = pltpu.make_async_copy(
@@ -60,9 +84,10 @@
                 lon_copies.append(copy)
     for copy in lat_copies:
         copy.wait()
+    rows = pl.ds(pl.multiple_of((1 - core[0]) * 192, 64), 192)
     for s in range(3):
         across = jnp.dot(lat[s], field[...], preferred_element_type=F32)
-        mid[:, pl.ds(768 * s, 768)] = (scale[s] * member[0] * across).astype(BF16)
+        mid[rows, pl.ds(768 * s, 768)] = (scale[s] * member[0] * across).astype(BF16)
     for copy in lon_copies:
         copy.wait()
     total = lax.dot_general(
@@ -71,22 +96,23 @@
     out[...] = total.astype(BF16)
 
 
-def filter_pair(core, scale, member, field, mine, other):
+def filter_pair(core, scale, member, field, first, mine, other):
     return pl.pallas_call(
         filter_kernel,
         out_shape=jax.ShapeDtypeStruct((384, 768), BF16),
-        in_specs=[SMEM, SMEM, SMEM, VMEM, HBM, HBM],
+        in_specs=[SMEM, SMEM, SMEM, VMEM, VMEM, ANY, ANY],
         out_specs=VMEM,
         scratch_shapes=[
             pltpu.VMEM((768, 2304), BF16),
-            pltpu.VMEM((3, 384, 384), BF16),
+            pltpu.VMEM((3, 192, 384), BF16),
             pltpu.VMEM((384, 2304), BF16),
             pltpu.SemaphoreType.DMA((2, 3, 4)),
-            pltpu.SemaphoreType.DMA((2, 3, 2)),
+            pltpu.SemaphoreType.DMA((3, 2)),
+            pltpu.SemaphoreType.DMA,
         ],
         compiler_params=pltpu.CompilerParams(vmem_limit_bytes=40 * 2**20),
         cost_estimate=pl.CostEstimate(flops=2 * 10**9, bytes_accessed=5 * 10**6, transcendentals=0),
-    )(core, scale, member, field, mine, other)
+    )(core, scale, member, field, first, mine, other)
 
 
 def member_sum(own, back, h, r):
@@ -151,7 +177,8 @@
     field = lax.all_to_all(schur, COL, split_axis=0, concat_axis=0, tiled=True).reshape(384, 768)
     mine = lax.optimization_barrier((mine, field))[0]
     other = lax.ppermute(mine, "c", SWAP)
-    filtered = filter_pair(core, scale_weights, weight, field, mine, other).reshape(64, 2, 2304)
+    first = filter_first(scale_weights, weight, field, mine)
+    filtered = filter_pair(core, scale_weights, weight, field, first, mine, other).reshape(64, 2, 2304)
     back = lax.all_to_all(filtered, ("c", "zl", "y"), split_axis=0, concat_axis=0, tiled=True)
     total = final_sum(side, own, back.reshape(2, 4, 8, 6, 768))
     return total.transpose(1, 0, 2)

time: 137 us -> 134 us (0.978)
  waiting for transfers between devices: 14.5 us -> 10.7 us
    ppermute x1, waiting for transfers between devices: 4.35 us -> 0.66 us  [on_device(): other = lax.ppermute(mine, 'c', SWAP)]
    pallas_call x0 -> x1, Pallas kernels: none -> 2 us  [filter_first(): pl.pallas_call(first_kernel, out_shape=jax.ShapeDtypeStruct((192, 2304),...]
  transfers between devices with their start and end apart: 6 -> 6, of which waited for: 3 -> 3; matrix products, arithmetic and copies ran while one was open for 2% -> 2% of each run, Pallas kernels for 0% -> 2%
where the time goes in v13:
time: 134 us; the launch traced here: 131 us
  blocking collectives  67.2 us (50%)
  starting transfers between devices  25.9 us (19%)
  between operations  13.5 us (10%)
  waiting for transfers between devices  10.7 us (8%)
  Pallas kernels  8.97 us (7%)
  local copies, waits for them, and re-layouts  4.96 us (4%)
    all_to_all x1, blocking collectives, on_device(): lax.all_to_all(filtered, ('c', 'zl', 'y'), split_axis=0, concat_axis=0, t...  26.6 us
    all_to_all x1, blocking collectives, on_device(): lax.all_to_all(schur, COL, split_axis=0, concat_axis=0, tiled=True)  23 us
    all_to_all x1, blocking collectives, on_device(): lax.all_to_all(tiles, ('zl', 'y'), split_axis=0, concat_axis=0, tiled=True)  17.7 us
    ppermute x1, starting transfers between devices, on_device(): block = lax.ppermute(lon_filter, ('zh', 'zl', 'c'), pairs)  12.2 us
    all_to_all x1, waiting for transfers between devices, on_device(): own = lax.all_to_all(own, 'x', split_axis=0, concat_axis=0, tiled=True)  6.29 us
    ppermute x1, starting transfers between devices, final_sum(): lax.ppermute(send, 'zh', SWAP)  5.38 us
    pallas_call x1, Pallas kernels, filter_pair(): pl.pallas_call(filter_kernel, out_shape=jax.ShapeDtypeStruct((384, 768),...  4.43 us
    all_to_all x1, starting transfers between devices, on_device(): own = lax.all_to_all(own, 'x', split_axis=0, concat_axis=0, tiled=True)  4.01 us
  transfers between devices with their start and end apart: 6, of which 3 were waited for; matrix products, arithmetic and copies ran while one was open for 2% of the time, Pallas kernels for 2%

profile of v13, /device:TPU:1, one launch (start us, length us, event | category | flops | bytes accessed | tf_op | source)
XLA Modules:
  0.0 131.4 jit_solution(7811519603758715018)
XLA Ops:
  6.5 12.2 %collective-permute-start.1 = (bf16[3,96,768]{2,1,0:T(8,128)(2,1)}, bf16[3,96,768]{2,1,0:T(8,128)(2,1)S(1)}, u32[]{:S(2)}, u32[]{:S(2)}) collective-permute-start(bf16[3,96,768]{2,1,0:T(8,128)(2,1)} %param.10), channel_id=1, source_target_pairs={{0,0},{16,16},{32,32},{48,48},{65,65},{81,81},{97,97},{113,113},{1... | collective-permute-start | bytes 1327112 | tf_op jit(solution)/shard_map/ppermute | solution.py:161
  18.7 0.7 dynamic-slice_bitcast_fusion.1
  19.5 17.7 %all_to_all.20.tiles = bf16[32,8,384]{2,1,0:T(8,128)(2,1)S(1)} all-to-all(bf16[32,8,384]{2,1,0:T(8,128)(2,1)S(1)} %broadcast_in_dim.2), channel_id=1, replica_groups=mesh['x'=4,'zh'=2,'zl'=4,'y'=8,'c'=2] {'zl','y'}, dimensions={0} | all-to-all | bytes 393216 | tf_op jit(solution)/shard_map/all_to_all | solution.py:164
  37.1 0.9 shard_map.64
  38.1 0.9 copy.10
  38.9 4.0 %all-to-all-start = ((bf16[4,6,2,8,768]{4,3,2,1,0:T(8,128)(2,1)}), bf16[4,6,2,8,768]{4,3,2,1,0:T(8,128)(2,1)S(1)}, u32[]{:S(2)}, u32[]{:S(2)}) async-start(bf16[4,6,2,8,768]{4,3,2,1,0:T(8,128)(2,1)} %bitcast.20), calls=%async_computation | async-start | bytes 1179648 | tf_op jit(solution)/shard_map/all_to_all | solution.py:169
  43.0 1.8 %collective-permute-start = (f32[1]{0:T(128)}, f32[1]{0:T(128)}, u32[]{:S(2)}, u32[]{:S(2)}) collective-permute-start(f32[1]{0:T(128)} %param.8), channel_id=1, source_target_pairs={{0,0},{16,128},{32,256},{48,384},{128,16},{144,144},{160,272},{176... | collective-permute-start | bytes 20 | tf_op jit(solution)/shard_map/ppermute | solution.py:171
  44.8 6.3 %all-to-all-done.own = bf16[4,6,2,8,768]{4,3,2,1,0:T(8,128)(2,1)S(1)} async-done(((bf16[4,6,2,8,768]{4,3,2,1,0:T(8,128)(2,1)}), bf16[4,6,2,8,768]{4,3,2,1,0:T(8,128)(2,1)S(1)}, u32[]{:S(2)}, u32[]{:S(2)}) %all-to-all-start) | async-done | bytes 589856 | tf_op jit(solution)/shard_map/all_to_all | solution.py:169
  51.2 0.2 copy.8
  51.4 0.4 reshape.30
  51.8 23.0 %all_to_all.21 = bf16[64,2,2304]{2,1,0:T(2,128)(2,1)S(1)} all-to-all(bf16[64,2,2304]{2,1,0:T(2,128)(2,1)S(1)} %reshape.30), channel_id=1, replica_groups=mesh['x'=4,'zh'=2,'zl'=4,'y'=8,'c'=2] {'zl','y','c'}, dimensions={0} | all-to-all | bytes 1179648 | tf_op jit(solution)/shard_map/all_to_all | solution.py:177
  74.8 0.4 reshape.31.field
  75.2 2.5 %collective-permute-start.2 = (bf16[4,384,768]{2,1,0:T(8,128)(2,1)}, bf16[4,384,768]{2,1,0:T(8,128)(2,1)S(1)}, u32[]{:S(2)}, u32[]{:S(2)}) collective-permute-start(bf16[4,384,768]{2,1,0:T(8,128)(2,1)} %bitcast.21), channel_id=1, source_target_pairs={{0,1},{1,0},{2,3},{3,2},{4,5},{5,4},{6,7},{7,6},{8,9},{9,8},{10,11... | collective-permute-start | bytes 7077896 | tf_op jit(solution)/shard_map/ppermute | solution.py:179
  77.8 1.7 %copy-done.1 = bf16[1536,768]{1,0:T(8,128)(2,1)S(1)} copy-done((bf16[1536,768]{1,0:T(8,128)(2,1)S(1)}, bf16[1536,768]{1,0:T(8,128)(2,1)}, u32[]{:S(2)}) %copy-start.1) | copy-done | bytes 2359320
  79.4 2.0 %shard_map.65.first = bf16[192,2304]{1,0:T(8,128)(2,1)S(1)} custom-call(f32[3]{0:T(128)S(1)} %copy-done.3, f32[1]{0:T(128)} %collective-permute-done.member, bf16[384,768]{1,0:T(8,128)(2,1)S(1)} %reshape.31.field, bf16[4,384,768]{2,1,0:T(8,128)(2,1)S(1)} %bitcast.22), custom_call_target="tpu_custom_call" | custom-call | flops 400000000 | bytes 2000000 | tf_op jit(solution)/shard_map/pallas_call | solution.py:60
  81.5 0.7 collective-permute-done.2.other
  82.1 4.4 %shard_map.66 = bf16[384,768]{1,0:T(8,128)(2,1)S(1)} custom-call(s32[1]{0:T(128)} %bitcast.4.core, f32[3]{0:T(128)S(1)} %copy-done.3, f32[1]{0:T(128)} %collective-permute-done.member, bf16[384,768]{1,0:T(8,128)(2,1)S(1)} %reshape.31.field, bf16[192,2304]{1,0:T(8,128)(2,1)S(1)} %shard_map.65.first, bf16[4,384,768]{2,1,0:T(8,128)(2,1)S(1)} %bitcast.23, ...), custom_call_target="tpu_custom_call" | custom-call | flops 2000000000 | bytes 5000000 | tf_op jit(solution)/shard_map/pallas_call | solution.py:100
  86.6 0.3 reshape.33
  86.9 26.6 %all_to_all.22 = bf16[64,2,2304]{2,1,0:T(2,128)(2,1)S(1)} all-to-all(bf16[64,2,2304]{2,1,0:T(2,128)(2,1)S(1)} %reshape.33), channel_id=1, replica_groups=mesh['x'=4,'zh'=2,'zl'=4,'y'=8,'c'=2] {'c','zl','y'}, dimensions={0} | all-to-all | bytes 1179648 | tf_op jit(solution)/shard_map/all_to_all | solution.py:182
  113.4 0.4 reshape.34.back
  113.8 0.5 shard_map.67
  114.3 5.4 %collective-permute-start.3 = (bf16[6,8,768]{2,1,0:T(8,128)(2,1)S(1)}, bf16[6,8,768]{2,1,0:T(8,128)(2,1)S(1)}, u32[]{:S(2)}, u32[]{:S(2)}) collective-permute-start(bf16[6,8,768]{2,1,0:T(8,128)(2,1)S(1)} %shard_map.67), channel_id=1, source_target_pairs={{0,64},{64,0},{1,65},{65,1},{2,66},{66,2},{3,67},{67,3},{4,68},{68... | collective-permute-start | bytes 221192 | tf_op jit(solution)/shard_map/ppermute | solution.py:154
  119.7 3.7 %collective-permute-done.3.other = bf16[6,8,768]{2,1,0:T(8,128)(2,1)S(1)} collective-permute-done((bf16[6,8,768]{2,1,0:T(8,128)(2,1)S(1)}, bf16[6,8,768]{2,1,0:T(8,128)(2,1)S(1)}, u32[]{:S(2)}, u32[]{:S(2)}) %collective-permute-start.3) | collective-permute-done | bytes 73760 | tf_op jit(solution)/shard_map/ppermute | solution.py:154
  123.4 1.1 shard_map.68
  (18 shorter events, 0.2 us)
Async XLA Ops:
  6.5 38.2 %copy-start = (f32[64,6,768]{2,0,1:T(8,128)S(1)}, f32[64,6,768]{2,0,1:T(8,128)}, u32[]{:S(2)}) copy-start(f32[64,6,768]{2,0,1:T(8,128)} %param.7) | copy-start | bytes 3538948
  6.5 68.7 %all-gather.3.cloned.1.call-start = ((), (), s32[]{:S(2)}) async-start(), calls=%async_computation.4 | async-start | bytes 2949120 | tf_op jit(solution)/shard_map/all_gather | solution.py:166
  6.5 30.6 %collective-permute-start.1 = (bf16[3,96,768]{2,1,0:T(8,128)(2,1)}, bf16[3,96,768]{2,1,0:T(8,128)(2,1)S(1)}, u32[]{:S(2)}, u32[]{:S(2)}) collective-permute-start(bf16[3,96,768]{2,1,0:T(8,128)(2,1)} %param.10), channel_id=1, source_target_pairs={{0,0},{16,16},{32,32},{48,48},{65,65},{81,81},{97,97},{113,113},{1... | collective-permute-start | bytes 1327112 | tf_op jit(solution)/shard_map/ppermute | solution.py:161
  19.4 18.6 %copy-start.4 = (bf16[1,64,6,768]{3,1,2,0:T(8,128)(2,1)S(1)}, bf16[1,64,6,768]{3,1,2,0:T(8,128)(2,1)}, u32[]{:S(2)}) copy-start(bf16[1,64,6,768]{3,1,2,0:T(8,128)(2,1)} %param.6) | copy-start | bytes 1769476
  38.9 12.2 %all-to-all-start = ((bf16[4,6,2,8,768]{4,3,2,1,0:T(8,128)(2,1)}), bf16[4,6,2,8,768]{4,3,2,1,0:T(8,128)(2,1)S(1)}, u32[]{:S(2)}, u32[]{:S(2)}) async-start(bf16[4,6,2,8,768]{4,3,2,1,0:T(8,128)(2,1)} %bitcast.20), calls=%async_computation | async-start | bytes 1179648 | tf_op jit(solution)/shard_map/all_to_all | solution.py:169
  43.0 1.8 %collective-permute-start = (f32[1]{0:T(128)}, f32[1]{0:T(128)}, u32[]{:S(2)}, u32[]{:S(2)}) collective-permute-start(f32[1]{0:T(128)} %param.8), channel_id=1, source_target_pairs={{0,0},{16,128},{32,256},{48,384},{128,16},{144,144},{160,272},{176... | collective-permute-start | bytes 20 | tf_op jit(solution)/shard_map/ppermute | solution.py:171
  51.8 25.9 %copy-start.3 = (f32[3]{0:T(128)S(1)}, f32[3]{0:T(128)}, u32[]{:S(2)}) copy-start(f32[3]{0:T(128)} %scale.3) | copy-start | bytes 40
  75.2 6.9 %collective-permute-start.2 = (bf16[4,384,768]{2,1,0:T(8,128)(2,1)}, bf16[4,384,768]{2,1,0:T(8,128)(2,1)S(1)}, u32[]{:S(2)}, u32[]{:S(2)}) collective-permute-start(bf16[4,384,768]{2,1,0:T(8,128)(2,1)} %bitcast.21), channel_id=1, source_target_pairs={{0,1},{1,0},{2,3},{3,2},{4,5},{5,4},{6,7},{7,6},{8,9},{9,8},{10,11... | collective-permute-start | bytes 7077896 | tf_op jit(solution)/shard_map/ppermute | solution.py:179
  77.8 1.7 %copy-start.1 = (bf16[1536,768]{1,0:T(8,128)(2,1)S(1)}, bf16[1536,768]{1,0:T(8,128)(2,1)}, u32[]{:S(2)}) copy-start(bf16[1536,768]{1,0:T(8,128)(2,1)} %all-gather.3.cloned.1.call-done) | copy-start | bytes 7077892
  79.4 2.7 %copy-start.2 = (bf16[1536,768]{1,0:T(8,128)(2,1)S(1)}, bf16[1536,768]{1,0:T(8,128)(2,1)}, u32[]{:S(2)}) copy-start(bf16[1536,768]{1,0:T(8,128)(2,1)} %all-gather.3.cloned.1.call-done) | copy-start | bytes 7077892
  114.3 9.1 %collective-permute-start.3 = (bf16[6,8,768]{2,1,0:T(8,128)(2,1)S(1)}, bf16[6,8,768]{2,1,0:T(8,128)(2,1)S(1)}, u32[]{:S(2)}, u32[]{:S(2)}) collective-permute-start(bf16[6,8,768]{2,1,0:T(8,128)(2,1)S(1)} %shard_map.67), channel_id=1, source_target_pairs={{0,64},{64,0},{1,65},{65,1},{2,66},{66,2},{3,67},{67,3},{4,68},{68... | collective-permute-start | bytes 221192 | tf_op jit(solution)/shard_map/ppermute | solution.py:154
Sparse Core Ops, SparseCore 0:
  38.2 33.2 all-gather.2

commit v14 on v13

--- a/solution.py
+++ b/solution.py
@@ -19,10 +19,7 @@
 def pack_kernel(block, tiles, out):
     out[pl.ds(0, 288), :] = block[...]
     for half in range(2):
-        for part in range(4):
-            first = 16 * half + 4 * part
-            rows = [tiles[first + n, :6, :].astype(F32) for n in range(4)]
-            out[pl.ds(288 + 24 * part, 24), pl.ds(384 * half, 384)] = jnp.concatenate(rows, axis=0).astype(BF16)
+        out[pl.ds(288, 96), pl.ds(384 * half, 384)] = tiles[pl.ds(96 * half, 96), :]
 
 
 def pack(block, tiles):
@@ -160,8 +157,8 @@
     pairs += [(8 * h + 2 * z + 1 - h, 8 * (1 - h) + 2 * (3 - z) + h) for h in range(2) for z in range(4)]
     block = lax.ppermute(lon_filter, ("zh", "zl", "c"), pairs)
     rows = lax.dynamic_index_in_dim(lat_filter, jnp.minimum(x, 2), 0, False)
-    tiles = jnp.broadcast_to(jnp.pad(rows, ((0, 2), (0, 0)))[None], (32, 8, 384))
-    tiles = lax.all_to_all(tiles, ("zl", "y"), split_axis=0, concat_axis=0, tiled=True)
+    tiles = jnp.broadcast_to(rows.reshape(1, 2, 1152), (32, 2, 1152))
+    tiles = lax.all_to_all(tiles, ("zl", "y"), split_axis=0, concat_axis=0, tiled=True).reshape(192, 384)
     packed = pack(block.reshape(288, 768), tiles)
     mine = lax.all_gather(packed, "x", axis=0)
 

time: 134 us -> 133 us (level)
  no operation moved by 1% of the time
where the time goes in v14:
time: 133 us; the launch traced here: 131 us
  blocking collectives  66.2 us (50%)
  starting transfers between devices  25.8 us (19%)
  between operations  13.6 us (10%)
  waiting for transfers between devices  11 us (8%)
  Pallas kernels  8.94 us (7%)
  local copies, waits for them, and re-layouts  5.14 us (4%)
    all_to_all x1, blocking collectives, on_device(): lax.all_to_all(filtered, ('c', 'zl', 'y'), split_axis=0, concat_axis=0, t...  26.2 us
    all_to_all x1, blocking collectives, on_device(): lax.all_to_all(schur, COL, split_axis=0, concat_axis=0, tiled=True)  22.6 us
    all_to_all x1, blocking collectives, on_device(): lax.all_to_all(tiles, ('zl', 'y'), split_axis=0, concat_axis=0, tiled=True)  17.5 us
    ppermute x1, starting transfers between devices, on_device(): block = lax.ppermute(lon_filter, ('zh', 'zl', 'c'), pairs)  12.2 us
    all_to_all x1, waiting for transfers between devices, on_device(): own = lax.all_to_all(own, 'x', split_axis=0, concat_axis=0, tiled=True)  6.39 us
    ppermute x1, starting transfers between devices, final_sum(): lax.ppermute(send, 'zh', SWAP)  5.24 us
    pallas_call x1, Pallas kernels, filter_pair(): pl.pallas_call(filter_kernel, out_shape=jax.ShapeDtypeStruct((384, 768),...  4.43 us
    all_to_all x1, starting transfers between devices, on_device(): own = lax.all_to_all(own, 'x', split_axis=0, concat_axis=0, tiled=True)  4.01 us
  transfers between devices with their start and end apart: 6, of which 3 were waited for; matrix products, arithmetic and copies ran while one was open for 2% of the time, Pallas kernels for 2%

profile of v14, /device:TPU:1, one launch (start us, length us, event | category | flops | bytes accessed | tf_op | source)
XLA Modules:
  0.0 130.7 jit_solution(2323939032829381424)
XLA Ops:
  6.5 12.2 %collective-permute-start.1 = (bf16[3,96,768]{2,1,0:T(8,128)(2,1)}, bf16[3,96,768]{2,1,0:T(8,128)(2,1)S(1)}, u32[]{:S(2)}, u32[]{:S(2)}) collective-permute-start(bf16[3,96,768]{2,1,0:T(8,128)(2,1)} %param.10), channel_id=1, source_target_pairs={{0,0},{16,16},{32,32},{48,48},{65,65},{81,81},{97,97},{113,113},{1... | collective-permute-start | bytes 1327112 | tf_op jit(solution)/shard_map/ppermute | solution.py:158
  18.7 0.7 constant_dynamic-slice_fusion
  19.5 17.5 %all_to_all.20 = bf16[32,2,1152]{2,1,0:T(2,128)(2,1)S(1)} all-to-all(bf16[32,2,1152]{2,1,0:T(2,128)(2,1)S(1)} %broadcast_in_dim.8), channel_id=1, replica_groups=mesh['x'=4,'zh'=2,'zl'=4,'y'=8,'c'=2] {'zl','y'}, dimensions={0} | all-to-all | bytes 294912 | tf_op jit(solution)/shard_map/all_to_all | solution.py:161
  37.1 0.9 shard_map.64
  38.0 0.9 copy.10
  38.9 4.0 %all-to-all-start = ((bf16[4,6,2,8,768]{4,3,2,1,0:T(8,128)(2,1)}), bf16[4,6,2,8,768]{4,3,2,1,0:T(8,128)(2,1)S(1)}, u32[]{:S(2)}, u32[]{:S(2)}) async-start(bf16[4,6,2,8,768]{4,3,2,1,0:T(8,128)(2,1)} %bitcast.18), calls=%async_computation | async-start | bytes 1179648 | tf_op jit(solution)/shard_map/all_to_all | solution.py:166
  42.9 1.8 %collective-permute-start = (f32[1]{0:T(128)}, f32[1]{0:T(128)}, u32[]{:S(2)}, u32[]{:S(2)}) collective-permute-start(f32[1]{0:T(128)} %param.8), channel_id=1, source_target_pairs={{0,0},{16,128},{32,256},{48,384},{128,16},{144,144},{160,272},{176... | collective-permute-start | bytes 20 | tf_op jit(solution)/shard_map/ppermute | solution.py:168
  44.8 6.4 %all-to-all-done.own = bf16[4,6,2,8,768]{4,3,2,1,0:T(8,128)(2,1)S(1)} async-done(((bf16[4,6,2,8,768]{4,3,2,1,0:T(8,128)(2,1)}), bf16[4,6,2,8,768]{4,3,2,1,0:T(8,128)(2,1)S(1)}, u32[]{:S(2)}, u32[]{:S(2)}) %all-to-all-start) | async-done | bytes 589856 | tf_op jit(solution)/shard_map/all_to_all | solution.py:166
  51.3 0.2 copy.8
  51.5 0.4 reshape.35
  51.9 22.6 %all_to_all.21 = bf16[64,2,2304]{2,1,0:T(2,128)(2,1)S(1)} all-to-all(bf16[64,2,2304]{2,1,0:T(2,128)(2,1)S(1)} %reshape.35), channel_id=1, replica_groups=mesh['x'=4,'zh'=2,'zl'=4,'y'=8,'c'=2] {'zl','y','c'}, dimensions={0} | all-to-all | bytes 1179648 | tf_op jit(solution)/shard_map/all_to_all | solution.py:174
  74.5 0.4 reshape.36.field
  74.9 2.5 %collective-permute-start.2 = (bf16[4,384,768]{2,1,0:T(8,128)(2,1)}, bf16[4,384,768]{2,1,0:T(8,128)(2,1)S(1)}, u32[]{:S(2)}, u32[]{:S(2)}) collective-permute-start(bf16[4,384,768]{2,1,0:T(8,128)(2,1)} %bitcast.19), channel_id=1, source_target_pairs={{0,1},{1,0},{2,3},{3,2},{4,5},{5,4},{6,7},{7,6},{8,9},{9,8},{10,11... | collective-permute-start | bytes 7077896 | tf_op jit(solution)/shard_map/ppermute | solution.py:176
  77.4 1.7 %copy-done.1 = bf16[1536,768]{1,0:T(8,128)(2,1)S(1)} copy-done((bf16[1536,768]{1,0:T(8,128)(2,1)S(1)}, bf16[1536,768]{1,0:T(8,128)(2,1)}, u32[]{:S(2)}) %copy-start.1) | copy-done | bytes 2359320
  79.1 2.0 %shard_map.65.first = bf16[192,2304]{1,0:T(8,128)(2,1)S(1)} custom-call(f32[3]{0:T(128)S(1)} %copy-done.3, f32[1]{0:T(128)} %collective-permute-done.member, bf16[384,768]{1,0:T(8,128)(2,1)S(1)} %reshape.36.field, bf16[4,384,768]{2,1,0:T(8,128)(2,1)S(1)} %bitcast.20), custom_call_target="tpu_custom_call" | custom-call | flops 400000000 | bytes 2000000 | tf_op jit(solution)/shard_map/pallas_call | solution.py:57
  81.1 0.7 collective-permute-done.2.other
  81.8 4.4 %shard_map.66 = bf16[384,768]{1,0:T(8,128)(2,1)S(1)} custom-call(s32[1]{0:T(128)} %bitcast.4.core, f32[3]{0:T(128)S(1)} %copy-done.3, f32[1]{0:T(128)} %collective-permute-done.member, bf16[384,768]{1,0:T(8,128)(2,1)S(1)} %reshape.36.field, bf16[192,2304]{1,0:T(8,128)(2,1)S(1)} %shard_map.65.first, bf16[4,384,768]{2,1,0:T(8,128)(2,1)S(1)} %bitcast.21, ...), custom_call_target="tpu_custom_call" | custom-call | flops 2000000000 | bytes 5000000 | tf_op jit(solution)/shard_map/pallas_call | solution.py:97
  86.2 0.3 reshape.39
  86.5 26.2 %all_to_all.22 = bf16[64,2,2304]{2,1,0:T(2,128)(2,1)S(1)} all-to-all(bf16[64,2,2304]{2,1,0:T(2,128)(2,1)S(1)} %reshape.39), channel_id=1, replica_groups=mesh['x'=4,'zh'=2,'zl'=4,'y'=8,'c'=2] {'c','zl','y'}, dimensions={0} | all-to-all | bytes 1179648 | tf_op jit(solution)/shard_map/all_to_all | solution.py:179
  112.7 0.4 reshape.40.back
  113.1 0.5 shard_map.67
  113.6 5.2 %collective-permute-start.3 = (bf16[6,8,768]{2,1,0:T(8,128)(2,1)S(1)}, bf16[6,8,768]{2,1,0:T(8,128)(2,1)S(1)}, u32[]{:S(2)}, u32[]{:S(2)}) collective-permute-start(bf16[6,8,768]{2,1,0:T(8,128)(2,1)S(1)} %shard_map.67), channel_id=1, source_target_pairs={{0,64},{64,0},{1,65},{65,1},{2,66},{66,2},{3,67},{67,3},{4,68},{68... | collective-permute-start | bytes 221192 | tf_op jit(solution)/shard_map/ppermute | solution.py:151
  118.8 3.9 %collective-permute-done.3.other = bf16[6,8,768]{2,1,0:T(8,128)(2,1)S(1)} collective-permute-done((bf16[6,8,768]{2,1,0:T(8,128)(2,1)S(1)}, bf16[6,8,768]{2,1,0:T(8,128)(2,1)S(1)}, u32[]{:S(2)}, u32[]{:S(2)}) %collective-permute-start.3) | collective-permute-done | bytes 73760 | tf_op jit(solution)/shard_map/ppermute | solution.py:151
  122.7 1.1 shard_map.68
  (19 shorter events, 0.4 us)
Async XLA Ops:
  6.5 38.2 %copy-start = (f32[64,6,768]{2,0,1:T(8,128)S(1)}, f32[64,6,768]{2,0,1:T(8,128)}, u32[]{:S(2)}) copy-start(f32[64,6,768]{2,0,1:T(8,128)} %param.7) | copy-start | bytes 3538948
  6.5 68.3 %all-gather.3.cloned.1.call-start = ((), (), s32[]{:S(2)}) async-start(), calls=%async_computation.4 | async-start | bytes 2949120 | tf_op jit(solution)/shard_map/all_gather | solution.py:163
  6.5 30.6 %collective-permute-start.1 = (bf16[3,96,768]{2,1,0:T(8,128)(2,1)}, bf16[3,96,768]{2,1,0:T(8,128)(2,1)S(1)}, u32[]{:S(2)}, u32[]{:S(2)}) collective-permute-start(bf16[3,96,768]{2,1,0:T(8,128)(2,1)} %param.10), channel_id=1, source_target_pairs={{0,0},{16,16},{32,32},{48,48},{65,65},{81,81},{97,97},{113,113},{1... | collective-permute-start | bytes 1327112 | tf_op jit(solution)/shard_map/ppermute | solution.py:158
  19.5 18.5 %copy-start.4 = (bf16[1,64,6,768]{3,1,2,0:T(8,128)(2,1)S(1)}, bf16[1,64,6,768]{3,1,2,0:T(8,128)(2,1)}, u32[]{:S(2)}) copy-start(bf16[1,64,6,768]{3,1,2,0:T(8,128)(2,1)} %param.6) | copy-start | bytes 1769476
  38.9 12.3 %all-to-all-start = ((bf16[4,6,2,8,768]{4,3,2,1,0:T(8,128)(2,1)}), bf16[4,6,2,8,768]{4,3,2,1,0:T(8,128)(2,1)S(1)}, u32[]{:S(2)}, u32[]{:S(2)}) async-start(bf16[4,6,2,8,768]{4,3,2,1,0:T(8,128)(2,1)} %bitcast.18), calls=%async_computation | async-start | bytes 1179648 | tf_op jit(solution)/shard_map/all_to_all | solution.py:166
  42.9 1.8 %collective-permute-start = (f32[1]{0:T(128)}, f32[1]{0:T(128)}, u32[]{:S(2)}, u32[]{:S(2)}) collective-permute-start(f32[1]{0:T(128)} %param.8), channel_id=1, source_target_pairs={{0,0},{16,128},{32,256},{48,384},{128,16},{144,144},{160,272},{176... | collective-permute-start | bytes 20 | tf_op jit(solution)/shard_map/ppermute | solution.py:168
  51.9 25.5 %copy-start.3 = (f32[3]{0:T(128)S(1)}, f32[3]{0:T(128)}, u32[]{:S(2)}) copy-start(f32[3]{0:T(128)} %scale.3) | copy-start | bytes 40
  74.9 6.9 %collective-permute-start.2 = (bf16[4,384,768]{2,1,0:T(8,128)(2,1)}, bf16[4,384,768]{2,1,0:T(8,128)(2,1)S(1)}, u32[]{:S(2)}, u32[]{:S(2)}) collective-permute-start(bf16[4,384,768]{2,1,0:T(8,128)(2,1)} %bitcast.19), channel_id=1, source_target_pairs={{0,1},{1,0},{2,3},{3,2},{4,5},{5,4},{6,7},{7,6},{8,9},{9,8},{10,11... | collective-permute-start | bytes 7077896 | tf_op jit(solution)/shard_map/ppermute | solution.py:176
  77.4 1.7 %copy-start.1 = (bf16[1536,768]{1,0:T(8,128)(2,1)S(1)}, bf16[1536,768]{1,0:T(8,128)(2,1)}, u32[]{:S(2)}) copy-start(bf16[1536,768]{1,0:T(8,128)(2,1)} %all-gather.3.cloned.1.call-done) | copy-start | bytes 7077892
  79.1 2.7 %copy-start.2 = (bf16[1536,768]{1,0:T(8,128)(2,1)S(1)}, bf16[1536,768]{1,0:T(8,128)(2,1)}, u32[]{:S(2)}) copy-start(bf16[1536,768]{1,0:T(8,128)(2,1)} %all-gather.3.cloned.1.call-done) | copy-start | bytes 7077892
  113.6 9.1 %collective-permute-start.3 = (bf16[6,8,768]{2,1,0:T(8,128)(2,1)S(1)}, bf16[6,8,768]{2,1,0:T(8,128)(2,1)S(1)}, u32[]{:S(2)}, u32[]{:S(2)}) collective-permute-start(bf16[6,8,768]{2,1,0:T(8,128)(2,1)S(1)} %shard_map.67), channel_id=1, source_target_pairs={{0,64},{64,0},{1,65},{65,1},{2,66},{66,2},{3,67},{67,3},{4,68},{68... | collective-permute-start | bytes 221192 | tf_op jit(solution)/shard_map/ppermute | solution.py:151
Sparse Core Ops, SparseCore 0:
  38.1 32.5 all-gather.2

commit v15 on v14

--- a/solution.py
+++ b/solution.py
@@ -159,10 +159,11 @@
     rows = lax.dynamic_index_in_dim(lat_filter, jnp.minimum(x, 2), 0, False)
     tiles = jnp.broadcast_to(rows.reshape(1, 2, 1152), (32, 2, 1152))
     tiles = lax.all_to_all(tiles, ("zl", "y"), split_axis=0, concat_axis=0, tiled=True).reshape(192, 384)
+    own = perturbations[0].transpose(1, 0, 2).reshape(6, 4, 2, 8, 768).transpose(1, 0, 2, 3, 4)
+    own, block = lax.optimization_barrier((own, block))
     packed = pack(block.reshape(288, 768), tiles)
     mine = lax.all_gather(packed, "x", axis=0)
 
-    own = perturbations[0].transpose(1, 0, 2).reshape(6, 4, 2, 8, 768).transpose(1, 0, 2, 3, 4)
     own = lax.all_to_all(own, "x", split_axis=0, concat_axis=0, tiled=True)
     turn = [(4 * a + b, 4 * b + a) for a in range(4) for b in range(4)]
     weight = lax.ppermute(member_weights, ("x", "zl"), turn)

time: 133 us -> 134 us (level)
  blocking collectives: 66.2 us -> 49.6 us
  starting transfers between devices: 25.8 us -> 33.8 us
  waiting for transfers between devices: 11 us -> 18.5 us
  local copies, waits for them, and re-layouts: 5.14 us -> 6.86 us
    all_to_all x1 -> x0, blocking collectives: 17.5 us -> none  [on_device(): lax.all_to_all(tiles, ('zl', 'y'), split_axis=0, concat_axis=0, tiled=True)]
    all_to_all x0 -> x1, starting transfers between devices: none -> 8.1 us  [on_device(): lax.all_to_all(tiles, ('zl', 'y'), split_axis=0, concat_axis=0, tiled=True)]
    all_to_all x0 -> x1, waiting for transfers between devices: none -> 7.46 us  [on_device(): lax.all_to_all(tiles, ('zl', 'y'), split_axis=0, concat_axis=0, tiled=True)]
  transfers between devices with their start and end apart: 6 -> 7, of which waited for: 3 -> 4; matrix products, arithmetic and copies ran while one was open for 2% -> 3% of each run, Pallas kernels for 2% -> 2%
where the time goes in v15:
time: 134 us; the launch traced here: 131 us
  blocking collectives  49.6 us (37%)
  starting transfers between devices  33.8 us (25%)
  waiting for transfers between devices  18.5 us (14%)
  between operations  13.6 us (10%)
  Pallas kernels  9.02 us (7%)
  local copies, waits for them, and re-layouts  6.86 us (5%)
    all_to_all x1, blocking collectives, on_device(): lax.all_to_all(filtered, ('c', 'zl', 'y'), split_axis=0, concat_axis=0, t...  27 us
    all_to_all x1, blocking collectives, on_device(): lax.all_to_all(schur, COL, split_axis=0, concat_axis=0, tiled=True)  22.6 us
    ppermute x1, starting transfers between devices, on_device(): block = lax.ppermute(lon_filter, ('zh', 'zl', 'c'), pairs)  12.2 us
    all_to_all x1, starting transfers between devices, on_device(): lax.all_to_all(tiles, ('zl', 'y'), split_axis=0, concat_axis=0, tiled=True)  8.1 us
    all_to_all x1, waiting for transfers between devices, on_device(): lax.all_to_all(tiles, ('zl', 'y'), split_axis=0, concat_axis=0, tiled=True)  7.46 us
    all_to_all x1, waiting for transfers between devices, on_device(): own = lax.all_to_all(own, 'x', split_axis=0, concat_axis=0, tiled=True)  6.34 us
    ppermute x1, starting transfers between devices, final_sum(): lax.ppermute(send, 'zh', SWAP)  5.03 us
    pallas_call x1, Pallas kernels, filter_pair(): pl.pallas_call(filter_kernel, out_shape=jax.ShapeDtypeStruct((384, 768),...  4.48 us
  transfers between devices with their start and end apart: 7, of which 4 were waited for; matrix products, arithmetic and copies ran while one was open for 3% of the time, Pallas kernels for 2%

profile of v15, /device:TPU:1, one launch (start us, length us, event | category | flops | bytes accessed | tf_op | source)
XLA Modules:
  0.0 131.4 jit_solution(6213869749189088525)
XLA Ops:
  6.5 12.2 %collective-permute-start = (bf16[3,96,768]{2,1,0:T(8,128)(2,1)}, bf16[3,96,768]{2,1,0:T(8,128)(2,1)S(1)}, u32[]{:S(2)}, u32[]{:S(2)}) collective-permute-start(bf16[3,96,768]{2,1,0:T(8,128)(2,1)} %param.10), channel_id=1, source_target_pairs={{0,0},{16,16},{32,32},{48,48},{65,65},{81,81},{97,97},{113,113},{1... | collective-permute-start | bytes 1327112 | tf_op jit(solution)/shard_map/ppermute | solution.py:158
  18.7 0.7 constant_dynamic-slice_fusion
  19.4 0.7 broadcast_in_dim.8
  20.2 8.1 %all-to-all-start.2 = ((bf16[32,2,1152]{2,1,0:T(2,128)(2,1)}), bf16[32,2,1152]{2,1,0:T(2,128)(2,1)S(1)}, u32[]{:S(2)}, u32[]{:S(2)}) async-start(bf16[32,2,1152]{2,1,0:T(2,128)(2,1)} %broadcast_in_dim.8), calls=%async_computation.2 | async-start | bytes 294912 | tf_op jit(solution)/shard_map/all_to_all | solution.py:161
  28.3 1.9 %copy.10 = bf16[6,4,2,8,768]{4,3,2,0,1:T(8,128)(2,1)} copy(bf16[6,4,2,8,768]{4,3,2,1,0:T(8,128)(2,1)} %bitcast.23) | data formatting | bytes 1179648 | tf_op jit(solution)/shard_map/reshape | solution.py:162
  30.3 7.5 %all-to-all-done.2 = bf16[32,2,1152]{2,1,0:T(2,128)(2,1)S(1)} async-done(((bf16[32,2,1152]{2,1,0:T(2,128)(2,1)}), bf16[32,2,1152]{2,1,0:T(2,128)(2,1)S(1)}, u32[]{:S(2)}, u32[]{:S(2)}) %all-to-all-start.2) | async-done | bytes 147488 | tf_op jit(solution)/shard_map/all_to_all | solution.py:161
  37.8 0.9 shard_map.64
  38.7 4.0 %all-to-all-start = ((bf16[4,6,2,8,768]{4,3,2,1,0:T(8,128)(2,1)}), bf16[4,6,2,8,768]{4,3,2,1,0:T(8,128)(2,1)S(1)}, u32[]{:S(2)}, u32[]{:S(2)}) async-start(bf16[4,6,2,8,768]{4,3,2,1,0:T(8,128)(2,1)} %bitcast.18), calls=%async_computation | async-start | bytes 1179648 | tf_op jit(solution)/shard_map/all_to_all | solution.py:167
  42.8 1.9 %collective-permute-start.1 = (f32[1]{0:T(128)}, f32[1]{0:T(128)}, u32[]{:S(2)}, u32[]{:S(2)}) collective-permute-start(f32[1]{0:T(128)} %param.8), channel_id=1, source_target_pairs={{0,0},{16,128},{32,256},{48,384},{128,16},{144,144},{160,272},{176... | collective-permute-start | bytes 20 | tf_op jit(solution)/shard_map/ppermute | solution.py:169
  44.7 6.3 %all-to-all-done.own = bf16[4,6,2,8,768]{4,3,2,1,0:T(8,128)(2,1)S(1)} async-done(((bf16[4,6,2,8,768]{4,3,2,1,0:T(8,128)(2,1)}), bf16[4,6,2,8,768]{4,3,2,1,0:T(8,128)(2,1)S(1)}, u32[]{:S(2)}, u32[]{:S(2)}) %all-to-all-start) | async-done | bytes 589856 | tf_op jit(solution)/shard_map/all_to_all | solution.py:167
  51.3 0.4 reshape.35
  51.7 22.6 %all_to_all.20 = bf16[64,2,2304]{2,1,0:T(2,128)(2,1)S(1)} all-to-all(bf16[64,2,2304]{2,1,0:T(2,128)(2,1)S(1)} %reshape.35), channel_id=1, replica_groups=mesh['x'=4,'zh'=2,'zl'=4,'y'=8,'c'=2] {'zl','y','c'}, dimensions={0} | all-to-all | bytes 1179648 | tf_op jit(solution)/shard_map/all_to_all | solution.py:175
  74.3 0.4 reshape.36.field
  74.7 2.5 %collective-permute-start.2 = (bf16[4,384,768]{2,1,0:T(8,128)(2,1)}, bf16[4,384,768]{2,1,0:T(8,128)(2,1)S(1)}, u32[]{:S(2)}, u32[]{:S(2)}) collective-permute-start(bf16[4,384,768]{2,1,0:T(8,128)(2,1)} %bitcast.19), channel_id=1, source_target_pairs={{0,1},{1,0},{2,3},{3,2},{4,5},{5,4},{6,7},{7,6},{8,9},{9,8},{10,11... | collective-permute-start | bytes 7077896 | tf_op jit(solution)/shard_map/ppermute | solution.py:177
  77.3 1.7 %copy-done.1 = bf16[1536,768]{1,0:T(8,128)(2,1)S(1)} copy-done((bf16[1536,768]{1,0:T(8,128)(2,1)S(1)}, bf16[1536,768]{1,0:T(8,128)(2,1)}, u32[]{:S(2)}) %copy-start.1) | copy-done | bytes 2359320
  79.0 2.1 %shard_map.65.first = bf16[192,2304]{1,0:T(8,128)(2,1)S(1)} custom-call(f32[3]{0:T(128)S(1)} %copy-done.3, f32[1]{0:T(128)} %collective-permute-done.1.member, bf16[384,768]{1,0:T(8,128)(2,1)S(1)} %reshape.36.field, bf16[4,384,768]{2,1,0:T(8,128)(2,1)S(1)} %bitcast.20), custom_call_target="tpu_custom_call" | custom-call | flops 400000000 | bytes 2000000 | tf_op jit(solution)/shard_map/pallas_call | solution.py:57
  81.0 0.6 collective-permute-done.2.other
  81.6 4.5 %shard_map.66 = bf16[384,768]{1,0:T(8,128)(2,1)S(1)} custom-call(s32[1]{0:T(128)} %bitcast.4.core, f32[3]{0:T(128)S(1)} %copy-done.3, f32[1]{0:T(128)} %collective-permute-done.1.member, bf16[384,768]{1,0:T(8,128)(2,1)S(1)} %reshape.36.field, bf16[192,2304]{1,0:T(8,128)(2,1)S(1)} %shard_map.65.first, bf16[4,384,768]{2,1,0:T(8,128)(2,1)S(1)} %bitcast.21, ...), custom_call_target="tpu_custom_call" | custom-call | flops 2000000000 | bytes 5000000 | tf_op jit(solution)/shard_map/pallas_call | solution.py:97
  86.4 27.0 %all_to_all.21 = bf16[64,2,2304]{2,1,0:T(2,128)(2,1)S(1)} all-to-all(bf16[64,2,2304]{2,1,0:T(2,128)(2,1)S(1)} %reshape.39), channel_id=1, replica_groups=mesh['x'=4,'zh'=2,'zl'=4,'y'=8,'c'=2] {'c','zl','y'}, dimensions={0} | all-to-all | bytes 1179648 | tf_op jit(solution)/shard_map/all_to_all | solution.py:180
  113.4 0.4 reshape.40.back
  113.8 0.5 shard_map.67
  114.3 5.0 %collective-permute-start.3 = (bf16[6,8,768]{2,1,0:T(8,128)(2,1)S(1)}, bf16[6,8,768]{2,1,0:T(8,128)(2,1)S(1)}, u32[]{:S(2)}, u32[]{:S(2)}) collective-permute-start(bf16[6,8,768]{2,1,0:T(8,128)(2,1)S(1)} %shard_map.67), channel_id=1, source_target_pairs={{0,64},{64,0},{1,65},{65,1},{2,66},{66,2},{3,67},{67,3},{4,68},{68... | collective-permute-start | bytes 221192 | tf_op jit(solution)/shard_map/ppermute | solution.py:151
  119.4 4.1 %collective-permute-done.3.other = bf16[6,8,768]{2,1,0:T(8,128)(2,1)S(1)} collective-permute-done((bf16[6,8,768]{2,1,0:T(8,128)(2,1)S(1)}, bf16[6,8,768]{2,1,0:T(8,128)(2,1)S(1)}, u32[]{:S(2)}, u32[]{:S(2)}) %collective-permute-start.3) | collective-permute-done | bytes 73760 | tf_op jit(solution)/shard_map/ppermute | solution.py:151
  123.4 1.1 shard_map.68
  (18 shorter events, 0.8 us)
Async XLA Ops:
  6.5 38.1 %copy-start = (f32[64,6,768]{2,0,1:T(8,128)S(1)}, f32[64,6,768]{2,0,1:T(8,128)}, u32[]{:S(2)}) copy-start(f32[64,6,768]{2,0,1:T(8,128)} %param.7) | copy-start | bytes 3538948
  6.5 31.3 %collective-permute-start = (bf16[3,96,768]{2,1,0:T(8,128)(2,1)}, bf16[3,96,768]{2,1,0:T(8,128)(2,1)S(1)}, u32[]{:S(2)}, u32[]{:S(2)}) collective-permute-start(bf16[3,96,768]{2,1,0:T(8,128)(2,1)} %param.10), channel_id=1, source_target_pairs={{0,0},{16,16},{32,32},{48,48},{65,65},{81,81},{97,97},{113,113},{1... | collective-permute-start | bytes 1327112 | tf_op jit(solution)/shard_map/ppermute | solution.py:158
  20.2 17.5 %all-to-all-start.2 = ((bf16[32,2,1152]{2,1,0:T(2,128)(2,1)}), bf16[32,2,1152]{2,1,0:T(2,128)(2,1)S(1)}, u32[]{:S(2)}, u32[]{:S(2)}) async-start(bf16[32,2,1152]{2,1,0:T(2,128)(2,1)} %broadcast_in_dim.8), calls=%async_computation.2 | async-start | bytes 294912 | tf_op jit(solution)/shard_map/all_to_all | solution.py:161
  28.3 46.4 %all-gather.3.cloned.1.call-start = ((), (), s32[]{:S(2)}) async-start(), calls=%async_computation.4 | async-start | bytes 2949120 | tf_op jit(solution)/shard_map/all_gather | solution.py:165
  38.7 12.3 %all-to-all-start = ((bf16[4,6,2,8,768]{4,3,2,1,0:T(8,128)(2,1)}), bf16[4,6,2,8,768]{4,3,2,1,0:T(8,128)(2,1)S(1)}, u32[]{:S(2)}, u32[]{:S(2)}) async-start(bf16[4,6,2,8,768]{4,3,2,1,0:T(8,128)(2,1)} %bitcast.18), calls=%async_computation | async-start | bytes 1179648 | tf_op jit(solution)/shard_map/all_to_all | solution.py:167
  42.8 1.9 %collective-permute-start.1 = (f32[1]{0:T(128)}, f32[1]{0:T(128)}, u32[]{:S(2)}, u32[]{:S(2)}) collective-permute-start(f32[1]{0:T(128)} %param.8), channel_id=1, source_target_pairs={{0,0},{16,128},{32,256},{48,384},{128,16},{144,144},{160,272},{176... | collective-permute-start | bytes 20 | tf_op jit(solution)/shard_map/ppermute | solution.py:169
  51.7 25.6 %copy-start.3 = (f32[3]{0:T(128)S(1)}, f32[3]{0:T(128)}, u32[]{:S(2)}) copy-start(f32[3]{0:T(128)} %scale.3) | copy-start | bytes 40
  74.7 6.9 %collective-permute-start.2 = (bf16[4,384,768]{2,1,0:T(8,128)(2,1)}, bf16[4,384,768]{2,1,0:T(8,128)(2,1)S(1)}, u32[]{:S(2)}, u32[]{:S(2)}) collective-permute-start(bf16[4,384,768]{2,1,0:T(8,128)(2,1)} %bitcast.19), channel_id=1, source_target_pairs={{0,1},{1,0},{2,3},{3,2},{4,5},{5,4},{6,7},{7,6},{8,9},{9,8},{10,11... | collective-permute-start | bytes 7077896 | tf_op jit(solution)/shard_map/ppermute | solution.py:177
  77.3 1.7 %copy-start.1 = (bf16[1536,768]{1,0:T(8,128)(2,1)S(1)}, bf16[1536,768]{1,0:T(8,128)(2,1)}, u32[]{:S(2)}) copy-start(bf16[1536,768]{1,0:T(8,128)(2,1)} %all-gather.3.cloned.1.call-done) | copy-start | bytes 7077892
  79.0 2.7 %copy-start.2 = (bf16[1536,768]{1,0:T(8,128)(2,1)S(1)}, bf16[1536,768]{1,0:T(8,128)(2,1)}, u32[]{:S(2)}) copy-start(bf16[1536,768]{1,0:T(8,128)(2,1)} %all-gather.3.cloned.1.call-done) | copy-start | bytes 7077892
  114.3 9.1 %collective-permute-start.3 = (bf16[6,8,768]{2,1,0:T(8,128)(2,1)S(1)}, bf16[6,8,768]{2,1,0:T(8,128)(2,1)S(1)}, u32[]{:S(2)}, u32[]{:S(2)}) collective-permute-start(bf16[6,8,768]{2,1,0:T(8,128)(2,1)S(1)} %shard_map.67), channel_id=1, source_target_pairs={{0,64},{64,0},{1,65},{65,1},{2,66},{66,2},{3,67},{67,3},{4,68},{68... | collective-permute-start | bytes 221192 | tf_op jit(solution)/shard_map/ppermute | solution.py:151
Sparse Core Ops, SparseCore 0:
  38.8 32.5 all-gather.2
